TPU v7x, 256 devices: a whole 4x4x8 slice. The times are simulated.
256 devices in a mesh: graph: 16 (over z, core), feat: 16 (over y, x).
Axes of the slice: x: 4, y: 4, z: 8, core: 2. Of those that a mesh axis runs over, the one named last changes fastest.
Arguments:
- features: bfloat16 [131072, 768], P('graph', 'feat'), may hold values from -6 to 6
- frontier_ids: int32 [16, 16, 512], P('graph'), may hold values from 0 to 8191
- self_one_ids: int32 [16, 2048], P('graph'), may hold values from 0 to 8191
- neigh_one_ids: int32 [16, 16, 2048], P('graph'), may hold values from 0 to 8191
- count_one: int32 [16, 2048], P('graph'), may hold values from 1 to 16, as said below
- self_two_ids: int32 [16, 1536], P('graph', 'feat'), may hold values from 0 to 2047
- neigh_two_ids: int32 [16, 16, 1536], P('graph', None, 'feat'), may hold values from 0 to 2047
- count_two: int32 [16, 1536], P('graph', 'feat'), may hold values from 1 to 16, as said below
- pos_pairs: int32 [16, 2, 512], P('graph', None, 'feat'), may hold values from 0 to 1535
- neg_ids: int32 [16, 512], P('graph'), may hold values from 0 to 1535
- first_self: bfloat16 [768, 256], P('feat'), may hold values from -0.21875 to 0.21875
- first_neigh: bfloat16 [768, 256], P('feat'), may hold values from -0.21875 to 0.21875
- second_self: bfloat16 [256, 256], replicated, may hold values from -0.25 to 0.25
- second_neigh: bfloat16 [256, 256], replicated, may hold values from -0.25 to 0.25
Outputs:
- grad_first_self: float32 [768, 256], P('feat')
- grad_first_neigh: float32 [768, 256], P('feat')
- grad_second_self: float32 [256, 256], replicated
- grad_second_neigh: float32 [256, 256], replicated
- mean_loss: float32 [], replicated
Inputs may be any that keep to these rules, and one draw needn't show every extreme that they name: `frontier_ids`: row of owner o's block of 8192 nodes that group g asks for in slot s. `neigh_one_ids`: only the first count_one[g, i] of the 16 slots are live. `count_one`: every group has a first-hop node with 16 live neighbours. `neigh_two_ids`: only the first count_two[g, t] of the 16 slots are live. `count_two`: every group has a target with 16 live neighbours.
All inputs are finite; a program needn't handle non-finite values.
Results may differ from a plain program's by a relative error of at most 0.025.
Values may be sent and summed in bfloat16 or wider, within the bound.
No kernel may reach another device: no remote copies, remote signals or barrier semaphores. Data moves between devices by JAX's collectives and lax.ppermute only.
A program may use at most 64 MiB of HBM per device.

v0:
```python
import math

import jax
import jax.numpy as jnp
from jax import lax
from jax.sharding import PartitionSpec as P


def neighbour_mean(source, neigh_ids, counts):
    running = jnp.zeros((neigh_ids.shape[1], source.shape[1]), jnp.float32)
    for position in range(neigh_ids.shape[0]):
        picked = jnp.take(source, neigh_ids[position], axis=0).astype(jnp.float32)
        running = running + jnp.where((position < counts)[:, None], picked, 0.0)
    return (running / counts.astype(jnp.float32)[:, None]).astype(jnp.bfloat16)


def spread_back(grad_rows, neigh_ids, counts, row_total):
    weights = 1.0 / counts.astype(jnp.float32)
    result = jnp.zeros((row_total, grad_rows.shape[1]), jnp.float32)
    for position in range(neigh_ids.shape[0]):
        scaled = jnp.where((position < counts)[:, None], grad_rows * weights[:, None], 0.0)
        result = result.at[neigh_ids[position]].add(scaled)
    return result


def contract_rows(former, latter):
    return lax.dot_general(
        former, latter, (((0,), (0,)), ((), ())), preferred_element_type=jnp.float32
    )


def contract_cols(former, latter):
    return lax.dot_general(
        former, latter, (((1,), (1,)), ((), ())), preferred_element_type=jnp.float32
    )


def local(
    features,
    frontier_ids,
    self_one_ids,
    neigh_one_ids,
    count_one,
    self_two_ids,
    neigh_two_ids,
    count_two,
    pos_pairs,
    neg_ids,
    first_self,
    first_neigh,
    second_self,
    second_neigh,
):
    hidden_width = second_self.shape[0]
    scale = 1.0 / math.sqrt(hidden_width)
    negative_total = neg_ids.shape[1]
    first_rows = self_one_ids.shape[1]
    served = jnp.take(
        features,
        lax.all_to_all(frontier_ids[0], "graph", split_axis=0, concat_axis=0, tiled=True),
        axis=0,
    )
    frontier = lax.all_to_all(served, "graph", split_axis=0, concat_axis=0, tiled=True).reshape(
        -1, features.shape[1]
    )
    self_rows = jnp.take(frontier, self_one_ids[0], axis=0)
    neigh_rows = neighbour_mean(frontier, neigh_one_ids[0], count_one[0])
    partial_value = jnp.dot(self_rows, first_self, preferred_element_type=jnp.float32) + jnp.dot(
        neigh_rows, first_neigh, preferred_element_type=jnp.float32
    )
    hidden_pre = lax.psum(partial_value, "feat")
    hidden = jnp.maximum(hidden_pre, 0.0).astype(jnp.bfloat16)
    hidden_self = jnp.take(hidden, self_two_ids[0], axis=0)
    hidden_neigh = neighbour_mean(hidden, neigh_two_ids[0], count_two[0])
    embed_share = (
        jnp.dot(hidden_self, second_self, preferred_element_type=jnp.float32)
        + jnp.dot(hidden_neigh, second_neigh, preferred_element_type=jnp.float32)
    ).astype(jnp.bfloat16)
    embed = lax.all_gather(embed_share, "feat", axis=0, tiled=True)
    pair_block = pos_pairs[0]
    sources = pair_block[0]
    targets = pair_block[1]
    negatives = neg_ids[0]
    source_rows = jnp.take(embed, sources, axis=0)
    dest_rows = jnp.take(embed, targets, axis=0)
    negative_rows = jnp.take(embed, negatives, axis=0)
    pos_score = (
        jnp.sum(source_rows.astype(jnp.float32) * dest_rows.astype(jnp.float32), axis=1) * scale
    )
    neg_score = contract_cols(source_rows, negative_rows) * scale
    loss_part = (
        jnp.sum(jax.nn.softplus(-pos_score)) + jnp.sum(jax.nn.softplus(neg_score)) / negative_total
    )
    pos_grad = -jax.nn.sigmoid(-pos_score)
    neg_grad = (jax.nn.sigmoid(neg_score) / negative_total).astype(jnp.bfloat16)
    source_grad = (
        pos_grad[:, None] * dest_rows.astype(jnp.float32)
        + jnp.dot(neg_grad, negative_rows, preferred_element_type=jnp.float32)
    ) * scale
    dest_grad = pos_grad[:, None] * source_rows.astype(jnp.float32) * scale
    negative_grad = contract_rows(neg_grad, source_rows) * scale
    embed_partial = jnp.zeros(embed.shape, jnp.float32)
    embed_partial = (
        embed_partial.at[sources]
        .add(source_grad)
        .at[targets]
        .add(dest_grad)
        .at[negatives]
        .add(negative_grad)
    )
    embed_grad = lax.psum_scatter(
        embed_partial.astype(jnp.bfloat16), "feat", scatter_dimension=0, tiled=True
    )
    grad_ss = contract_rows(hidden_self, embed_grad)
    grad_sn = contract_rows(hidden_neigh, embed_grad)
    self_back = contract_cols(embed_grad, second_self)
    neigh_back = contract_cols(embed_grad, second_neigh)
    hidden_partial = (
        jnp.zeros((first_rows, hidden_width), jnp.float32).at[self_two_ids[0]].add(self_back)
    )
    hidden_partial = hidden_partial + spread_back(
        neigh_back, neigh_two_ids[0], count_two[0], first_rows
    )
    second_sums = lax.psum((grad_ss, grad_sn, loss_part), ("graph", "feat"))
    hidden_grad = lax.psum(hidden_partial.astype(jnp.bfloat16), "feat").astype(jnp.float32)
    pre_grad = jnp.where(hidden_pre > 0, hidden_grad, 0.0).astype(jnp.bfloat16)
    grad_fs_part = contract_rows(self_rows, pre_grad)
    grad_fn_part = contract_rows(neigh_rows, pre_grad)
    first_sums = (
        lax.psum(grad_fs_part.astype(jnp.bfloat16), "graph").astype(jnp.float32),
        lax.psum(grad_fn_part.astype(jnp.bfloat16), "graph").astype(jnp.float32),
    )
    pair_total = pos_pairs.shape[2] * lax.axis_size("feat") * lax.axis_size("graph")
    return (
        first_sums[0],
        first_sums[1],
        second_sums[0],
        second_sums[1],
        second_sums[2] / pair_total,
    )


def solution(mesh):
    placed = (
        P("graph", "feat"),
        P("graph", None, None),
        P("graph", None),
        P("graph", None, None),
        P("graph", None),
        P("graph", "feat"),
        P("graph", None, "feat"),
        P("graph", "feat"),
        P("graph", None, "feat"),
        P("graph", None),
        P("feat", None),
        P("feat", None),
        P(),
        P(),
    )
    return jax.shard_map(
        local,
        mesh=mesh,
        in_specs=placed,
        out_specs=(P("feat", None), P("feat", None), P(), P(), P()),
        check_vma=False,
    )
```

profile of v0, /device:TPU:1, one launch (start us, length us, event | category | flops | bytes accessed | tf_op | source)
XLA Modules:
  0.0 912.9 jit_solution(14901338500739851035)
XLA Ops:
  7.2 1.4 all_to_all.13
  8.7 10.0 %all-to-all-start = ((s32[16,1,512]{2,1,0:T(1,128)}), s32[16,1,512]{2,1,0:T(1,128)S(1)}, u32[]{:S(2)}, u32[]{:S(2)}) async-start(s32[16,1,512]{2,1,0:T(1,128)} %all_to_all.13), calls=%async_computation | async-start | bytes 65536 | tf_op jit(solution)/shard_map/all_to_all | solution.py:60
  18.6 1.9 fusion.120
  23.0 1.3 fusion.79
  24.3 1.3 compare_and_fusion.17
  25.6 2.0 copy.21
  37.9 29.2 %gather_fusion = bf16[8192,48]{1,0:T(8,128)(2,1)} fusion(bf16[8192,48]{1,0:T(8,128)(2,1)S(1)} %copy.21, s32[8192]{0:T(1024)S(1)} %broadcast_clamp_fusion), kind=kCustom, calls=%fused_computation.36 | custom fusion | bytes 1605632 | tf_op jit(solution)/shard_map/jit(_take)/gather | solution.py:58
  67.1 1.9 copy.22
  69.1 1.0 broadcast_select_fusion
  70.1 7.4 all-to-all-start.1
  83.2 16.9 %all-to-all-done.1 = bf16[16,512,48]{1,2,0:T(8,128)(2,1)S(1)} async-done(((bf16[16,512,48]{1,2,0:T(8,128)(2,1)}), bf16[16,512,48]{1,2,0:T(8,128)(2,1)S(1)}, u32[]{:S(2)}, u32[]{:S(2)}) %all-to-all-start.1) | async-done | bytes 786464 | tf_op jit(solution)/shard_map/all_to_all | solution.py:63
  100.1 1.0 copy.23
  101.2 6.2 gather_fusion.3
  107.4 8.0 gather_fusion.4
  115.3 8.0 gather_fusion.5
  123.3 8.0 gather_fusion.6
  131.3 8.0 gather_fusion.7
  139.3 8.0 gather_fusion.8
  147.3 8.0 gather_fusion.9
  155.3 8.0 gather_fusion.10
  163.2 8.0 gather_fusion.11
  171.2 8.0 gather_fusion.12
  179.2 8.0 gather_fusion.13
  187.2 8.0 gather_fusion.14
  195.1 8.0 gather_fusion.15
  203.1 8.0 gather_fusion.16
  211.1 8.0 gather_fusion.17
  219.0 8.0 gather_fusion.18
  227.0 6.2 gather_fusion.2
  235.2 13.5 %divide_convert_fusion = bf16[2048,48]{1,0:T(8,128)(2,1)S(1)} fusion(bf16[2048,48]{1,0:T(8,128)(2,1)} %gather_fusion.18, bf16[2048,48]{1,0:T(8,128)(2,1)} %gather_fusion.17, bf16[2048,48]{1,0:T(8,128)(2,1)} %gather_fusion.16, bf16[2048,48]{1,0:T(8,128)(2,1)} %gather_fusion.15, bf16[2048,48]{1,0:T(8,128)(2,1)} %gather_fusion.14, ...), kind=kLoop, calls=%fused_computation.71 | loop fusion | flops 6389760 | bytes 3416064 | tf_op jit(solution)/shard_map/convert_element_type | solution.py:14
  248.8 1.8 convolution_add_fusion
  252.7 94.4 %all-reduce.6.cloned.1.call-done = f32[2048,256]{1,0:T(8,128)} async-done(((f32[2048,256]{1,0:T(8,128)}), f32[2048,256]{1,0:T(8,128)}) %all-reduce.6.cloned.1.call-update) | async-done | bytes 2097168 | tf_op jit(solution)/shard_map/psum | solution.py:71
  347.1 1.8 maximum_convert_fusion
  364.6 18.4 %all_gather.3 = bf16[1536,256]{1,0:T(8,128)(2,1)S(1)} all-gather(bf16[96,256]{1,0:T(8,128)(2,1)S(1)} %fusion), channel_id=1, replica_groups=mesh['graph'=16,'feat'=16] {'feat'}, dimensions={0}, use_global_device_ids=true | all-gather | bytes 835584 | tf_op jit(solution)/shard_map/all_gather | solution.py:79
  383.0 2.0 gather_fusion.1
  388.2 1.5 fusion.1
  389.7 1.4 scatter_custom_fusion
  391.1 1.6 scatter_custom_fusion.1
  392.7 3.9 scatter_fusion
  397.8 81.2 %reduce-scatter.2.cloned.1.call-done = bf16[96,256]{1,0:T(8,128)(2,1)} async-done(((bf16[1536,256]{1,0:T(8,128)(2,1)}), bf16[96,256]{1,0:T(8,128)(2,1)}) %reduce-scatter.2.cloned.1.call-update) | async-done | bytes 49168 | tf_op jit(solution)/shard_map/reduce_scatter | solution.py:111
  480.0 2.6 scatter_custom_fusion.3
  482.6 4.0 scatter_custom_fusion.4
  486.7 4.0 scatter_custom_fusion.5
  490.7 4.0 scatter_custom_fusion.6
  494.7 4.0 scatter_custom_fusion.7
  498.7 4.0 scatter_custom_fusion.8
  502.7 4.0 scatter_custom_fusion.9
  506.7 4.0 scatter_custom_fusion.10
  510.7 4.0 scatter_custom_fusion.11
  514.7 4.0 scatter_custom_fusion.12
  518.8 4.0 scatter_custom_fusion.13
  522.8 4.0 scatter_custom_fusion.14
  526.8 4.0 scatter_custom_fusion.15
  530.8 4.0 scatter_custom_fusion.16
  534.8 4.0 scatter_custom_fusion.17
  539.0 4.4 scatter_custom_fusion.18
  543.4 2.8 convert_element_type.211
  547.6 77.4 %psum.55 = f32[]{:T(128)} all-reduce(f32[]{:T(128)S(6)} %add.498), channel_id=1, replica_groups=mesh['graph'=16,'feat'=16] {'graph','feat'}, use_global_device_ids=true, to_apply=%region_29.33 | all-reduce | flops 1 | bytes 8 | tf_op jit(solution)/shard_map/psum | solution.py:124
  627.5 15.6 %all-reduce.8.cloned.1.call-done = bf16[2048,256]{1,0:T(8,128)(2,1)} async-done(((bf16[2048,256]{1,0:T(8,128)(2,1)}), bf16[2048,256]{1,0:T(8,128)(2,1)}) %all-reduce.8.cloned.1.call-update) | async-done | bytes 1048592 | tf_op jit(solution)/shard_map/psum | solution.py:125
  643.2 2.0 convolution_convert_fusion.1
  645.6 46.9 %all-reduce.1 = (bf16[48,256]{1,0:T(8,128)(2,1)S(1)}, bf16[48,256]{1,0:T(8,128)(2,1)S(1)}) all-reduce(bf16[48,256]{1,0:T(8,128)(2,1)S(1)} %convolution_convert_fusion.1, bf16[48,256]{1,0:T(8,128)(2,1)S(1)} %convolution_convert_fusion), channel_id=1, replica_groups=mesh['graph'=16,'feat'=16] {'graph'}, use_global_device_ids=true, to_apply=%region_23.27 | all-reduce | flops 24576 | bytes 98304 | tf_op jit(solution)/shard_map/psum | solution.py:130
  693.8 208.1 %all-reduce.10.cloned.1.call-done = (f32[256,256]{1,0:T(8,128)}, f32[256,256]{1,0:T(8,128)}) async-done(((f32[256,256]{1,0:T(8,128)}, f32[256,256]{1,0:T(8,128)}), (f32[256,256]{1,0:T(8,128)}, f32[256,256]{1,0:T(8,128)})) %all-reduce.10.cloned.1.call-update) | async-done | bytes 524304 | tf_op jit(solution)/shard_map/psum | solution.py:124
  901.9 1.7 copy.49
  903.6 1.7 copy.50
  (363 shorter events, 46.3 us)
Async XLA Ops:
  7.2 357.2 %copy-start = (bf16[256,256]{1,0:T(8,128)(2,1)S(1)}, bf16[256,256]{1,0:T(8,128)(2,1)}, u32[]{:S(2)}) copy-start(bf16[256,256]{1,0:T(8,128)(2,1)} %param.33) | copy-start | bytes 393220
  7.2 27.5 %copy-start.27 = (s32[1,16,96]{2,1,0:T(8,128)S(1)}, s32[1,16,96]{2,1,0:T(8,128)}, u32[]{:S(2)}) copy-start(s32[1,16,96]{2,1,0:T(8,128)} %param.26) | copy-start | bytes 18436
  7.2 28.2 %copy-start.130 = (s32[1,96]{1,0:T(1,128)S(1)}, s32[1,96]{1,0:T(1,128)}, u32[]{:S(2)}) copy-start(s32[1,96]{1,0:T(1,128)} %param.25) | copy-start | bytes 1156
  7.2 28.2 %copy-start.63 = (s32[1,512]{1,0:T(1,128)S(1)}, s32[1,512]{1,0:T(1,128)}, u32[]{:S(2)}) copy-start(s32[1,512]{1,0:T(1,128)} %param.29) | copy-start | bytes 6148
  8.7 29.2 %all-to-all-start = ((s32[16,1,512]{2,1,0:T(1,128)}), s32[16,1,512]{2,1,0:T(1,128)S(1)}, u32[]{:S(2)}, u32[]{:S(2)}) async-start(s32[16,1,512]{2,1,0:T(1,128)} %all_to_all.13), calls=%async_computation | async-start | bytes 65536 | tf_op jit(solution)/shard_map/all_to_all | solution.py:60
  69.0 9.0 copy-start.26
  70.1 31.1 %copy-start.24 = (s32[2048]{0:T(1024)S(1)}, s32[2048]{0:T(1024)}, u32[]{:S(2)}) copy-start(s32[2048]{0:T(1024)} %fusion.80) | copy-start | bytes 24580
  70.1 30.0 %all-to-all-start.1 = ((bf16[16,512,48]{1,2,0:T(8,128)(2,1)}), bf16[16,512,48]{1,2,0:T(8,128)(2,1)S(1)}, u32[]{:S(2)}, u32[]{:S(2)}) async-start(bf16[16,512,48]{1,2,0:T(8,128)(2,1)} %broadcast_select_fusion), calls=%async_computation.1 | async-start | bytes 1572864 | tf_op jit(solution)/shard_map/all_to_all | solution.py:63
  77.4 269.7 %all-reduce.6.cloned.1.call-start = ((), (), s32[]{:S(2)}) async-start(), calls=%async_computation.3 | async-start | bytes 4194304 | tf_op jit(solution)/shard_map/psum | solution.py:71
  107.4 8.0 copy-start.22
  115.3 8.0 copy-start.21
  123.3 8.0 copy-start.20
  131.3 8.0 copy-start.19
  139.3 8.0 copy-start.18
  147.3 8.0 copy-start.17
  155.3 8.0 copy-start.16
  163.2 8.0 copy-start.15
  171.2 8.0 copy-start.13
  179.2 8.0 copy-start.14
  187.2 8.0 copy-start.12
  195.1 8.0 copy-start.10
  219.0 8.0 copy-start.11
  235.2 13.6 %copy-start.30 = (bf16[48,256]{1,0:T(8,128)(2,1)S(1)}, bf16[48,256]{1,0:T(8,128)(2,1)}, u32[]{:S(2)}) copy-start(bf16[48,256]{1,0:T(8,128)(2,1)} %param.31) | copy-start | bytes 73732
  250.7 228.3 %reduce-scatter.2.cloned.1.call-start = ((), (), s32[]{:S(2)}) async-start(), calls=%async_computation.4 | async-start | bytes 835584 | tf_op jit(solution)/shard_map/reduce_scatter | solution.py:111
  251.9 111.2 %copy-start.98 = (pred[96]{0:T(512)(128)(4,1)}, pred[96]{0:T(512)(128)(4,1)S(1)}, u32[]{:S(2)}) copy-start(pred[96]{0:T(512)(128)(4,1)S(1)} %compare_and_fusion.36) | copy-start | bytes 292
  252.5 133.1 %copy-start.129 = (pred[512]{0:T(512)(128)(4,1)}, pred[512]{0:T(512)(128)(4,1)S(1)}, u32[]{:S(2)}) copy-start(pred[512]{0:T(512)(128)(4,1)S(1)} %compare_and_fusion.37) | copy-start | bytes 1540
  252.5 110.8 %copy-start.65 = (pred[96]{0:T(512)(128)(4,1)}, pred[96]{0:T(512)(128)(4,1)S(1)}, u32[]{:S(2)}) copy-start(pred[96]{0:T(512)(128)(4,1)S(1)} %get-tuple-element.132) | copy-start | bytes 292
  252.5 110.8 %copy-start.67 = (pred[96]{0:T(512)(128)(4,1)}, pred[96]{0:T(512)(128)(4,1)S(1)}, u32[]{:S(2)}) copy-start(pred[96]{0:T(512)(128)(4,1)S(1)} %get-tuple-element.147) | copy-start | bytes 292
  252.6 110.8 %copy-start.69 = (pred[96]{0:T(512)(128)(4,1)}, pred[96]{0:T(512)(128)(4,1)S(1)}, u32[]{:S(2)}) copy-start(pred[96]{0:T(512)(128)(4,1)S(1)} %get-tuple-element.133) | copy-start | bytes 292
  252.6 110.8 %copy-start.71 = (pred[96]{0:T(512)(128)(4,1)}, pred[96]{0:T(512)(128)(4,1)S(1)}, u32[]{:S(2)}) copy-start(pred[96]{0:T(512)(128)(4,1)S(1)} %get-tuple-element.134) | copy-start | bytes 292
  252.6 110.8 %copy-start.73 = (pred[96]{0:T(512)(128)(4,1)}, pred[96]{0:T(512)(128)(4,1)S(1)}, u32[]{:S(2)}) copy-start(pred[96]{0:T(512)(128)(4,1)S(1)} %get-tuple-element.135) | copy-start | bytes 292
  252.6 110.8 %copy-start.75 = (pred[96]{0:T(512)(128)(4,1)}, pred[96]{0:T(512)(128)(4,1)S(1)}, u32[]{:S(2)}) copy-start(pred[96]{0:T(512)(128)(4,1)S(1)} %get-tuple-element.136) | copy-start | bytes 292
  252.6 110.8 %copy-start.77 = (pred[96]{0:T(512)(128)(4,1)}, pred[96]{0:T(512)(128)(4,1)S(1)}, u32[]{:S(2)}) copy-start(pred[96]{0:T(512)(128)(4,1)S(1)} %get-tuple-element.137) | copy-start | bytes 292
  252.6 110.8 %copy-start.79 = (pred[96]{0:T(512)(128)(4,1)}, pred[96]{0:T(512)(128)(4,1)S(1)}, u32[]{:S(2)}) copy-start(pred[96]{0:T(512)(128)(4,1)S(1)} %get-tuple-element.138) | copy-start | bytes 292
  252.6 110.8 %copy-start.81 = (pred[96]{0:T(512)(128)(4,1)}, pred[96]{0:T(512)(128)(4,1)S(1)}, u32[]{:S(2)}) copy-start(pred[96]{0:T(512)(128)(4,1)S(1)} %get-tuple-element.139) | copy-start | bytes 292
  252.6 110.8 %copy-start.83 = (pred[96]{0:T(512)(128)(4,1)}, pred[96]{0:T(512)(128)(4,1)S(1)}, u32[]{:S(2)}) copy-start(pred[96]{0:T(512)(128)(4,1)S(1)} %get-tuple-element.140) | copy-start | bytes 292
  252.6 110.8 %copy-start.85 = (pred[96]{0:T(512)(128)(4,1)}, pred[96]{0:T(512)(128)(4,1)S(1)}, u32[]{:S(2)}) copy-start(pred[96]{0:T(512)(128)(4,1)S(1)} %get-tuple-element.141) | copy-start | bytes 292
  252.6 110.8 %copy-start.87 = (pred[96]{0:T(512)(128)(4,1)}, pred[96]{0:T(512)(128)(4,1)S(1)}, u32[]{:S(2)}) copy-start(pred[96]{0:T(512)(128)(4,1)S(1)} %get-tuple-element.142) | copy-start | bytes 292
  252.7 110.8 %copy-start.89 = (pred[96]{0:T(512)(128)(4,1)}, pred[96]{0:T(512)(128)(4,1)S(1)}, u32[]{:S(2)}) copy-start(pred[96]{0:T(512)(128)(4,1)S(1)} %get-tuple-element.143) | copy-start | bytes 292
  252.7 110.8 %copy-start.91 = (pred[96]{0:T(512)(128)(4,1)}, pred[96]{0:T(512)(128)(4,1)S(1)}, u32[]{:S(2)}) copy-start(pred[96]{0:T(512)(128)(4,1)S(1)} %get-tuple-element.144) | copy-start | bytes 292
  252.7 110.8 %copy-start.93 = (pred[96]{0:T(512)(128)(4,1)}, pred[96]{0:T(512)(128)(4,1)S(1)}, u32[]{:S(2)}) copy-start(pred[96]{0:T(512)(128)(4,1)S(1)} %get-tuple-element.145) | copy-start | bytes 292
  252.7 110.8 %copy-start.95 = (pred[96]{0:T(512)(128)(4,1)}, pred[96]{0:T(512)(128)(4,1)S(1)}, u32[]{:S(2)}) copy-start(pred[96]{0:T(512)(128)(4,1)S(1)} %get-tuple-element.146) | copy-start | bytes 292
  355.8 7.6 copy-start.100
  396.6 82.4 %copy-start.68 = (pred[96]{0:T(512)(128)(4,1)S(1)}, pred[96]{0:T(512)(128)(4,1)}, u32[]{:S(2)}) copy-start(pred[96]{0:T(512)(128)(4,1)} %copy-done.67) | copy-start | bytes 292
  396.6 83.4 %copy-start.66 = (pred[96]{0:T(512)(128)(4,1)S(1)}, pred[96]{0:T(512)(128)(4,1)}, u32[]{:S(2)}) copy-start(pred[96]{0:T(512)(128)(4,1)} %copy-done.65) | copy-start | bytes 292
  397.6 85.0 %copy-start.96 = (pred[96]{0:T(512)(128)(4,1)S(1)}, pred[96]{0:T(512)(128)(4,1)}, u32[]{:S(2)}) copy-start(pred[96]{0:T(512)(128)(4,1)} %copy-done.95) | copy-start | bytes 292
  397.6 245.5 %all-reduce.8.cloned.1.call-start = ((), (), s32[]{:S(2)}) async-start(), calls=%async_computation.5 | async-start | bytes 2097152 | tf_op jit(solution)/shard_map/psum | solution.py:125
  482.6 8.0 copy-start.92
  486.6 8.0 copy-start.90
  490.7 8.0 copy-start.88
  494.7 8.0 copy-start.86
  498.7 8.0 copy-start.84
  502.7 8.0 copy-start.82
  506.7 8.0 copy-start.80
  510.7 8.0 copy-start.78
  514.7 8.0 copy-start.76
  518.8 8.0 copy-start.74
  522.8 8.0 copy-start.72
  526.8 8.0 copy-start.70
  530.8 8.0 copy-start.8
  543.4 83.1 %copy-start.99 = (pred[96]{0:T(512)(128)(4,1)S(1)}, pred[96]{0:T(512)(128)(4,1)}, u32[]{:S(2)}) copy-start(pred[96]{0:T(512)(128)(4,1)} %copy-done.98) | copy-start | bytes 292
  543.4 99.8 %copy-start.1 = (f32[2048,256]{1,0:T(8,128)S(1)}, f32[2048,256]{1,0:T(8,128)}, u32[]{:S(2)}) copy-start(f32[2048,256]{1,0:T(8,128)} %all-reduce.6.cloned.1.call-done) | copy-start | bytes 6291460
  543.4 99.8 %copy-start.33 = (pred[2048]{0:T(1024)(128)(4,1)S(1)}, pred[2048]{0:T(1024)(128)(4,1)}, u32[]{:S(2)}) copy-start(pred[2048]{0:T(1024)(128)(4,1)} %compare_and_fusion.17) | copy-start | bytes 6148
  546.3 355.6 %all-reduce.10.cloned.1.call-start = ((), (), s32[]{:S(2)}) async-start(), calls=%async_computation.6 | async-start | bytes 1048576 | tf_op jit(solution)/shard_map/psum | solution.py:124
  (75 other events, 224.9 us)
Sparse Core Ops, SparseCore 0:
  250.8 96.2 all-reduce.5
  397.8 81.2 reduce-scatter.1
  546.4 96.7 all-reduce.7
  650.2 251.7 all-reduce.9
where the time goes:
time: 915 us; the launch traced here: 913 us
  waiting for transfers between devices  416 us (45%)
  local copies, waits for them, and re-layouts  191 us (21%)
  blocking collectives  143 us (16%)
  other arithmetic  115 us (13%)
  between operations  18.6 us (2%)
  starting transfers between devices  17.7 us (2%)
  matrix products  11.1 us (1%)
    psum x1, waiting for transfers between devices, local(): second_sums = lax.psum((grad_ss, grad_sn, loss_part), ('graph', 'feat'))  208 us
    gather x32, local copies, waits for them, and re-layouts, neighbour_mean(): picked = jnp.take(source, neigh_ids[position], axis=0).astype(jnp.float32)  139 us
    psum x1, waiting for transfers between devices, local(): hidden_pre = lax.psum(partial_value, 'feat')  94.4 us
    reduce_scatter x1, waiting for transfers between devices, local(): lax.psum_scatter(embed_partial.astype(jnp.bfloat16), 'feat', scatter_dime...  81.2 us
    psum x1, blocking collectives, local(): second_sums = lax.psum((grad_ss, grad_sn, loss_part), ('graph', 'feat'))  77.4 us
    scatter-add x15, other arithmetic, spread_back(): result = result.at[neigh_ids[position]].add(scaled)  58.7 us
    psum x1, blocking collectives, local(): lax.psum(grad_fs_part.astype(jnp.bfloat16), 'graph').astype(jnp.float32)  46.9 us
    gather x2, local copies, waits for them, and re-layouts, local(): jnp.take(features, lax.all_to_all(frontier_ids[0], 'graph', split_axis=0,...  31.1 us
  transfers between devices with their start and end apart: 6, of which 5 were waited for; matrix products, arithmetic and copies ran while one was open for 3% of the time, Pallas kernels for 0%

commit v1 on v0

v1 whole, which is shorter than its diff:
```python
import functools
import math

import jax
import jax.numpy as jnp
from jax import lax
from jax.experimental import pallas as pl
from jax.experimental.pallas import tpu as pltpu
from jax.sharding import PartitionSpec as P

BF = jnp.bfloat16
F32 = jnp.float32
VMEM_LIMIT = 48 * 2**20


def swap(value, axis):
    return lax.all_to_all(value, axis, split_axis=0, concat_axis=0, tiled=True)


def gather_all(value, axis):
    size = lax.axis_size(axis)
    return swap(jnp.broadcast_to(value[None], (size,) + value.shape), axis)


def dot(former, latter, dims):
    return lax.dot_general(former, latter, (dims, ((), ())), preferred_element_type=F32)


def serve_kernel(ids_ref, feat_ref, out_ref, table, picked):
    width, rows = feat_ref.shape
    groups, _, cap = out_ref.shape
    step = 512

    def fill(at, _):
        at = pl.multiple_of(at * step, step)
        table[pl.ds(at, step), 0:width] = feat_ref[:, pl.ds(at, step)].astype(F32).T
        return 0

    lax.fori_loop(0, rows // step, fill, 0)

    def per_group(group, _):
        base = group * cap

        def pick(at, _):
            for lane in range(32):
                row = at * 32 + lane
                picked[pl.ds(row, 1), :] = table[pl.ds(ids_ref[base + row], 1), :]
            return 0

        lax.fori_loop(0, cap // 32, pick, 0)
        out_ref[group] = picked[:, 0:width].T.astype(out_ref.dtype)
        return 0

    lax.fori_loop(0, groups, per_group, 0)


def serve(features_t, ids, groups, cap):
    width, rows = features_t.shape
    return pl.pallas_call(
        serve_kernel,
        out_shape=jax.ShapeDtypeStruct((groups, width, cap), features_t.dtype),
        in_specs=[
            pl.BlockSpec(memory_space=pltpu.SMEM),
            pl.BlockSpec(memory_space=pltpu.VMEM),
        ],
        out_specs=pl.BlockSpec(memory_space=pltpu.VMEM),
        scratch_shapes=[pltpu.VMEM((rows, 128), F32), pltpu.VMEM((cap, 128), F32)],
        compiler_params=pltpu.CompilerParams(vmem_limit_bytes=VMEM_LIMIT),
        name="serve",
    )(ids, features_t)


def hop_kernel(fan, ids_ref, self_ref, front_ref, inv_ref, out_ref, table, own, total):
    owners, width, cap = front_ref.shape
    nodes = out_ref.shape[0] * out_ref.shape[2]
    block = out_ref.shape[2]

    def fill(owner, _):
        at = pl.multiple_of(owner * cap, cap)
        table[pl.ds(at, cap), 0:width] = front_ref[owner].astype(F32).T
        return 0

    lax.fori_loop(0, owners, fill, 0)
    table[pl.ds(owners * cap, 8), :] = jnp.zeros((8, 128), F32)

    def per_block(dest, _):
        base = dest * block

        def pick(at, _):
            for lane in range(8):
                row = at * 8 + lane
                node = base + row
                rows = [
                    table[pl.ds(ids_ref[node * fan + slot], 1), :] for slot in range(fan)
                ]
                while len(rows) > 1:
                    rows = [rows[at] + rows[at + 1] for at in range(0, len(rows), 2)]
                total[pl.ds(row, 1), :] = rows[0]
                own[pl.ds(row, 1), :] = table[pl.ds(self_ref[node], 1), :]
            return 0

        lax.fori_loop(0, block // 8, pick, 0)
        out_ref[dest, 0:width, :] = own[:, 0:width].T.astype(out_ref.dtype)
        inv = inv_ref[pl.ds(dest, 1), :]
        out_ref[dest, width : 2 * width, :] = (total[:, 0:width].T * inv).astype(out_ref.dtype)
        return 0

    lax.fori_loop(0, out_ref.shape[0], per_block, 0)


def hop(frontier, ids, self_ids, inv, blocks):
    owners, width, cap = frontier.shape
    nodes = self_ids.shape[0]
    fan = ids.shape[0] // nodes
    block = nodes // blocks
    return pl.pallas_call(
        functools.partial(hop_kernel, fan),
        out_shape=jax.ShapeDtypeStruct((blocks, 2 * width, block), frontier.dtype),
        in_specs=[
            pl.BlockSpec(memory_space=pltpu.SMEM),
            pl.BlockSpec(memory_space=pltpu.SMEM),
            pl.BlockSpec(memory_space=pltpu.VMEM),
            pl.BlockSpec(memory_space=pltpu.VMEM),
        ],
        out_specs=pl.BlockSpec(memory_space=pltpu.VMEM),
        scratch_shapes=[
            pltpu.VMEM((owners * cap + 8, 128), F32),
            pltpu.VMEM((block, 128), F32),
            pltpu.VMEM((block, 128), F32),
        ],
        compiler_params=pltpu.CompilerParams(vmem_limit_bytes=VMEM_LIMIT),
        name="first_hop",
    )(ids, self_ids, frontier, inv)


def one_hot(ids, total):
    marks = lax.broadcasted_iota(jnp.int32, (ids.shape[0], total), 1)
    return (ids[:, None] == marks).astype(BF)


def count_hot(ids, counts, total):
    marks = lax.broadcasted_iota(jnp.int32, (ids.shape[1], total), 1)
    result = jnp.zeros((ids.shape[1], total), F32)
    for slot in range(ids.shape[0]):
        live = jnp.where(slot < counts, ids[slot], -1)
        result = result + (live[:, None] == marks).astype(F32)
    return result.astype(BF)


def local(
    features,
    frontier_ids,
    self_one_ids,
    neigh_one_ids,
    count_one,
    self_two_ids,
    neigh_two_ids,
    count_two,
    pos_pairs,
    neg_ids,
    first_self,
    first_neigh,
    second_self,
    second_neigh,
):
    graphs = lax.axis_size("graph")
    feats = lax.axis_size("feat")
    hidden_width = second_self.shape[0]
    scale = 1.0 / math.sqrt(hidden_width)
    negative_total = neg_ids.shape[1]
    nodes = self_one_ids.shape[1]
    fan = neigh_one_ids.shape[1]
    width = features.shape[1]
    cap = frontier_ids.shape[2]
    front = graphs * cap
    share = self_two_ids.shape[1]
    pair_share = pos_pairs.shape[2]

    asked = swap(frontier_ids[0], "graph")
    weights = gather_all(jnp.concatenate([first_self, first_neigh], axis=0), "feat")
    packed = jnp.concatenate(
        [
            self_two_ids[0],
            count_two[0],
            neigh_two_ids[0].reshape(-1),
            pos_pairs[0].reshape(-1),
        ]
    )
    packed = gather_all(packed, "feat")
    self_two = packed[:, :share].reshape(-1)
    counts_two = packed[:, share : 2 * share].reshape(-1)
    neigh_two = packed[:, 2 * share : (2 + fan) * share].reshape(feats, fan, share)
    neigh_two = neigh_two.transpose(1, 0, 2).reshape(fan, -1)
    pairs = packed[:, (2 + fan) * share :].reshape(feats, 2, pair_share)
    pairs = pairs.transpose(1, 0, 2).reshape(2, -1)
    targets_total = self_two.shape[0]

    slots = lax.broadcasted_iota(jnp.int32, (fan, nodes), 0)
    live_ids = jnp.where(slots < count_one, neigh_one_ids[0], front).T.reshape(-1)
    inv_one = (1.0 / count_one.astype(F32)).reshape(feats, -1)

    served = serve(features.T, asked.reshape(-1), graphs, cap)
    frontier = swap(served, "graph")
    rows_one = hop(frontier, live_ids, self_one_ids[0], inv_one, feats)
    mine = swap(rows_one, "feat")
    hidden_pre = dot(
        mine.reshape(feats * 2 * width, -1),
        weights.reshape(feats * 2 * width, hidden_width),
        ((0,), (0,)),
    )
    hidden = gather_all(jnp.maximum(hidden_pre, 0.0).astype(BF), "feat")
    hidden = hidden.reshape(nodes, hidden_width)

    pick_self = one_hot(self_two, nodes)
    pick_neigh = count_hot(neigh_two, counts_two, nodes)
    inv_two = (1.0 / counts_two.astype(F32))[:, None]
    hidden_self = dot(pick_self, hidden, ((1,), (0,))).astype(BF)
    hidden_neigh = (dot(pick_neigh, hidden, ((1,), (0,))) * inv_two).astype(BF)
    embed = (
        dot(hidden_self, second_self, ((1,), (0,)))
        + dot(hidden_neigh, second_neigh, ((1,), (0,)))
    ).astype(BF)

    pair_total = pairs.shape[1]
    ends = jnp.concatenate([pairs[0], pairs[1], neg_ids[0]])
    pick_ends = one_hot(ends, targets_total)
    end_rows = dot(pick_ends, embed, ((1,), (0,))).astype(BF)
    source_rows = end_rows[:pair_total]
    dest_rows = end_rows[pair_total : 2 * pair_total]
    negative_rows = end_rows[2 * pair_total :]
    pos_score = (
        jnp.sum(source_rows.astype(F32) * dest_rows.astype(F32), axis=1, keepdims=True) * scale
    )
    neg_score = dot(source_rows, negative_rows, ((1,), (1,))) * scale
    loss_part = (
        jnp.sum(jax.nn.softplus(-pos_score)) + jnp.sum(jax.nn.softplus(neg_score)) / negative_total
    )
    pos_grad = -jax.nn.sigmoid(-pos_score)
    neg_grad = (jax.nn.sigmoid(neg_score) / negative_total).astype(BF)
    source_grad = (
        pos_grad * dest_rows.astype(F32) + dot(neg_grad, negative_rows, ((1,), (0,)))
    ) * scale
    dest_grad = pos_grad * source_rows.astype(F32) * scale
    negative_grad = dot(neg_grad, source_rows, ((0,), (0,))) * scale
    end_grads = jnp.concatenate([source_grad, dest_grad, negative_grad]).astype(BF)
    embed_grad = dot(pick_ends, end_grads, ((0,), (0,))).astype(BF)

    grad_ss = dot(hidden_self, embed_grad, ((0,), (0,)))
    grad_sn = dot(hidden_neigh, embed_grad, ((0,), (0,)))
    self_back = dot(embed_grad, second_self, ((1,), (1,))).astype(BF)
    neigh_back = (dot(embed_grad, second_neigh, ((1,), (1,))) * inv_two).astype(BF)
    hidden_grad = dot(pick_self, self_back, ((0,), (0,))) + dot(
        pick_neigh, neigh_back, ((0,), (0,))
    )
    pre_grad = jnp.where(hidden > 0, hidden_grad, 0.0).astype(BF)
    first_part = dot(
        rows_one.transpose(1, 0, 2).reshape(2 * width, nodes), pre_grad, ((1,), (0,))
    )

    loss_high = loss_part.astype(BF)
    loss_mid = (loss_part - loss_high.astype(F32)).astype(BF)
    loss_low = (loss_part - loss_high.astype(F32) - loss_mid.astype(F32)).astype(BF)
    loss_row = jnp.zeros((graphs, 1, hidden_width), BF)
    loss_row = loss_row.at[:, 0, 0].set(loss_high).at[:, 0, 1].set(loss_mid)
    loss_row = loss_row.at[:, 0, 2].set(loss_low)
    parts = jnp.concatenate(
        [
            first_part.astype(BF).reshape(graphs, -1, hidden_width),
            grad_ss.astype(BF).reshape(graphs, -1, hidden_width),
            grad_sn.astype(BF).reshape(graphs, -1, hidden_width),
            loss_row,
        ],
        axis=1,
    )
    sums = jnp.sum(swap(parts, "graph").astype(F32), axis=0)
    loss = jnp.sum(sums[-1, 0:3])
    first_rows = 2 * width // graphs
    second_rows = hidden_width // graphs
    whole = gather_all(sums[:-1].astype(BF), "graph").astype(F32)
    first_sums = whole[:, :first_rows].reshape(2 * width, hidden_width)
    ss = whole[:, first_rows : first_rows + second_rows].reshape(hidden_width, hidden_width)
    sn = whole[:, first_rows + second_rows :].reshape(hidden_width, hidden_width)
    return (
        first_sums[:width],
        first_sums[width:],
        ss,
        sn,
        loss / (pair_total * graphs),
    )


def solution(mesh):
    placed = (
        P("graph", "feat"),
        P("graph", None, None),
        P("graph", None),
        P("graph", None, None),
        P("graph", None),
        P("graph", "feat"),
        P("graph", None, "feat"),
        P("graph", "feat"),
        P("graph", None, "feat"),
        P("graph", None),
        P("feat", None),
        P("feat", None),
        P(),
        P(),
    )
    return jax.shard_map(
        local,
        mesh=mesh,
        in_specs=placed,
        out_specs=(P("feat", None), P("feat", None), P(), P(), P()),
        check_vma=False,
    )
```

time: 915 us -> 248 us (0.27)
  waiting for transfers between devices: 416 us -> 44.4 us
  local copies, waits for them, and re-layouts: 191 us -> 20.6 us
  blocking collectives: 143 us -> 16.9 us
  other arithmetic: 115 us -> 35.5 us
  Pallas kernels: 0 us -> 53.2 us
  starting transfers between devices: 17.7 us -> 42.1 us
  matrix products: 11.1 us -> 30.5 us
  between operations: 18.6 us -> 4.24 us
    psum x3 -> x0, waiting for transfers between devices: 318 us -> none  [the longest x1 208 us: local(): second_sums = lax.psum((grad_ss, grad_sn, loss_part), ('graph', 'feat'))]
    gather x39 -> x0, local copies, waits for them, and re-layouts: 180 us -> none  [the longest x32 139 us: neighbour_mean(): picked = jnp.take(source, neigh_ids[position], axis=0).astype(jnp.float32)]
    psum x2 -> x0, blocking collectives: 124 us -> none  [the longest x1 77.4 us: local(): second_sums = lax.psum((grad_ss, grad_sn, loss_part), ('graph', 'feat'))]
    reduce_scatter x1 -> x0, waiting for transfers between devices: 81.2 us -> none  [local(): lax.psum_scatter(embed_partial.astype(jnp.bfloat16), 'feat', scatter_dime...]
    scatter-add x18 -> x0, other arithmetic: 65.5 us -> none  [the longest x15 58.7 us: spread_back(): result = result.at[neigh_ids[position]].add(scaled)]
    pallas_call x0 -> x2, Pallas kernels: none -> 53.2 us  [the longest x1 38.6 us: hop(): pl.pallas_call(functools.partial(hop_kernel, fan), out_shape=jax.ShapeDty...]
    all_to_all x2 -> x7, waiting for transfers between devices: 16.9 us -> 44.4 us  [swap(): return lax.all_to_all(value, axis, split_axis=0, concat_axis=0, tiled=True)]
    all_to_all x2 -> x7, starting transfers between devices: 17.3 us -> 42.1 us  [swap(): return lax.all_to_all(value, axis, split_axis=0, concat_axis=0, tiled=True)]
  transfers between devices with their start and end apart: 6 -> 7, of which waited for: 5 -> 4; matrix products, arithmetic and copies ran while one was open for 3% -> 16% of each run, Pallas kernels for 0% -> 21%
where the time goes in v1:
time: 248 us; the launch traced here: 247 us
  Pallas kernels  53.2 us (21%)
  waiting for transfers between devices  44.4 us (18%)
  starting transfers between devices  42.1 us (17%)
  other arithmetic  35.5 us (14%)
  matrix products  30.5 us (12%)
  local copies, waits for them, and re-layouts  20.6 us (8%)
  blocking collectives  16.9 us (7%)
  between operations  4.24 us (2%)
    all_to_all x7, waiting for transfers between devices, swap(): return lax.all_to_all(value, axis, split_axis=0, concat_axis=0, tiled=True)  44.4 us
    all_to_all x7, starting transfers between devices, swap(): return lax.all_to_all(value, axis, split_axis=0, concat_axis=0, tiled=True)  42.1 us
    pallas_call x1, Pallas kernels, hop(): pl.pallas_call(functools.partial(hop_kernel, fan), out_shape=jax.ShapeDty...  38.6 us
    convert_element_type x1, other arithmetic, count_hot(): return result.astype(BF)  30.5 us
    dot_general x14, matrix products, dot(): lax.dot_general(former, latter, (dims, ((), ())), preferred_element_type=...  30.5 us
    all_to_all x1, blocking collectives, swap(): return lax.all_to_all(value, axis, split_axis=0, concat_axis=0, tiled=True)  16.9 us
    pallas_call x1, Pallas kernels, serve(): pl.pallas_call(serve_kernel, out_shape=jax.ShapeDtypeStruct((groups, widt...  14.6 us
  transfers between devices with their start and end apart: 7, of which 4 were waited for; matrix products, arithmetic and copies ran while one was open for 16% of the time, Pallas kernels for 21%

profile of v1, /device:TPU:1, one launch (start us, length us, event | category | flops | bytes accessed | tf_op | source)
XLA Modules:
  0.0 247.4 jit_solution(14471720731586273871)
XLA Ops:
  0.7 1.4 all_to_all.30
  2.1 10.0 %all-to-all-start = ((s32[16,1,512]{2,1,0:T(1,128)}), s32[16,1,512]{2,1,0:T(1,128)S(1)}, u32[]{:S(2)}, u32[]{:S(2)}) async-start(s32[16,1,512]{2,1,0:T(1,128)} %all_to_all.30), calls=%async_computation | async-start | bytes 65536 | tf_op jit(solution)/shard_map/all_to_all | solution.py:17
  12.1 0.9 fusion.39
  13.1 0.8 reshape_squeeze.6
  13.8 0.8 reshape_squeeze.7
  14.6 0.3 copy.21
  14.9 0.3 reshape.417.ids_ref
  15.2 0.6 slice.212
  15.8 0.7 concatenate.27
  16.6 2.9 %all-to-all-done = s32[16,1,512]{2,1,0:T(1,128)S(1)} async-done(((s32[16,1,512]{2,1,0:T(1,128)}), s32[16,1,512]{2,1,0:T(1,128)S(1)}, u32[]{:S(2)}, u32[]{:S(2)}) %all-to-all-start) | async-done | bytes 32800 | tf_op jit(solution)/shard_map/all_to_all | solution.py:17
  19.5 0.7 broadcast_in_dim.38
  20.2 6.8 %all-to-all-start.5 = ((s32[16,1,1792]{2,1,0:T(1,128)}), s32[16,1,1792]{2,1,0:T(1,128)S(1)}, u32[]{:S(2)}, u32[]{:S(2)}) async-start(s32[16,1,1792]{2,1,0:T(1,128)} %broadcast_in_dim.38), calls=%async_computation.5 | async-start | bytes 229376 | tf_op jit(solution)/shard_map/all_to_all | solution.py:17
  27.0 0.6 slice.213
  27.6 1.1 copy-done.1
  28.7 14.6 %serve.1 = bf16[16,48,512]{2,1,0:T(8,128)(2,1)} custom-call(s32[8192]{0:T(1024)S(1)} %bitcast.63, bf16[48,8192]{1,0:T(8,128)(2,1)S(1)} %bitcast.62), custom_call_target="tpu_custom_call" | custom-call | tf_op jit(solution)/shard_map/serve/pallas_call | solution.py:59
  43.3 4.6 %all-to-all-start.1 = ((bf16[16,48,512]{2,1,0:T(8,128)(2,1)}), bf16[16,48,512]{2,1,0:T(8,128)(2,1)S(1)}, u32[]{:S(2)}, u32[]{:S(2)}) async-start(bf16[16,48,512]{2,1,0:T(8,128)(2,1)} %serve.1), calls=%async_computation.1 | async-start | bytes 1572864 | tf_op jit(solution)/shard_map/all_to_all | solution.py:17
  47.9 0.7 and_reduce_fusion
  48.8 0.1 broadcast_compare_fusion.15
  48.9 0.1 gt.263
  49.0 0.1 reshape.423
  49.1 0.4 slice_reduce_fusion.15
  49.5 0.1 gt.260
  49.7 0.1 gt.257
  49.8 0.1 gt.254
  50.3 20.2 %all-to-all-done.1.front_ref = bf16[16,48,512]{2,1,0:T(8,128)(2,1)S(1)} async-done(((bf16[16,48,512]{2,1,0:T(8,128)(2,1)}), bf16[16,48,512]{2,1,0:T(8,128)(2,1)S(1)}, u32[]{:S(2)}, u32[]{:S(2)}) %all-to-all-start.1) | async-done | bytes 786464 | tf_op jit(solution)/shard_map/all_to_all | solution.py:17
  70.6 1.0 broadcast_in_dim.35
  71.5 6.9 %all-to-all-start.3 = ((bf16[16,96,256]{2,1,0:T(8,128)(2,1)}), bf16[16,96,256]{2,1,0:T(8,128)(2,1)S(1)}, u32[]{:S(2)}, u32[]{:S(2)}) async-start(bf16[16,96,256]{2,1,0:T(8,128)(2,1)} %broadcast_in_dim.35), calls=%async_computation.3 | async-start | bytes 1572864 | tf_op jit(solution)/shard_map/all_to_all | solution.py:17
  78.5 0.1 gt.245
  80.1 38.6 %first_hop.1 = bf16[16,96,128]{2,1,0:T(8,128)(2,1)} custom-call(s32[32768]{0:T(1024)S(1)} %reshape.417.ids_ref, s32[2048]{0:T(1024)S(1)} %bitcast.65, bf16[16,48,512]{2,1,0:T(8,128)(2,1)S(1)} %all-to-all-done.1.front_ref, f32[16,128]{1,0:T(8,128)S(1)} %bitcast.64), custom_call_target="tpu_custom_call" | custom-call | tf_op jit(solution)/shard_map/first_hop/pallas_call | solution.py:116
  118.7 6.8 %all-to-all-start.2 = ((bf16[16,96,128]{2,1,0:T(8,128)(2,1)}), bf16[16,96,128]{2,1,0:T(8,128)(2,1)S(1)}, u32[]{:S(2)}, u32[]{:S(2)}) async-start(bf16[16,96,128]{2,1,0:T(8,128)(2,1)} %first_hop.1), calls=%async_computation.2 | async-start | bytes 786432 | tf_op jit(solution)/shard_map/all_to_all | solution.py:17
  125.5 9.8 %all-to-all-done.2 = bf16[16,96,128]{2,1,0:T(8,128)(2,1)S(1)} async-done(((bf16[16,96,128]{2,1,0:T(8,128)(2,1)}), bf16[16,96,128]{2,1,0:T(8,128)(2,1)S(1)}, u32[]{:S(2)}, u32[]{:S(2)}) %all-to-all-start.2) | async-done | bytes 393248 | tf_op jit(solution)/shard_map/all_to_all | solution.py:17
  135.3 0.3 fusion.22
  135.6 1.1 broadcast_in_dim.36
  136.8 3.7 %all-to-all-start.4 = ((bf16[16,128,256]{2,1,0:T(8,128)(2,1)}), bf16[16,128,256]{2,1,0:T(8,128)(2,1)S(1)}, u32[]{:S(2)}, u32[]{:S(2)}) async-start(bf16[16,128,256]{2,1,0:T(8,128)(2,1)} %broadcast_in_dim.36), calls=%async_computation.4 | async-start | bytes 2097152 | tf_op jit(solution)/shard_map/all_to_all | solution.py:17
  140.4 30.5 %add_convert_fusion = bf16[1536,2048]{1,0:T(8,128)(2,1)} fusion(s32[1536]{0:T(1024)S(1)} %get-tuple-element.83, s32[1536]{0:T(1024)S(1)} %get-tuple-element.84, s32[1536]{0:T(1024)S(1)} %get-tuple-element.85, s32[1536]{0:T(1024)S(1)} %get-tuple-element.86, s32[1536]{0:T(1024)S(1)} %get-tuple-element.87, s32[1536]{0:T(1024)S(1)} %get-tuple-element.88, ...), kind=kLoop, calls=%fused_computation | loop fusion | flops 150994944 | bytes 6389760 | tf_op jit(solution)/shard_map/convert_element_type | solution.py:147
  171.5 2.4 fusion.15
  173.9 0.9 copy-done.3
  174.8 1.5 fusion.44
  176.4 2.8 %fusion.12 = bf16[1536,256]{1,0:T(8,128)(2,1)} fusion(bf16[1536,2048]{1,0:T(8,128)(2,1)S(1)} %bitcast.67, bf16[2048,256]{1,0:T(8,128)(2,1)S(1)} %bitcast.69, f32[1536]{0:T(1024)S(1)} %div.46), kind=kOutput, calls=%fused_computation.36 | convolution fusion | flops 1611399168 | bytes 8132608 | tf_op jit(solution)/shard_map/dot_general | solution.py:26
  179.1 3.8 %fusion.13 = bf16[1536,256]{1,0:T(8,128)(2,1)S(1)} fusion(s32[1536]{0:T(1024)S(1)} %pad_add_fusion, f32[1536,256]{1,0:T(8,128)} %fusion.44, bf16[1536,256]{1,0:T(8,128)(2,1)} %fusion.12, bf16[256,256]{1,0:T(8,128)(2,1)S(1)} %copy-done), kind=kOutput, calls=%fused_computation.37 | convolution fusion | flops 1412825088 | bytes 3282944 | tf_op jit(solution)/shard_map/dot_general | solution.py:26
  182.9 0.1 fusion.32
  183.1 1.7 multiply_convert_fusion
  184.7 0.6 divide_negate_fusion
  185.3 0.3 fusion.20
  185.7 0.1 fusion.31
  185.8 0.3 fusion.19
  186.2 2.9 %fusion.14 = bf16[1536,256]{1,0:T(8,128)(2,1)S(1)} fusion(s32[1536]{0:T(1024)S(1)} %pad_add_fusion, bf16[512,256]{1,0:T(8,128)(2,1)S(1)} %fusion.20, bf16[512,256]{1,0:T(8,128)(2,1)S(1)} %fusion.31, bf16[512,256]{1,0:T(8,128)(2,1)S(1)} %fusion.19), kind=kOutput, calls=%fused_computation.38 | convolution fusion | flops 1213071360 | bytes 1579008 | tf_op jit(solution)/shard_map/dot_general | solution.py:26
  189.1 0.4 convolution_convert_fusion.1
  189.5 0.4 convolution_convert_fusion.2
  189.9 6.7 %fusion.18 = f32[2048,256]{1,0:T(8,128)} fusion(bf16[1536,2048]{1,0:T(8,128)(2,1)} %add_convert_fusion, bf16[1536,256]{1,0:T(8,128)(2,1)S(1)} %fusion.14, bf16[256,256]{1,0:T(8,128)(2,1)S(1)} %copy-done, f32[1536]{0:T(1024)S(1)} %div.46), kind=kOutput, calls=%fused_computation.45 | convolution fusion | flops 1812725760 | bytes 9312256 | tf_op jit(solution)/shard_map/dot_general | solution.py:26
  198.0 1.9 scatter.22
  199.9 1.4 broadcast_select_fusion
  201.3 1.9 scatter.23
  203.1 5.7 %fusion.16 = bf16[2048,256]{1,0:T(8,128)(2,1)S(1)} fusion(f32[2048,256]{1,0:T(8,128)} %fusion.18, s32[1536]{0:T(1024)S(1)} %eq.146, bf16[2048,256]{1,0:T(8,128)(2,1)S(1)} %bitcast.70, bf16[1536,256]{1,0:T(8,128)(2,1)} %copy-done.11, bf16[256,256]{1,0:T(8,128)(2,1)S(1)} %copy-done.5), kind=kOutput, calls=%fused_computation.40 | convolution fusion | flops 1818624000 | bytes 5117952 | tf_op jit(solution)/shard_map/dot_general | solution.py:26
  208.8 1.3 convolution_convert_fusion.3
  210.2 0.2 pad_maximum_fusion
  210.3 16.9 %all_to_all.48 = bf16[16,39,256]{2,1,0:T(8,128)(2,1)S(1)} all-to-all(bf16[16,39,256]{2,1,0:T(8,128)(2,1)S(1)} %pad_maximum_fusion), channel_id=1, replica_groups=mesh['graph'=16,'feat'=16] {'graph'}, dimensions={0} | all-to-all | bytes 638976 | tf_op jit(solution)/shard_map/all_to_all | solution.py:17
  227.3 0.7 broadcast_in_dim.41
  228.0 3.4 %all-to-all-start.7 = ((bf16[16,38,256]{2,1,0:T(8,128)(2,1)}), bf16[16,38,256]{2,1,0:T(8,128)(2,1)S(1)}, u32[]{:S(2)}, u32[]{:S(2)}) async-start(bf16[16,38,256]{2,1,0:T(8,128)(2,1)} %broadcast_in_dim.41), calls=%async_computation.7 | async-start | bytes 655360 | tf_op jit(solution)/shard_map/all_to_all | solution.py:17
  231.4 0.6 slice_reduce_fusion.18
  232.7 11.4 %all-to-all-done.7 = bf16[16,38,256]{2,1,0:T(8,128)(2,1)S(1)} async-done(((bf16[16,38,256]{2,1,0:T(8,128)(2,1)}), bf16[16,38,256]{2,1,0:T(8,128)(2,1)S(1)}, u32[]{:S(2)}, u32[]{:S(2)}) %all-to-all-start.7) | async-done | bytes 311328 | tf_op jit(solution)/shard_map/all_to_all | solution.py:17
  244.1 0.6 slice.216
  244.7 0.6 slice.218
  245.4 0.9 fusion.42
  (90 shorter events, 3.1 us)
Async XLA Ops:
  0.6 178.5 %copy-start = (bf16[256,256]{1,0:T(8,128)(2,1)S(1)}, bf16[256,256]{1,0:T(8,128)(2,1)}, u32[]{:S(2)}) copy-start(bf16[256,256]{1,0:T(8,128)(2,1)} %param.33) | copy-start | bytes 393220
  0.6 47.2 %copy-start.10 = (s32[3]{0:T(128)S(1)}, s32[3]{0:T(128)}, u32[]{:S(2)}) copy-start(s32[3]{0:T(128)} %constant.142.clone.1) | copy-start | bytes 40
  0.7 48.0 %copy-start.6 = (s32[1,2048]{1,0:T(1,128)S(1)}, s32[1,2048]{1,0:T(1,128)}, u32[]{:S(2)}) copy-start(s32[1,2048]{1,0:T(1,128)} %param.24) | copy-start | bytes 24580
  0.7 47.9 %copy-start.7 = (bf16[48,256]{1,0:T(8,128)(2,1)S(1)}, bf16[48,256]{1,0:T(8,128)(2,1)}, u32[]{:S(2)}) copy-start(bf16[48,256]{1,0:T(8,128)(2,1)} %param.31) | copy-start | bytes 73732
  0.7 47.9 %copy-start.8 = (bf16[48,256]{1,0:T(8,128)(2,1)S(1)}, bf16[48,256]{1,0:T(8,128)(2,1)}, u32[]{:S(2)}) copy-start(bf16[48,256]{1,0:T(8,128)(2,1)} %param.30) | copy-start | bytes 73732
  0.7 79.4 %copy-start.2 = (s32[1,2048]{1,0:T(1,128)S(1)}, s32[1,2048]{1,0:T(1,128)}, u32[]{:S(2)}) copy-start(s32[1,2048]{1,0:T(1,128)} %param.22) | copy-start | bytes 24580
  2.1 17.4 %all-to-all-start = ((s32[16,1,512]{2,1,0:T(1,128)}), s32[16,1,512]{2,1,0:T(1,128)S(1)}, u32[]{:S(2)}, u32[]{:S(2)}) async-start(s32[16,1,512]{2,1,0:T(1,128)} %all_to_all.30), calls=%async_computation | async-start | bytes 65536 | tf_op jit(solution)/shard_map/all_to_all | solution.py:17
  20.2 23.1 %all-to-all-start.5 = ((s32[16,1,1792]{2,1,0:T(1,128)}), s32[16,1,1792]{2,1,0:T(1,128)S(1)}, u32[]{:S(2)}, u32[]{:S(2)}) async-start(s32[16,1,1792]{2,1,0:T(1,128)} %broadcast_in_dim.38), calls=%async_computation.5 | async-start | bytes 229376 | tf_op jit(solution)/shard_map/all_to_all | solution.py:17
  27.6 1.1 copy-start.1
  43.3 27.2 %all-to-all-start.1 = ((bf16[16,48,512]{2,1,0:T(8,128)(2,1)}), bf16[16,48,512]{2,1,0:T(8,128)(2,1)S(1)}, u32[]{:S(2)}, u32[]{:S(2)}) async-start(bf16[16,48,512]{2,1,0:T(8,128)(2,1)} %serve.1), calls=%async_computation.1 | async-start | bytes 1572864 | tf_op jit(solution)/shard_map/all_to_all | solution.py:17
  71.5 47.2 %all-to-all-start.3 = ((bf16[16,96,256]{2,1,0:T(8,128)(2,1)}), bf16[16,96,256]{2,1,0:T(8,128)(2,1)S(1)}, u32[]{:S(2)}, u32[]{:S(2)}) async-start(bf16[16,96,256]{2,1,0:T(8,128)(2,1)} %broadcast_in_dim.35), calls=%async_computation.3 | async-start | bytes 1572864 | tf_op jit(solution)/shard_map/all_to_all | solution.py:17
  118.7 52.8 %copy-start.9 = (s32[1,512]{1,0:T(1,128)S(1)}, s32[1,512]{1,0:T(1,128)}, u32[]{:S(2)}) copy-start(s32[1,512]{1,0:T(1,128)} %param.29) | copy-start | bytes 6148
  118.7 16.6 %all-to-all-start.2 = ((bf16[16,96,128]{2,1,0:T(8,128)(2,1)}), bf16[16,96,128]{2,1,0:T(8,128)(2,1)S(1)}, u32[]{:S(2)}, u32[]{:S(2)}) async-start(bf16[16,96,128]{2,1,0:T(8,128)(2,1)} %first_hop.1), calls=%async_computation.2 | async-start | bytes 786432 | tf_op jit(solution)/shard_map/all_to_all | solution.py:17
  136.8 34.8 %all-to-all-start.4 = ((bf16[16,128,256]{2,1,0:T(8,128)(2,1)}), bf16[16,128,256]{2,1,0:T(8,128)(2,1)S(1)}, u32[]{:S(2)}, u32[]{:S(2)}) async-start(bf16[16,128,256]{2,1,0:T(8,128)(2,1)} %broadcast_in_dim.36), calls=%async_computation.4 | async-start | bytes 2097152 | tf_op jit(solution)/shard_map/all_to_all | solution.py:17
  171.0 5.4 %slice-start = ((s8[6291456]{0:T(1024)(128)(4,1)}), s8[2097152]{0:T(1024)(128)(4,1)S(1)}, s32[]{:S(2)}) async-start(s8[6291456]{0:T(1024)(128)(4,1)} %bitcast.66), calls=%async_computation.8 | async-start | bytes 4194304
  171.5 3.3 %copy-start.5 = (bf16[256,256]{1,0:T(8,128)(2,1)S(1)}, bf16[256,256]{1,0:T(8,128)(2,1)}, u32[]{:S(2)}) copy-start(bf16[256,256]{1,0:T(8,128)(2,1)} %param.32) | copy-start | bytes 393220
  171.5 4.8 %slice-start.1 = ((s8[6291456]{0:T(1024)(128)(4,1)}), s8[4194304]{0:T(1024)(128)(4,1)S(1)}, s32[]{:S(2)}) async-start(s8[6291456]{0:T(1024)(128)(4,1)} %bitcast.66), calls=%async_computation.9 | async-start | bytes 8388608
  173.9 0.9 copy-start.3
  185.3 3.7 %copy-start.12 = (bf16[1536,256]{1,0:T(8,128)(2,1)S(1)}, bf16[1536,256]{1,0:T(8,128)(2,1)}, u32[]{:S(2)}) copy-start(bf16[1536,256]{1,0:T(8,128)(2,1)} %fusion.12) | copy-start | bytes 2359300
  185.8 3.6 %copy-start.4 = (bf16[1536,256]{1,0:T(8,128)(2,1)S(1)}, bf16[1536,256]{1,0:T(8,128)(2,1)}, u32[]{:S(2)}) copy-start(bf16[1536,256]{1,0:T(8,128)(2,1)} %copy-done.3) | copy-start | bytes 2359300
  189.0 12.2 %copy-start.11 = (bf16[1536,256]{1,0:T(8,128)(2,1)}, bf16[1536,256]{1,0:T(8,128)(2,1)S(1)}, u32[]{:S(2)}) copy-start(bf16[1536,256]{1,0:T(8,128)(2,1)S(1)} %fusion.14) | copy-start | bytes 2359300
  228.0 16.1 %all-to-all-start.7 = ((bf16[16,38,256]{2,1,0:T(8,128)(2,1)}), bf16[16,38,256]{2,1,0:T(8,128)(2,1)S(1)}, u32[]{:S(2)}, u32[]{:S(2)}) async-start(bf16[16,38,256]{2,1,0:T(8,128)(2,1)} %broadcast_in_dim.41), calls=%async_computation.7 | async-start | bytes 655360 | tf_op jit(solution)/shard_map/all_to_all | solution.py:17

commit v2 on v1

--- a/solution.py
+++ b/solution.py
@@ -70,67 +70,138 @@
     )(ids, features_t)
 
 
-def hop_kernel(fan, ids_ref, self_ref, front_ref, inv_ref, out_ref, table, own, total):
+def count_kernel(keys_ref, lows_ref, out_ref, marks):
+    chunks, _, chunk = out_ref.shape
+    spans = chunks * chunk // 256
+    across = chunk // 256
+
+    @pl.when(pl.program_id(0) == 0)
+    def _():
+        marks[...] = lax.broadcasted_iota(jnp.int32, (256, 256), 0).astype(F32).astype(BF)
+
+    def stretch(row, rows):
+        small = jnp.broadcast_to(row, (16, 256)).astype(BF)
+        return jnp.concatenate([small] * (rows // 16), axis=0)
+
+    def block(at, _):
+        one = jnp.ones((256, 256), BF)
+        zero = jnp.zeros((256, 256), BF)
+        low = stretch(lows_ref[pl.ds(at, 1), :], 256)
+        right = jnp.where(low == marks[...], one, zero)
+        place = pl.multiple_of(at * 16, 16)
+        for first in range(0, spans, 16):
+            size = min(16, spans - first)
+            key = stretch(keys_ref[pl.ds(at, 1), :] - float(first * 16), size * 16)
+            left = jnp.where(key == marks[0 : size * 16, :], one[: size * 16], zero[: size * 16])
+            part = dot(left, right, ((1,), (1,))).astype(BF)
+            for inner in range(size):
+                span = first + inner
+                lane = (span % across) * 256
+                out_ref[span // across, pl.ds(place, 16), lane : lane + 256] = part[
+                    inner * 16 : (inner + 1) * 16
+                ]
+        return 0
+
+    lax.fori_loop(0, 16, block, 0, unroll=8)
+
+
+def count_matrix(highs, lows, total, chunk):
+    fan, nodes = highs.shape
+
+    def order(value):
+        return value.reshape(fan, nodes // 16, 16).transpose(1, 0, 2).reshape(nodes // 16, -1)
+
+    node = (lax.broadcasted_iota(jnp.int32, (fan, nodes), 1) % 16).astype(F32)
+    keys = order(highs * 16.0 + node)
+    return pl.pallas_call(
+        count_kernel,
+        grid=(nodes // 256,),
+        out_shape=jax.ShapeDtypeStruct((total // chunk, nodes, chunk), BF),
+        in_specs=[
+            pl.BlockSpec((16, 256), lambda at: (at, 0)),
+            pl.BlockSpec((16, 256), lambda at: (at, 0)),
+        ],
+        out_specs=pl.BlockSpec((total // chunk, 256, chunk), lambda at: (0, at, 0)),
+        scratch_shapes=[pltpu.VMEM((256, 256), BF)],
+        compiler_params=pltpu.CompilerParams(vmem_limit_bytes=VMEM_LIMIT),
+        cost_estimate=pl.CostEstimate(
+            flops=2 * nodes * total * 256 // 16 * 16,
+            bytes_accessed=2 * nodes * total,
+            transcendentals=0,
+        ),
+        name="count_matrix",
+    )(keys, order(lows))
+
+
+def hop_kernel(self_ref, counts_ref, front_ref, inv_ref, out_ref, table, total, own):
     owners, width, cap = front_ref.shape
-    nodes = out_ref.shape[0] * out_ref.shape[2]
-    block = out_ref.shape[2]
-
-    def fill(owner, _):
-        at = pl.multiple_of(owner * cap, cap)
-        table[pl.ds(at, cap), 0:width] = front_ref[owner].astype(F32).T
-        return 0
-
-    lax.fori_loop(0, owners, fill, 0)
-    table[pl.ds(owners * cap, 8), :] = jnp.zeros((8, 128), F32)
-
-    def per_block(dest, _):
-        base = dest * block
-
-        def pick(at, _):
-            for lane in range(8):
-                row = at * 8 + lane
-                node = base + row
-                rows = [
-                    table[pl.ds(ids_ref[node * fan + slot], 1), :] for slot in range(fan)
-                ]
-                while len(rows) > 1:
-                    rows = [rows[at] + rows[at + 1] for at in range(0, len(rows), 2)]
-                total[pl.ds(row, 1), :] = rows[0]
-                own[pl.ds(row, 1), :] = table[pl.ds(self_ref[node], 1), :]
+    blocks, _, block = out_ref.shape
+    step = pl.program_id(0)
+    parts = []
+    for owner in range(owners):
+        rows = front_ref[owner].astype(F32).T
+        at = pl.multiple_of((step * owners + owner) * cap, cap)
+        table[pl.ds(at, cap), 0:width] = rows
+        parts.append(rows.astype(BF))
+    part = dot(counts_ref[0], jnp.concatenate(parts, axis=0), ((1,), (0,)))
+
+    @pl.when(step == 0)
+    def _():
+        total[...] = part
+
+    @pl.when(step > 0)
+    def _():
+        total[...] += part
+
+    @pl.when(step == pl.num_programs(0) - 1)
+    def _():
+        def per_block(dest, _):
+            base = pl.multiple_of(dest * block, block)
+
+            def pick(at, _):
+                for lane in range(32):
+                    row = at * 32 + lane
+                    own[pl.ds(row, 1), :] = table[pl.ds(self_ref[base + row], 1), :]
+                return 0
+
+            lax.fori_loop(0, block // 32, pick, 0)
+            out_ref[dest, 0:width, :] = own[:, 0:width].T.astype(BF)
+            mean = total[pl.ds(base, block), :].T * inv_ref[pl.ds(dest, 1), :]
+            out_ref[dest, width : 2 * width, :] = mean.astype(BF)
             return 0
 
-        lax.fori_loop(0, block // 8, pick, 0)
-        out_ref[dest, 0:width, :] = own[:, 0:width].T.astype(out_ref.dtype)
-        inv = inv_ref[pl.ds(dest, 1), :]
-        out_ref[dest, width : 2 * width, :] = (total[:, 0:width].T * inv).astype(out_ref.dtype)
-        return 0
-
-    lax.fori_loop(0, out_ref.shape[0], per_block, 0)
-
-
-def hop(frontier, ids, self_ids, inv, blocks):
+        lax.fori_loop(0, blocks, per_block, 0)
+
+
+def hop(frontier, counts, self_ids, inv, blocks):
     owners, width, cap = frontier.shape
-    nodes = self_ids.shape[0]
-    fan = ids.shape[0] // nodes
+    chunks, nodes, chunk = counts.shape
     block = nodes // blocks
+    per = chunk // cap
     return pl.pallas_call(
-        functools.partial(hop_kernel, fan),
-        out_shape=jax.ShapeDtypeStruct((blocks, 2 * width, block), frontier.dtype),
+        hop_kernel,
+        grid=(chunks,),
+        out_shape=jax.ShapeDtypeStruct((blocks, 2 * width, block), BF),
         in_specs=[
             pl.BlockSpec(memory_space=pltpu.SMEM),
-            pl.BlockSpec(memory_space=pltpu.SMEM),
-            pl.BlockSpec(memory_space=pltpu.VMEM),
-            pl.BlockSpec(memory_space=pltpu.VMEM),
-        ],
-        out_specs=pl.BlockSpec(memory_space=pltpu.VMEM),
+            pl.BlockSpec((1, nodes, chunk), lambda at: (at, 0, 0)),
+            pl.BlockSpec((per, width, cap), lambda at: (at, 0, 0)),
+            pl.BlockSpec(inv.shape, lambda at: (0, 0)),
+        ],
+        out_specs=pl.BlockSpec((blocks, 2 * width, block), lambda at: (0, 0, 0)),
         scratch_shapes=[
-            pltpu.VMEM((owners * cap + 8, 128), F32),
+            pltpu.VMEM((owners * cap, 128), F32),
+            pltpu.VMEM((nodes, width), F32),
             pltpu.VMEM((block, 128), F32),
-            pltpu.VMEM((block, 128), F32),
         ],
         compiler_params=pltpu.CompilerParams(vmem_limit_bytes=VMEM_LIMIT),
+        cost_estimate=pl.CostEstimate(
+            flops=2 * nodes * chunks * chunk * 128,
+            bytes_accessed=2 * nodes * chunks * chunk,
+            transcendentals=0,
+        ),
         name="first_hop",
-    )(ids, self_ids, frontier, inv)
+    )(self_ids, counts, frontier, inv)
 
 
 def one_hot(ids, total):
@@ -138,13 +209,8 @@
     return (ids[:, None] == marks).astype(BF)
 
 
-def count_hot(ids, counts, total):
-    marks = lax.broadcasted_iota(jnp.int32, (ids.shape[1], total), 1)
-    result = jnp.zeros((ids.shape[1], total), F32)
-    for slot in range(ids.shape[0]):
-        live = jnp.where(slot < counts, ids[slot], -1)
-        result = result + (live[:, None] == marks).astype(F32)
-    return result.astype(BF)
+def halves(ids):
+    return (ids // 256).astype(F32), (ids % 256).astype(F32)
 
 
 def local(
@@ -177,43 +243,60 @@
     pair_share = pos_pairs.shape[2]
 
     asked = swap(frontier_ids[0], "graph")
-    weights = gather_all(jnp.concatenate([first_self, first_neigh], axis=0), "feat")
-    packed = jnp.concatenate(
-        [
-            self_two_ids[0],
-            count_two[0],
-            neigh_two_ids[0].reshape(-1),
-            pos_pairs[0].reshape(-1),
-        ]
-    )
-    packed = gather_all(packed, "feat")
-    self_two = packed[:, :share].reshape(-1)
-    counts_two = packed[:, share : 2 * share].reshape(-1)
-    neigh_two = packed[:, 2 * share : (2 + fan) * share].reshape(feats, fan, share)
-    neigh_two = neigh_two.transpose(1, 0, 2).reshape(fan, -1)
-    pairs = packed[:, (2 + fan) * share :].reshape(feats, 2, pair_share)
+
+    slots = lax.broadcasted_iota(jnp.int32, (fan, 1), 0)
+    neigh_high, neigh_low = halves(neigh_two_ids[0])
+    neigh_low = jnp.where(slots < count_two, neigh_low, -1.0)
+    fields = [*halves(self_two_ids), count_two.astype(F32), neigh_high, neigh_low]
+    fields = [field.reshape(-1) for field in fields + list(halves(pos_pairs[0]))]
+    field_sizes = [field.shape[0] for field in fields]
+    spare = -sum(field_sizes) % (16 * hidden_width)
+    fields = jnp.concatenate(fields + [jnp.zeros((spare,), F32)]).astype(BF)
+    early = jnp.concatenate(
+        [first_self, first_neigh, fields.reshape(-1, hidden_width)], axis=0
+    )
+    early = gather_all(early, "feat")
+
+    served = serve(features.T, asked.reshape(-1), graphs, cap)
+    one_ids, served = lax.optimization_barrier((neigh_one_ids[0], served))
+    one_high, one_low = halves(one_ids)
+    one_low = jnp.where(slots < count_one, one_low, -1.0)
+    one_counts = count_matrix(one_high, one_low, front, 2 * cap)
+    inv_one = (1.0 / count_one.astype(F32)).reshape(feats, -1)
+    frontier = swap(served, "graph")
+    frontier, early = lax.optimization_barrier((frontier, early))
+    rows_one = hop(frontier, one_counts, self_one_ids[0], inv_one, feats)
+    rows_one, early = lax.optimization_barrier((rows_one, early))
+    mine = swap(rows_one, "feat")
+
+    weights = early[:, : 2 * width].reshape(feats * 2 * width, hidden_width)
+    sent = early[:, 2 * width :].reshape(feats, -1).astype(F32)
+    got = []
+    start = 0
+    for size in field_sizes:
+        got.append(sent[:, start : start + size])
+        start += size
+    self_two = (got[0] * 256.0 + got[1]).astype(jnp.int32).reshape(-1)
+    counts_two = got[2].reshape(-1)
+    neigh_high, neigh_low = (
+        value.reshape(feats, fan, share).transpose(1, 0, 2).reshape(fan, -1) for value in got[3:5]
+    )
+    pairs = (got[5] * 256.0 + got[6]).astype(jnp.int32).reshape(feats, 2, pair_share)
     pairs = pairs.transpose(1, 0, 2).reshape(2, -1)
     targets_total = self_two.shape[0]
-
-    slots = lax.broadcasted_iota(jnp.int32, (fan, nodes), 0)
-    live_ids = jnp.where(slots < count_one, neigh_one_ids[0], front).T.reshape(-1)
-    inv_one = (1.0 / count_one.astype(F32)).reshape(feats, -1)
-
-    served = serve(features.T, asked.reshape(-1), graphs, cap)
-    frontier = swap(served, "graph")
-    rows_one = hop(frontier, live_ids, self_one_ids[0], inv_one, feats)
-    mine = swap(rows_one, "feat")
-    hidden_pre = dot(
-        mine.reshape(feats * 2 * width, -1),
-        weights.reshape(feats * 2 * width, hidden_width),
-        ((0,), (0,)),
-    )
+    pair_total = pairs.shape[1]
+    pick_neigh = count_matrix(neigh_high, neigh_low, nodes, nodes)[0]
+    pick_self = one_hot(self_two, nodes)
+    pick_ends = one_hot(jnp.concatenate([pairs[0], pairs[1], neg_ids[0]]), targets_total)
+    pick_self, pick_ends = lax.optimization_barrier(
+        (pick_self, pick_ends)
+    )
+
+    hidden_pre = dot(mine.reshape(feats * 2 * width, -1), weights, ((0,), (0,)))
     hidden = gather_all(jnp.maximum(hidden_pre, 0.0).astype(BF), "feat")
     hidden = hidden.reshape(nodes, hidden_width)
 
-    pick_self = one_hot(self_two, nodes)
-    pick_neigh = count_hot(neigh_two, counts_two, nodes)
-    inv_two = (1.0 / counts_two.astype(F32))[:, None]
+    inv_two = (1.0 / counts_two)[:, None]
     hidden_self = dot(pick_self, hidden, ((1,), (0,))).astype(BF)
     hidden_neigh = (dot(pick_neigh, hidden, ((1,), (0,))) * inv_two).astype(BF)
     embed = (
@@ -221,9 +304,6 @@
         + dot(hidden_neigh, second_neigh, ((1,), (0,)))
     ).astype(BF)
 
-    pair_total = pairs.shape[1]
-    ends = jnp.concatenate([pairs[0], pairs[1], neg_ids[0]])
-    pick_ends = one_hot(ends, targets_total)
     end_rows = dot(pick_ends, embed, ((1,), (0,))).astype(BF)
     source_rows = end_rows[:pair_total]
     dest_rows = end_rows[pair_total : 2 * pair_total]
@@ -249,20 +329,19 @@
     grad_sn = dot(hidden_neigh, embed_grad, ((0,), (0,)))
     self_back = dot(embed_grad, second_self, ((1,), (1,))).astype(BF)
     neigh_back = (dot(embed_grad, second_neigh, ((1,), (1,))) * inv_two).astype(BF)
-    hidden_grad = dot(pick_self, self_back, ((0,), (0,))) + dot(
-        pick_neigh, neigh_back, ((0,), (0,))
-    )
-    pre_grad = jnp.where(hidden > 0, hidden_grad, 0.0).astype(BF)
+    hidden_grad = dot(self_back, pick_self, ((0,), (0,))) + dot(
+        neigh_back, pick_neigh, ((0,), (0,))
+    )
+    pre_grad = jnp.where(hidden.T > 0, hidden_grad, 0.0).astype(BF)
     first_part = dot(
-        rows_one.transpose(1, 0, 2).reshape(2 * width, nodes), pre_grad, ((1,), (0,))
+        rows_one.transpose(1, 0, 2).reshape(2 * width, nodes), pre_grad, ((1,), (1,))
     )
 
     loss_high = loss_part.astype(BF)
     loss_mid = (loss_part - loss_high.astype(F32)).astype(BF)
     loss_low = (loss_part - loss_high.astype(F32) - loss_mid.astype(F32)).astype(BF)
-    loss_row = jnp.zeros((graphs, 1, hidden_width), BF)
-    loss_row = loss_row.at[:, 0, 0].set(loss_high).at[:, 0, 1].set(loss_mid)
-    loss_row = loss_row.at[:, 0, 2].set(loss_low)
+    lanes = lax.broadcasted_iota(jnp.int32, (graphs, 1, hidden_width), 2)
+    loss_row = jnp.where(lanes == 1, loss_mid, jnp.where(lanes == 2, loss_low, loss_high))
     parts = jnp.concatenate(
         [
             first_part.astype(BF).reshape(graphs, -1, hidden_width),

time: 248 us -> 208 us (0.84)
  other arithmetic: 35.5 us -> 11.1 us
  waiting for transfers between devices: 44.4 us -> 34.6 us
  local copies, waits for them, and re-layouts: 20.6 us -> 12.5 us
  starting transfers between devices: 42.1 us -> 34.8 us
  matrix products: 30.5 us -> 36.4 us
  Pallas kernels: 53.2 us -> 57.9 us
    convert_element_type x1 -> x4, other arithmetic: 30.5 us -> 6.71 us  [the longest x2 6.61 us: one_hot(): return (ids[:, None] == marks).astype(BF)]
    all_to_all x7 -> x6, waiting for transfers between devices: 44.4 us -> 34.6 us  [swap(): return lax.all_to_all(value, axis, split_axis=0, concat_axis=0, tiled=True)]
    all_to_all x7 -> x6, starting transfers between devices: 42.1 us -> 34.8 us  [swap(): return lax.all_to_all(value, axis, split_axis=0, concat_axis=0, tiled=True)]
    dot_general x14, matrix products: 30.5 us -> 36.4 us  [dot(): lax.dot_general(former, latter, (dims, ((), ())), preferred_element_type=...]
    pallas_call x1 -> x3, Pallas kernels: 38.6 us -> 43.3 us  [the longest x2 22.4 us: count_matrix(): pl.pallas_call(count_kernel, grid=(nodes // 256,), out_shape=jax.ShapeDty...]
    scatter x5 -> x0, local copies, waits for them, and re-layouts: 3.75 us -> none  [the longest x4 1.89 us: local(): loss_row = loss_row.at[:, 0, 0].set(loss_high).at[:, 0, 1].set(loss_mid)]
  transfers between devices with their start and end apart: 7 -> 6, of which waited for: 4 -> 6; matrix products, arithmetic and copies ran while one was open for 16% -> 7% of each run, Pallas kernels for 21% -> 18%
where the time goes in v2:
time: 208 us; the launch traced here: 207 us
  Pallas kernels  57.9 us (28%)
  matrix products  36.4 us (18%)
  starting transfers between devices  34.8 us (17%)
  waiting for transfers between devices  34.6 us (17%)
  blocking collectives  15.9 us (8%)
  local copies, waits for them, and re-layouts  12.5 us (6%)
  other arithmetic  11.1 us (5%)
  between operations  4.18 us (2%)
    dot_general x14, matrix products, dot(): lax.dot_general(former, latter, (dims, ((), ())), preferred_element_type=...  36.4 us
    all_to_all x6, starting transfers between devices, swap(): return lax.all_to_all(value, axis, split_axis=0, concat_axis=0, tiled=True)  34.8 us
    all_to_all x6, waiting for transfers between devices, swap(): return lax.all_to_all(value, axis, split_axis=0, concat_axis=0, tiled=True)  34.6 us
    pallas_call x2, Pallas kernels, count_matrix(): pl.pallas_call(count_kernel, grid=(nodes // 256,), out_shape=jax.ShapeDty...  22.4 us
    pallas_call x1, Pallas kernels, hop(): pl.pallas_call(hop_kernel, grid=(chunks,), out_shape=jax.ShapeDtypeStruct...  20.9 us
    all_to_all x1, blocking collectives, swap(): return lax.all_to_all(value, axis, split_axis=0, concat_axis=0, tiled=True)  15.9 us
    pallas_call x1, Pallas kernels, serve(): pl.pallas_call(serve_kernel, out_shape=jax.ShapeDtypeStruct((groups, widt...  14.6 us
    convert_element_type x2, other arithmetic, one_hot(): return (ids[:, None] == marks).astype(BF)  6.61 us
  transfers between devices with their start and end apart: 6, of which 6 were waited for; matrix products, arithmetic and copies ran while one was open for 7% of the time, Pallas kernels for 18%

profile of v2, /device:TPU:1, one launch (start us, length us, event | category | flops | bytes accessed | tf_op | source)
XLA Modules:
  0.0 207.3 jit_solution(8826330321573913803)
XLA Ops:
  0.7 1.5 all_to_all.24
  2.1 10.0 %all-to-all-start = ((s32[16,1,512]{2,1,0:T(1,128)}), s32[16,1,512]{2,1,0:T(1,128)S(1)}, u32[]{:S(2)}, u32[]{:S(2)}) async-start(s32[16,1,512]{2,1,0:T(1,128)} %all_to_all.24), calls=%async_computation | async-start | bytes 65536 | tf_op jit(solution)/shard_map/all_to_all | solution.py:17
  12.1 0.8 squeeze.28
  12.9 0.7 fusion.74
  13.6 0.7 iota_compare_fusion.3
  14.4 0.8 squeeze.29
  15.3 0.8 pad_maximum_fusion.1
  16.0 3.5 %all-to-all-done = s32[16,1,512]{2,1,0:T(1,128)S(1)} async-done(((s32[16,1,512]{2,1,0:T(1,128)}), s32[16,1,512]{2,1,0:T(1,128)S(1)}, u32[]{:S(2)}, u32[]{:S(2)}) %all-to-all-start) | async-done | bytes 32800 | tf_op jit(solution)/shard_map/all_to_all | solution.py:17
  19.5 1.0 broadcast_in_dim.51
  20.5 6.9 %all-to-all-start.2 = ((bf16[16,112,256]{2,1,0:T(8,128)(2,1)}), bf16[16,112,256]{2,1,0:T(8,128)(2,1)S(1)}, u32[]{:S(2)}, u32[]{:S(2)}) async-start(bf16[16,112,256]{2,1,0:T(8,128)(2,1)} %broadcast_in_dim.51), calls=%async_computation.2 | async-start | bytes 1835008 | tf_op jit(solution)/shard_map/all_to_all | solution.py:17
  27.5 14.6 %serve.1 = bf16[16,48,512]{2,1,0:T(8,128)(2,1)} custom-call(s32[8192]{0:T(1024)S(1)} %bitcast.99, bf16[48,8192]{1,0:T(8,128)(2,1)S(1)} %bitcast.98), custom_call_target="tpu_custom_call" | custom-call | tf_op jit(solution)/shard_map/serve/pallas_call | solution.py:59
  42.1 0.2 all-to-all-done.2
  42.3 5.4 %all-to-all-start.1 = ((bf16[16,48,512]{2,1,0:T(8,128)(2,1)}), bf16[16,48,512]{2,1,0:T(8,128)(2,1)S(1)}, u32[]{:S(2)}, u32[]{:S(2)}) async-start(bf16[16,48,512]{2,1,0:T(8,128)(2,1)} %serve.1), calls=%async_computation.1 | async-start | bytes 1572864 | tf_op jit(solution)/shard_map/all_to_all | solution.py:17
  47.7 0.2 fusion.54
  47.9 0.4 reshape.204
  48.2 0.3 copy.42
  48.5 0.1 copy.44.keys_ref
  48.7 0.4 reshape.206
  49.0 0.3 copy.43
  49.5 15.4 %count_matrix.2.counts_ref = bf16[8,2048,1024]{2,1,0:T(8,128)(2,1)} custom-call(f32[128,256]{1,0:T(8,128)S(1)} %copy.44.keys_ref, f32[128,256]{1,0:T(8,128)S(1)} %copy.45.lows_ref), custom_call_target="tpu_custom_call" | custom-call | flops 8589934592 | bytes 33554432 | tf_op jit(solution)/shard_map/count_matrix/pallas_call | solution.py:116
  64.8 5.6 %all-to-all-done.1.front_ref = bf16[16,48,512]{2,1,0:T(8,128)(2,1)S(1)} async-done(((bf16[16,48,512]{2,1,0:T(8,128)(2,1)}), bf16[16,48,512]{2,1,0:T(8,128)(2,1)S(1)}, u32[]{:S(2)}, u32[]{:S(2)}) %all-to-all-start.1) | async-done | bytes 786464 | tf_op jit(solution)/shard_map/all_to_all | solution.py:17
  70.4 20.9 %first_hop.1 = bf16[16,96,128]{2,1,0:T(8,128)(2,1)} custom-call(s32[2048]{0:T(1024)S(1)} %bitcast.101, bf16[8,2048,1024]{2,1,0:T(8,128)(2,1)} %count_matrix.2.counts_ref, bf16[16,48,512]{2,1,0:T(8,128)(2,1)S(1)} %all-to-all-done.1.front_ref, f32[16,128]{1,0:T(8,128)S(1)} %bitcast.100), custom_call_target="tpu_custom_call" | custom-call | flops 4294967296 | bytes 33554432 | tf_op jit(solution)/shard_map/first_hop/pallas_call | solution.py:181
  91.3 0.2 copy.57
  91.5 0.1 fusion.80
  91.8 0.2 mul.103
  92.1 5.4 %all-to-all-start.3 = ((bf16[16,96,128]{2,1,0:T(8,128)(2,1)}), bf16[16,96,128]{2,1,0:T(8,128)(2,1)S(1)}, u32[]{:S(2)}, u32[]{:S(2)}) async-start(bf16[16,96,128]{2,1,0:T(8,128)(2,1)} %first_hop.1), calls=%async_computation.3 | async-start | bytes 786432 | tf_op jit(solution)/shard_map/all_to_all | solution.py:17
  97.8 2.9 %fusion.1 = bf16[1536,1536]{1,0:T(8,128)(2,1)} fusion(s32[1536]{0:T(1024)S(1)} %pad_add_fusion), kind=kLoop, calls=%fused_computation.3 | loop fusion | flops 4718592 | bytes 4724736 | tf_op jit(solution)/shard_map/convert_element_type | solution.py:209
  100.8 0.2 copy.50
  101.3 0.2 reshape_reshape.3
  101.6 0.2 copy.52
  102.1 4.6 %all-to-all-done.3 = bf16[16,96,128]{2,1,0:T(8,128)(2,1)S(1)} async-done(((bf16[16,96,128]{2,1,0:T(8,128)(2,1)}), bf16[16,96,128]{2,1,0:T(8,128)(2,1)S(1)}, u32[]{:S(2)}, u32[]{:S(2)}) %all-to-all-start.3) | async-done | bytes 393248 | tf_op jit(solution)/shard_map/all_to_all | solution.py:17
  106.7 0.3 fusion.28
  107.1 0.1 copy.47
  107.2 1.2 broadcast_in_dim.52
  108.4 3.7 %all-to-all-start.4 = ((bf16[16,128,256]{1,2,0:T(8,128)(2,1)}), bf16[16,128,256]{1,2,0:T(8,128)(2,1)S(1)}, u32[]{:S(2)}, u32[]{:S(2)}) async-start(bf16[16,128,256]{1,2,0:T(8,128)(2,1)} %broadcast_in_dim.52), calls=%async_computation.4 | async-start | bytes 2097152 | tf_op jit(solution)/shard_map/all_to_all | solution.py:17
  112.0 3.7 %fusion = bf16[1536,2048]{1,0:T(8,128)(2,1)} fusion(s32[1536]{0:T(1024)S(1)} %eq.43), kind=kLoop, calls=%fused_computation.1 | loop fusion | flops 6291456 | bytes 6297600 | tf_op jit(solution)/shard_map/convert_element_type | solution.py:209
  115.7 7.0 %count_matrix.3 = bf16[1,1536,2048]{2,1,0:T(8,128)(2,1)} custom-call(f32[96,256]{1,0:T(8,128)S(1)} %copy.53.keys_ref, f32[96,256]{1,0:T(8,128)S(1)} %copy.54.lows_ref), custom_call_target="tpu_custom_call" | custom-call | flops 1610612736 | bytes 6291456 | tf_op jit(solution)/shard_map/count_matrix/pallas_call | solution.py:116
  122.8 9.3 %all-to-all-done.4 = bf16[16,128,256]{1,2,0:T(8,128)(2,1)S(1)} async-done(((bf16[16,128,256]{1,2,0:T(8,128)(2,1)}), bf16[16,128,256]{1,2,0:T(8,128)(2,1)S(1)}, u32[]{:S(2)}, u32[]{:S(2)}) %all-to-all-start.4) | async-done | bytes 1048608 | tf_op jit(solution)/shard_map/all_to_all | solution.py:17
  132.1 4.8 %convolution_convert_fusion.1 = bf16[1536,256]{1,0:T(8,128)(2,1)S(1)} fusion(bf16[1536,2048]{1,0:T(8,128)(2,1)} %fusion, bf16[16,128,256]{1,2,0:T(8,128)(2,1)S(1)} %all-to-all-done.4), kind=kOutput, calls=%fused_computation.19 | convolution fusion | flops 1611005952 | bytes 8126464 | tf_op jit(solution)/shard_map/dot_general | solution.py:26
  136.8 0.4 fusion.81
  137.2 0.5 copy-done.4
  137.7 2.8 %fusion.20 = bf16[1536,256]{1,0:T(8,128)(2,1)} fusion(bf16[1,1536,2048]{2,1,0:T(8,128)(2,1)S(1)} %copy-done.3, f32[1536]{0:T(1024)S(1)} %div.110, bf16[16,128,256]{1,2,0:T(8,128)(2,1)S(1)} %all-to-all-done.4), kind=kOutput, calls=%fused_computation.18 | convolution fusion | flops 1611399168 | bytes 8132608 | tf_op jit(solution)/shard_map/dot_general | solution.py:26
  140.5 5.4 %convolution_convert_fusion.3 = bf16[1536,256]{1,0:T(8,128)(2,1)} fusion(bf16[1536,1536]{1,0:T(8,128)(2,1)} %fusion.1, f32[1536,256]{1,0:T(8,128)S(1)} %fusion.81, bf16[1536,256]{1,0:T(8,128)(2,1)} %fusion.20, bf16[256,256]{1,0:T(8,128)(2,1)S(1)} %copy-done.10), kind=kOutput, calls=%fused_computation.21 | convolution fusion | flops 1410465792 | bytes 7995392 | tf_op jit(solution)/shard_map/dot_general | solution.py:26
  145.9 2.8 %multiply_convert_fusion = (bf16[512,512]{1,0:T(8,128)(2,1)S(1)}, f32[]{:T(128)}) fusion(bf16[1536,256]{1,0:T(8,128)(2,1)} %convolution_convert_fusion.3), kind=kOutput, calls=%fused_computation.38 | convolution fusion | flops 137625600 | bytes 1048580 | tf_op jit(solution)/shard_map/dot_general | solution.py:26
  148.8 0.1 fusion.43
  148.9 0.6 divide_negate_fusion
  149.6 0.1 fusion.42
  149.7 0.3 fusion.25
  150.0 0.3 fusion.26
  150.4 2.3 %convolution_convert_fusion.2 = bf16[1536,256]{1,0:T(8,128)(2,1)} fusion(bf16[1536,1536]{1,0:T(8,128)(2,1)S(1)} %bitcast.103, bf16[512,256]{1,0:T(8,128)(2,1)S(1)} %fusion.26, bf16[512,256]{1,0:T(8,128)(2,1)S(1)} %fusion.42, bf16[512,256]{1,0:T(8,128)(2,1)S(1)} %fusion.25), kind=kOutput, calls=%fused_computation.20 | convolution fusion | flops 1210712064 | bytes 6291456 | tf_op jit(solution)/shard_map/dot_general | solution.py:26
  152.7 6.9 %fusion.24 = f32[256,2048]{1,0:T(8,128)} fusion(bf16[1536,2048]{1,0:T(8,128)(2,1)} %fusion, bf16[1536,256]{1,0:T(8,128)(2,1)} %convolution_convert_fusion.2, bf16[256,256]{1,0:T(8,128)(2,1)S(1)} %copy-done), kind=kOutput, calls=%fused_computation.26 | convolution fusion | flops 1812332544 | bytes 9306112 | tf_op jit(solution)/shard_map/dot_general | solution.py:26
  159.6 0.4 convolution_convert_fusion.5
  160.1 1.8 convolution_convert_fusion.4
  161.9 6.3 %fusion.15 = bf16[256,2048]{1,0:T(8,128)(2,1)S(1)} fusion(f32[256,2048]{1,0:T(8,128)} %fusion.24, bf16[1,1536,2048]{2,1,0:T(8,128)(2,1)} %count_matrix.3, bf16[1536,256]{1,0:T(8,128)(2,1)} %convolution_convert_fusion.2, bf16[256,256]{1,0:T(8,128)(2,1)S(1)} %copy-done.10, f32[1536]{0:T(1024)S(1)} %div.110, bf16[16,128,256]{1,2,0:T(8,128)(2,1)S(1)} %all-to-all-done.4), kind=kOutput, calls=%fused_computation.14 | convolution fusion | flops 1815871488 | bytes 11409408 | tf_op jit(solution)/shard_map/dot_general | solution.py:26
  168.2 1.5 convolution_convert_fusion.6
  171.0 0.2 pad_maximum_fusion
  171.2 15.9 %all_to_all.39 = bf16[16,39,256]{2,1,0:T(8,128)(2,1)S(1)} all-to-all(bf16[16,39,256]{2,1,0:T(8,128)(2,1)S(1)} %pad_maximum_fusion), channel_id=1, replica_groups=mesh['graph'=16,'feat'=16] {'graph'}, dimensions={0} | all-to-all | bytes 638976 | tf_op jit(solution)/shard_map/all_to_all | solution.py:17
  187.1 0.7 broadcast_in_dim.57
  187.9 3.4 %all-to-all-start.6 = ((bf16[16,38,256]{2,1,0:T(8,128)(2,1)}), bf16[16,38,256]{2,1,0:T(8,128)(2,1)S(1)}, u32[]{:S(2)}, u32[]{:S(2)}) async-start(bf16[16,38,256]{2,1,0:T(8,128)(2,1)} %broadcast_in_dim.57), calls=%async_computation.6 | async-start | bytes 655360 | tf_op jit(solution)/shard_map/all_to_all | solution.py:17
  191.3 0.6 slice_reduce_fusion.2
  192.6 11.4 %all-to-all-done.6 = bf16[16,38,256]{2,1,0:T(8,128)(2,1)S(1)} async-done(((bf16[16,38,256]{2,1,0:T(8,128)(2,1)}), bf16[16,38,256]{2,1,0:T(8,128)(2,1)S(1)}, u32[]{:S(2)}, u32[]{:S(2)}) %all-to-all-start.6) | async-done | bytes 311328 | tf_op jit(solution)/shard_map/all_to_all | solution.py:17
  204.0 0.6 slice.88
  204.7 0.6 slice.90
  205.3 0.9 fusion.78
  (65 shorter events, 1.7 us)
Async XLA Ops:
  0.6 136.2 %copy-start = (bf16[256,256]{1,0:T(8,128)(2,1)S(1)}, bf16[256,256]{1,0:T(8,128)(2,1)}, u32[]{:S(2)}) copy-start(bf16[256,256]{1,0:T(8,128)(2,1)} %param.26) | copy-start | bytes 393220
  0.6 26.8 %copy-start.8 = (s32[1,2048]{1,0:T(1,128)S(1)}, s32[1,2048]{1,0:T(1,128)}, u32[]{:S(2)}) copy-start(s32[1,2048]{1,0:T(1,128)} %param.18) | copy-start | bytes 24580
  0.7 26.8 %copy-start.1 = (bf16[8192,48]{0,1:T(8,128)(2,1)S(1)}, bf16[8192,48]{0,1:T(8,128)(2,1)}, u32[]{:S(2)}) copy-start(bf16[8192,48]{0,1:T(8,128)(2,1)} %param.14) | copy-start | bytes 2359300
  2.1 17.4 %all-to-all-start = ((s32[16,1,512]{2,1,0:T(1,128)}), s32[16,1,512]{2,1,0:T(1,128)S(1)}, u32[]{:S(2)}, u32[]{:S(2)}) async-start(s32[16,1,512]{2,1,0:T(1,128)} %all_to_all.24), calls=%async_computation | async-start | bytes 65536 | tf_op jit(solution)/shard_map/all_to_all | solution.py:17
  20.5 27.2 %copy-start.7 = (s32[1,16,2048]{2,1,0:T(8,128)S(1)}, s32[1,16,2048]{2,1,0:T(8,128)}, u32[]{:S(2)}) copy-start(s32[1,16,2048]{2,1,0:T(8,128)} %param.17) | copy-start | bytes 393220
  20.5 21.8 %all-to-all-start.2 = ((bf16[16,112,256]{2,1,0:T(8,128)(2,1)}), bf16[16,112,256]{2,1,0:T(8,128)(2,1)S(1)}, u32[]{:S(2)}, u32[]{:S(2)}) async-start(bf16[16,112,256]{2,1,0:T(8,128)(2,1)} %broadcast_in_dim.51), calls=%async_computation.2 | async-start | bytes 1835008 | tf_op jit(solution)/shard_map/all_to_all | solution.py:17
  42.3 28.1 %all-to-all-start.1 = ((bf16[16,48,512]{2,1,0:T(8,128)(2,1)}), bf16[16,48,512]{2,1,0:T(8,128)(2,1)S(1)}, u32[]{:S(2)}, u32[]{:S(2)}) async-start(bf16[16,48,512]{2,1,0:T(8,128)(2,1)} %serve.1), calls=%async_computation.1 | async-start | bytes 1572864 | tf_op jit(solution)/shard_map/all_to_all | solution.py:17
  49.4 21.0 %copy-start.2 = (s32[1,2048]{1,0:T(1,128)S(1)}, s32[1,2048]{1,0:T(1,128)}, u32[]{:S(2)}) copy-start(s32[1,2048]{1,0:T(1,128)} %param.16) | copy-start | bytes 24580
  91.3 6.5 %copy-start.9 = (s32[1,512]{1,0:T(1,128)S(1)}, s32[1,512]{1,0:T(1,128)}, u32[]{:S(2)}) copy-start(s32[1,512]{1,0:T(1,128)} %param.23) | copy-start | bytes 6148
  92.1 14.7 %all-to-all-start.3 = ((bf16[16,96,128]{2,1,0:T(8,128)(2,1)}), bf16[16,96,128]{2,1,0:T(8,128)(2,1)S(1)}, u32[]{:S(2)}, u32[]{:S(2)}) async-start(bf16[16,96,128]{2,1,0:T(8,128)(2,1)} %first_hop.1), calls=%async_computation.3 | async-start | bytes 786432 | tf_op jit(solution)/shard_map/all_to_all | solution.py:17
  108.4 23.7 %all-to-all-start.4 = ((bf16[16,128,256]{1,2,0:T(8,128)(2,1)}), bf16[16,128,256]{1,2,0:T(8,128)(2,1)S(1)}, u32[]{:S(2)}, u32[]{:S(2)}) async-start(bf16[16,128,256]{1,2,0:T(8,128)(2,1)} %broadcast_in_dim.52), calls=%async_computation.4 | async-start | bytes 2097152 | tf_op jit(solution)/shard_map/all_to_all | solution.py:17
  132.0 5.7 %copy-start.3 = (bf16[1,1536,2048]{2,1,0:T(8,128)(2,1)S(1)}, bf16[1,1536,2048]{2,1,0:T(8,128)(2,1)}, u32[]{:S(2)}) copy-start(bf16[1,1536,2048]{2,1,0:T(8,128)(2,1)} %count_matrix.3) | copy-start | bytes 18874372
  136.8 0.9 copy-start.4
  137.7 2.8 %copy-start.10 = (bf16[256,256]{1,0:T(8,128)(2,1)S(1)}, bf16[256,256]{1,0:T(8,128)(2,1)}, u32[]{:S(2)}) copy-start(bf16[256,256]{1,0:T(8,128)(2,1)} %param.27) | copy-start | bytes 393220
  140.5 9.8 %slice-start = ((s8[4718592]{0:T(1024)(128)(4,1)}), s8[524288]{0:T(1024)(128)(4,1)S(1)}, s32[]{:S(2)}) async-start(s8[4718592]{0:T(1024)(128)(4,1)} %bitcast.102), calls=%async_computation.7 | async-start | bytes 1048576
  145.9 2.8 %copy-start.6 = (bf16[1536,256]{1,0:T(8,128)(2,1)S(1)}, bf16[1536,256]{1,0:T(8,128)(2,1)}, u32[]{:S(2)}) copy-start(bf16[1536,256]{1,0:T(8,128)(2,1)} %convolution_convert_fusion.3) | copy-start | bytes 2359300
  145.9 4.4 %slice-start.1 = ((s8[4718592]{0:T(1024)(128)(4,1)}), s8[4194304]{0:T(1024)(128)(4,1)S(1)}, s32[]{:S(2)}) async-start(s8[4718592]{0:T(1024)(128)(4,1)} %bitcast.102), calls=%async_computation.8 | async-start | bytes 8388608
  152.7 6.9 %copy-start.5 = (bf16[1536,256]{1,0:T(8,128)(2,1)S(1)}, bf16[1536,256]{1,0:T(8,128)(2,1)}, u32[]{:S(2)}) copy-start(bf16[1536,256]{1,0:T(8,128)(2,1)} %copy-done.4) | copy-start | bytes 2359300
  152.7 6.9 %copy-start.11 = (bf16[1536,256]{1,0:T(8,128)(2,1)S(1)}, bf16[1536,256]{1,0:T(8,128)(2,1)}, u32[]{:S(2)}) copy-start(bf16[1536,256]{1,0:T(8,128)(2,1)} %convolution_convert_fusion.2) | copy-start | bytes 2359300
  187.9 16.1 %all-to-all-start.6 = ((bf16[16,38,256]{2,1,0:T(8,128)(2,1)}), bf16[16,38,256]{2,1,0:T(8,128)(2,1)S(1)}, u32[]{:S(2)}, u32[]{:S(2)}) async-start(bf16[16,38,256]{2,1,0:T(8,128)(2,1)} %broadcast_in_dim.57), calls=%async_computation.6 | async-start | bytes 655360 | tf_op jit(solution)/shard_map/all_to_all | solution.py:17

commit v3 on v2

--- a/solution.py
+++ b/solution.py
@@ -10,7 +10,11 @@
 
 BF = jnp.bfloat16
 F32 = jnp.float32
-VMEM_LIMIT = 48 * 2**20
+F8 = jnp.float8_e4m3fn
+VMEM_LIMIT = 50 * 2**20
+NN = ((1,), (0,))
+NT = ((1,), (1,))
+TN = ((0,), (0,))
 
 
 def swap(value, axis):
@@ -83,29 +87,37 @@
         small = jnp.broadcast_to(row, (16, 256)).astype(BF)
         return jnp.concatenate([small] * (rows // 16), axis=0)
 
-    def block(at, _):
+    def block(pair, _):
         one = jnp.ones((256, 256), BF)
         zero = jnp.zeros((256, 256), BF)
-        low = stretch(lows_ref[pl.ds(at, 1), :], 256)
-        right = jnp.where(low == marks[...], one, zero)
-        place = pl.multiple_of(at * 16, 16)
+        place = pl.multiple_of(pair * 32, 32)
+        rights = []
+        for at in (pair * 2, pair * 2 + 1):
+            low = stretch(lows_ref[pl.ds(at, 1), :], 256)
+            rights.append(jnp.where(low == marks[...], one, zero))
         for first in range(0, spans, 16):
             size = min(16, spans - first)
-            key = stretch(keys_ref[pl.ds(at, 1), :] - float(first * 16), size * 16)
-            left = jnp.where(key == marks[0 : size * 16, :], one[: size * 16], zero[: size * 16])
-            part = dot(left, right, ((1,), (1,))).astype(BF)
+            parts = []
+            for side in range(2):
+                row = keys_ref[pl.ds(pair * 2 + side, 1), :]
+                key = stretch(row - float(first * 16), size * 16)
+                left = jnp.where(
+                    key == marks[0 : size * 16, :], one[: size * 16], zero[: size * 16]
+                )
+                parts.append(dot(left, rights[side], NT))
             for inner in range(size):
                 span = first + inner
                 lane = (span % across) * 256
-                out_ref[span // across, pl.ds(place, 16), lane : lane + 256] = part[
-                    inner * 16 : (inner + 1) * 16
-                ]
+                rows = [part[inner * 16 : (inner + 1) * 16] for part in parts]
+                out_ref[span // across, pl.ds(place, 32), lane : lane + 256] = jnp.concatenate(
+                    rows, axis=0
+                ).astype(out_ref.dtype)
         return 0
 
-    lax.fori_loop(0, 16, block, 0, unroll=8)
-
-
-def count_matrix(highs, lows, total, chunk):
+    lax.fori_loop(0, 8, block, 0, unroll=4)
+
+
+def count_matrix(highs, lows, total, chunk, kind):
     fan, nodes = highs.shape
 
     def order(value):
@@ -116,7 +128,7 @@
     return pl.pallas_call(
         count_kernel,
         grid=(nodes // 256,),
-        out_shape=jax.ShapeDtypeStruct((total // chunk, nodes, chunk), BF),
+        out_shape=jax.ShapeDtypeStruct((total // chunk, nodes, chunk), kind),
         in_specs=[
             pl.BlockSpec((16, 256), lambda at: (at, 0)),
             pl.BlockSpec((16, 256), lambda at: (at, 0)),
@@ -125,7 +137,7 @@
         scratch_shapes=[pltpu.VMEM((256, 256), BF)],
         compiler_params=pltpu.CompilerParams(vmem_limit_bytes=VMEM_LIMIT),
         cost_estimate=pl.CostEstimate(
-            flops=2 * nodes * total * 256 // 16 * 16,
+            flops=2 * nodes * total * 256,
             bytes_accessed=2 * nodes * total,
             transcendentals=0,
         ),
@@ -143,7 +155,7 @@
         at = pl.multiple_of((step * owners + owner) * cap, cap)
         table[pl.ds(at, cap), 0:width] = rows
         parts.append(rows.astype(BF))
-    part = dot(counts_ref[0], jnp.concatenate(parts, axis=0), ((1,), (0,)))
+    part = dot(counts_ref[0].astype(BF), jnp.concatenate(parts, axis=0), NN)
 
     @pl.when(step == 0)
     def _():
@@ -197,17 +209,80 @@
         compiler_params=pltpu.CompilerParams(vmem_limit_bytes=VMEM_LIMIT),
         cost_estimate=pl.CostEstimate(
             flops=2 * nodes * chunks * chunk * 128,
-            bytes_accessed=2 * nodes * chunks * chunk,
+            bytes_accessed=nodes * chunks * chunk,
             transcendentals=0,
         ),
         name="first_hop",
     )(self_ids, counts, frontier, inv)
 
 
-def one_hot(ids, total):
-    marks = lax.broadcasted_iota(jnp.int32, (ids.shape[0], total), 1)
-    return (ids[:, None] == marks).astype(BF)
-
+def mark_rows(ids_ref, out_ref, marks):
+    total, count = out_ref.shape
+    one = jnp.ones((256, count), BF); zero = jnp.zeros((256, count), BF)
+    for first in range(0, total, 256):
+        row = jnp.broadcast_to(ids_ref[...] - float(first), (16, count)).astype(BF)
+        row = jnp.concatenate([row] * 16, axis=0)
+        out_ref[first:first + 256, :] = jnp.where(row == marks, one, zero)
+
+def second_kernel(scale, negative_total, hidden_ref, rows_ref, self_ref, ends_ref, inv_ref, ws_ref, wn_ref, neigh_hbm,
+                  first_ref, second_ref, loss_ref, neigh, own, ends, hidden_t, sem):
+    copy = pltpu.make_async_copy(neigh_hbm, neigh, sem)
+    copy.start()
+    blocks, width, block = hidden_ref.shape
+    for at in range(blocks):
+        hidden_t[:, at * block:(at + 1) * block] = hidden_ref[at]
+    targets = own.shape[1]
+    marks = lax.broadcasted_iota(jnp.int32, (256, targets), 0).astype(F32).astype(BF)
+    mark_rows(self_ref, own, marks)
+    mark_rows(ends_ref, ends, marks)
+    inv = inv_ref[...]
+    hidden = hidden_t[...]
+    hs = dot(hidden, own[...], NN).astype(BF)
+    copy.wait()
+    hn = (dot(hidden, neigh[...], NT) * inv).astype(BF)
+    embed = (dot(ws_ref[...], hs, TN) + dot(wn_ref[...], hn, TN)).astype(BF)
+    rows = dot(embed, ends[...], NN).astype(BF)
+    count = rows.shape[1] // 3
+    source, dest, negative = rows[:, :count], rows[:, count:2 * count], rows[:, 2 * count:]
+    pos = jnp.sum(source.astype(F32) * dest.astype(F32), axis=0, keepdims=True) * scale
+    neg = dot(source, negative, TN) * scale
+    small = jnp.exp(-jnp.abs(neg))
+    neg_sig = jnp.where(neg >= 0, 1.0, small) / (1.0 + small)
+    neg_loss = jnp.maximum(neg, 0.0) + jnp.log1p(small)
+    small = jnp.exp(-jnp.abs(pos))
+    pos_grad = -(jnp.where(pos >= 0, small, 1.0) / (1.0 + small))
+    pos_loss = jnp.maximum(-pos, 0.0) + jnp.log1p(small)
+    loss = jnp.sum(neg_loss, axis=0, keepdims=True) * (1.0 / negative_total) + pos_loss
+    loss_ref[...] = jnp.broadcast_to(jnp.sum(loss, axis=1, keepdims=True), loss_ref.shape)
+    neg_grad = (neg_sig * (1.0 / negative_total)).astype(BF)
+    source_grad = (pos_grad * dest.astype(F32) + dot(negative, neg_grad, NT)) * scale
+    dest_grad = pos_grad * source.astype(F32) * scale
+    negative_grad = dot(source, neg_grad, NN) * scale
+    grads = jnp.concatenate([source_grad.astype(BF), dest_grad.astype(BF), negative_grad.astype(BF)], axis=1)
+    eg = dot(grads, ends[...], NT).astype(BF)
+    width2 = ws_ref.shape[0]
+    second_ref[0:width2, :] = dot(hs, eg, NT).astype(BF)
+    second_ref[width2:2 * width2, :] = dot(hn, eg, NT).astype(BF)
+    self_back = dot(ws_ref[...], eg, NN).astype(BF)
+    neigh_back = (dot(wn_ref[...], eg, NN) * inv).astype(BF)
+    hidden_grad = dot(self_back, own[...], NT) + dot(neigh_back, neigh[...], NN)
+    pre = jnp.where(hidden > 0, hidden_grad, 0.0).astype(BF)
+    rows_one = jnp.concatenate([rows_ref[at] for at in range(blocks)], axis=1)
+    first_ref[...] = dot(rows_one, pre, NT).astype(BF)
+
+def second(hidden, rows_one, pick_neigh, self_two, ends, inv, ws, wn, scale, negative_total):
+    blocks, width, block = hidden.shape
+    nodes = blocks * block
+    targets = self_two.shape[1]
+    many = ends.shape[1]
+    vm = pl.BlockSpec(memory_space=pltpu.VMEM)
+    return pl.pallas_call(functools.partial(second_kernel, scale, negative_total),
+        out_shape=[jax.ShapeDtypeStruct((rows_one.shape[1], width), BF), jax.ShapeDtypeStruct((2 * width, width), BF), jax.ShapeDtypeStruct((8, width), F32)],
+        in_specs=[vm] * 7 + [pl.BlockSpec(memory_space=pl.ANY)],
+        out_specs=[vm] * 3,
+        scratch_shapes=[pltpu.VMEM((targets, nodes), BF), pltpu.VMEM((nodes, targets), BF), pltpu.VMEM((targets, many), BF), pltpu.VMEM((width, nodes), BF), pltpu.SemaphoreType.DMA],
+        compiler_params=pltpu.CompilerParams(vmem_limit_bytes=VMEM_LIMIT),
+        name="second_layer")(hidden, rows_one, self_two, ends, inv, ws, wn, pick_neigh)
 
 def halves(ids):
     return (ids // 256).astype(F32), (ids % 256).astype(F32)
@@ -250,18 +325,18 @@
     fields = [*halves(self_two_ids), count_two.astype(F32), neigh_high, neigh_low]
     fields = [field.reshape(-1) for field in fields + list(halves(pos_pairs[0]))]
     field_sizes = [field.shape[0] for field in fields]
-    spare = -sum(field_sizes) % (16 * hidden_width)
+    spare = (128 - 2 * width) * hidden_width - sum(field_sizes)
     fields = jnp.concatenate(fields + [jnp.zeros((spare,), F32)]).astype(BF)
     early = jnp.concatenate(
         [first_self, first_neigh, fields.reshape(-1, hidden_width)], axis=0
     )
-    early = gather_all(early, "feat")
+    early = lax.all_gather(early, "feat")
 
     served = serve(features.T, asked.reshape(-1), graphs, cap)
     one_ids, served = lax.optimization_barrier((neigh_one_ids[0], served))
     one_high, one_low = halves(one_ids)
     one_low = jnp.where(slots < count_one, one_low, -1.0)
-    one_counts = count_matrix(one_high, one_low, front, 2 * cap)
+    one_counts = count_matrix(one_high, one_low, front, 2 * cap, F8)
     inv_one = (1.0 / count_one.astype(F32)).reshape(feats, -1)
     frontier = swap(served, "graph")
     frontier, early = lax.optimization_barrier((frontier, early))
@@ -276,66 +351,31 @@
     for size in field_sizes:
         got.append(sent[:, start : start + size])
         start += size
-    self_two = (got[0] * 256.0 + got[1]).astype(jnp.int32).reshape(-1)
-    counts_two = got[2].reshape(-1)
+    self_two = (got[0] * 256.0 + got[1]).reshape(1, -1)
+    inv_two = 1.0 / got[2].reshape(1, -1)
     neigh_high, neigh_low = (
         value.reshape(feats, fan, share).transpose(1, 0, 2).reshape(fan, -1) for value in got[3:5]
     )
-    pairs = (got[5] * 256.0 + got[6]).astype(jnp.int32).reshape(feats, 2, pair_share)
-    pairs = pairs.transpose(1, 0, 2).reshape(2, -1)
-    targets_total = self_two.shape[0]
-    pair_total = pairs.shape[1]
-    pick_neigh = count_matrix(neigh_high, neigh_low, nodes, nodes)[0]
-    pick_self = one_hot(self_two, nodes)
-    pick_ends = one_hot(jnp.concatenate([pairs[0], pairs[1], neg_ids[0]]), targets_total)
-    pick_self, pick_ends = lax.optimization_barrier(
-        (pick_self, pick_ends)
-    )
-
-    hidden_pre = dot(mine.reshape(feats * 2 * width, -1), weights, ((0,), (0,)))
+    pairs = (got[5] * 256.0 + got[6]).reshape(feats, 2, pair_share).transpose(1, 0, 2)
+    pair_total = feats * pair_share
+    ends = jnp.concatenate([pairs.reshape(1, -1), neg_ids.astype(F32)], axis=1)
+    pick_neigh = count_matrix(neigh_high, neigh_low, nodes, nodes, BF)[0]
+
+    hidden_pre = dot(weights, mine.reshape(feats * 2 * width, -1), TN)
     hidden = gather_all(jnp.maximum(hidden_pre, 0.0).astype(BF), "feat")
-    hidden = hidden.reshape(nodes, hidden_width)
-
-    inv_two = (1.0 / counts_two)[:, None]
-    hidden_self = dot(pick_self, hidden, ((1,), (0,))).astype(BF)
-    hidden_neigh = (dot(pick_neigh, hidden, ((1,), (0,))) * inv_two).astype(BF)
-    embed = (
-        dot(hidden_self, second_self, ((1,), (0,)))
-        + dot(hidden_neigh, second_neigh, ((1,), (0,)))
-    ).astype(BF)
-
-    end_rows = dot(pick_ends, embed, ((1,), (0,))).astype(BF)
-    source_rows = end_rows[:pair_total]
-    dest_rows = end_rows[pair_total : 2 * pair_total]
-    negative_rows = end_rows[2 * pair_total :]
-    pos_score = (
-        jnp.sum(source_rows.astype(F32) * dest_rows.astype(F32), axis=1, keepdims=True) * scale
-    )
-    neg_score = dot(source_rows, negative_rows, ((1,), (1,))) * scale
-    loss_part = (
-        jnp.sum(jax.nn.softplus(-pos_score)) + jnp.sum(jax.nn.softplus(neg_score)) / negative_total
-    )
-    pos_grad = -jax.nn.sigmoid(-pos_score)
-    neg_grad = (jax.nn.sigmoid(neg_score) / negative_total).astype(BF)
-    source_grad = (
-        pos_grad * dest_rows.astype(F32) + dot(neg_grad, negative_rows, ((1,), (0,)))
-    ) * scale
-    dest_grad = pos_grad * source_rows.astype(F32) * scale
-    negative_grad = dot(neg_grad, source_rows, ((0,), (0,))) * scale
-    end_grads = jnp.concatenate([source_grad, dest_grad, negative_grad]).astype(BF)
-    embed_grad = dot(pick_ends, end_grads, ((0,), (0,))).astype(BF)
-
-    grad_ss = dot(hidden_self, embed_grad, ((0,), (0,)))
-    grad_sn = dot(hidden_neigh, embed_grad, ((0,), (0,)))
-    self_back = dot(embed_grad, second_self, ((1,), (1,))).astype(BF)
-    neigh_back = (dot(embed_grad, second_neigh, ((1,), (1,))) * inv_two).astype(BF)
-    hidden_grad = dot(self_back, pick_self, ((0,), (0,))) + dot(
-        neigh_back, pick_neigh, ((0,), (0,))
-    )
-    pre_grad = jnp.where(hidden.T > 0, hidden_grad, 0.0).astype(BF)
-    first_part = dot(
-        rows_one.transpose(1, 0, 2).reshape(2 * width, nodes), pre_grad, ((1,), (1,))
-    )
+    first_part, second_part, loss_part = second(
+        hidden,
+        rows_one,
+        pick_neigh,
+        self_two,
+        ends,
+        inv_two,
+        second_self,
+        second_neigh,
+        scale,
+        negative_total,
+    )
+    loss_part = loss_part[0, 0]
 
     loss_high = loss_part.astype(BF)
     loss_mid = (loss_part - loss_high.astype(F32)).astype(BF)
@@ -344,9 +384,8 @@
     loss_row = jnp.where(lanes == 1, loss_mid, jnp.where(lanes == 2, loss_low, loss_high))
     parts = jnp.concatenate(
         [
-            first_part.astype(BF).reshape(graphs, -1, hidden_width),
-            grad_ss.astype(BF).reshape(graphs, -1, hidden_width),
-            grad_sn.astype(BF).reshape(graphs, -1, hidden_width),
+            first_part.reshape(graphs, -1, hidden_width),
+            second_part.reshape(graphs, -1, hidden_width),
             loss_row,
         ],
         axis=1,
@@ -354,16 +393,14 @@
     sums = jnp.sum(swap(parts, "graph").astype(F32), axis=0)
     loss = jnp.sum(sums[-1, 0:3])
     first_rows = 2 * width // graphs
-    second_rows = hidden_width // graphs
     whole = gather_all(sums[:-1].astype(BF), "graph").astype(F32)
     first_sums = whole[:, :first_rows].reshape(2 * width, hidden_width)
-    ss = whole[:, first_rows : first_rows + second_rows].reshape(hidden_width, hidden_width)
-    sn = whole[:, first_rows + second_rows :].reshape(hidden_width, hidden_width)
+    second_sums = whole[:, first_rows:].reshape(2 * hidden_width, hidden_width)
     return (
         first_sums[:width],
         first_sums[width:],
-        ss,
-        sn,
+        second_sums[:hidden_width],
+        second_sums[hidden_width:],
         loss / (pair_total * graphs),
     )
 

time: 208 us -> 198 us (0.952)
  matrix products: 36.4 us -> 1.54 us
  between operations: 4.18 us -> 17.4 us
  Pallas kernels: 57.9 us -> 69.2 us
  starting transfers between devices: 34.8 us -> 27.8 us
  waiting for transfers between devices: 34.6 us -> 40.1 us
    dot_general x14 -> x1, matrix products: 36.4 us -> 1.54 us  [dot(): lax.dot_general(former, latter, (dims, ((), ())), preferred_element_type=...]
    pallas_call x0 -> x1, Pallas kernels: none -> 15.9 us  [second(): pl.pallas_call(functools.partial(second_kernel, scale, negative_total), o...]
    all_to_all x6 -> x5, starting transfers between devices: 34.8 us -> 27.8 us  [swap(): return lax.all_to_all(value, axis, split_axis=0, concat_axis=0, tiled=True)]
    all_to_all x6 -> x5, waiting for transfers between devices: 34.6 us -> 40.1 us  [swap(): return lax.all_to_all(value, axis, split_axis=0, concat_axis=0, tiled=True)]
    convert_element_type x3 -> x1, other arithmetic: 6.69 us -> 1.26 us  [local(): ends = jnp.concatenate([pairs.reshape(1, -1), neg_ids.astype(F32)], axis=1)]
    pallas_call x1, Pallas kernels: 20.9 us -> 18.2 us  [hop(): pl.pallas_call(hop_kernel, grid=(chunks,), out_shape=jax.ShapeDtypeStruct...]
  transfers between devices with their start and end apart: 6 -> 6, of which waited for: 6 -> 5; matrix products, arithmetic and copies ran while one was open for 7% -> 5% of each run, Pallas kernels for 18% -> 18%
where the time goes in v3:
time: 198 us; the launch traced here: 196 us
  Pallas kernels  69.2 us (35%)
  waiting for transfers between devices  40.1 us (20%)
  starting transfers between devices  27.8 us (14%)
  between operations  17.4 us (9%)
  blocking collectives  15.9 us (8%)
  local copies, waits for them, and re-layouts  12.5 us (6%)
  other arithmetic  11.9 us (6%)
    all_to_all x5, waiting for transfers between devices, swap(): return lax.all_to_all(value, axis, split_axis=0, concat_axis=0, tiled=True)  40.1 us
    all_to_all x5, starting transfers between devices, swap(): return lax.all_to_all(value, axis, split_axis=0, concat_axis=0, tiled=True)  27.8 us
    pallas_call x2, Pallas kernels, count_matrix(): pl.pallas_call(count_kernel, grid=(nodes // 256,), out_shape=jax.ShapeDty...  20.5 us
    pallas_call x1, Pallas kernels, hop(): pl.pallas_call(hop_kernel, grid=(chunks,), out_shape=jax.ShapeDtypeStruct...  18.2 us
    pallas_call x1, Pallas kernels, second(): pl.pallas_call(functools.partial(second_kernel, scale, negative_total), o...  15.9 us
    all_to_all x1, blocking collectives, swap(): return lax.all_to_all(value, axis, split_axis=0, concat_axis=0, tiled=True)  15.9 us
    pallas_call x1, Pallas kernels, serve(): pl.pallas_call(serve_kernel, out_shape=jax.ShapeDtypeStruct((groups, widt...  14.6 us
  transfers between devices with their start and end apart: 6, of which 5 were waited for; matrix products, arithmetic and copies ran while one was open for 5% of the time, Pallas kernels for 18%

profile of v3, /device:TPU:1, one launch (start us, length us, event | category | flops | bytes accessed | tf_op | source)
XLA Modules:
  0.0 196.3 jit_solution(13129822534809170839)
XLA Ops:
  7.2 0.8 squeeze.22
  8.0 0.7 fusion.24
  8.7 0.7 iota_compare_fusion.1
  9.3 0.1 lt.79
  9.5 0.8 squeeze.23
  10.2 0.1 concatenate.13
  10.4 1.4 pad_maximum_fusion.1
  11.8 1.4 all_to_all.21
  13.2 10.0 %all-to-all-start = ((s32[16,1,512]{2,1,0:T(1,128)}), s32[16,1,512]{2,1,0:T(1,128)S(1)}, u32[]{:S(2)}, u32[]{:S(2)}) async-start(s32[16,1,512]{2,1,0:T(1,128)} %all_to_all.21), calls=%async_computation | async-start | bytes 65536 | tf_op jit(solution)/shard_map/all_to_all | solution.py:21
  23.2 0.6 compare_and_fusion
  23.8 1.3 convert_element_type.96
  25.0 0.7 convert_divide_fusion
  25.8 4.8 %all-to-all-done = s32[16,1,512]{2,1,0:T(1,128)S(1)} async-done(((s32[16,1,512]{2,1,0:T(1,128)}), s32[16,1,512]{2,1,0:T(1,128)S(1)}, u32[]{:S(2)}, u32[]{:S(2)}) %all-to-all-start) | async-done | bytes 32800 | tf_op jit(solution)/shard_map/all_to_all | solution.py:21
  30.5 1.1 copy-done
  31.7 14.6 %serve.1 = bf16[16,48,512]{2,1,0:T(8,128)(2,1)} custom-call(s32[8192]{0:T(1024)S(1)} %bitcast.44, bf16[48,8192]{1,0:T(8,128)(2,1)S(1)} %bitcast.42), custom_call_target="tpu_custom_call" | custom-call | tf_op jit(solution)/shard_map/serve/pallas_call | solution.py:63
  46.3 3.8 %all-to-all-start.1 = ((bf16[16,48,512]{2,1,0:T(8,128)(2,1)}), bf16[16,48,512]{2,1,0:T(8,128)(2,1)S(1)}, u32[]{:S(2)}, u32[]{:S(2)}) async-start(bf16[16,48,512]{2,1,0:T(8,128)(2,1)} %serve.1), calls=%async_computation.1 | async-start | bytes 1572864 | tf_op jit(solution)/shard_map/all_to_all | solution.py:21
  50.1 0.5 iota_compare_fusion.2
  50.6 0.6 add_and_fusion
  51.3 1.1 fusion.7
  52.3 0.4 reshape.175
  52.7 0.3 copy.42
  53.0 0.1 copy.44.keys_ref
  53.1 0.4 reshape.177
  53.5 0.3 copy.43
  53.8 0.1 copy.45.lows_ref
  53.9 13.6 %count_matrix.2.counts_ref = f8e4m3fn[8,2048,1024]{2,1,0:T(32,128)(4,1)} custom-call(f32[128,256]{1,0:T(8,128)S(1)} %copy.44.keys_ref, f32[128,256]{1,0:T(8,128)S(1)} %copy.45.lows_ref), custom_call_target="tpu_custom_call" | custom-call | flops 8589934592 | bytes 33554432 | tf_op jit(solution)/shard_map/count_matrix/pallas_call | solution.py:128
  67.5 5.2 %all-to-all-done.1.front_ref = bf16[16,48,512]{2,1,0:T(8,128)(2,1)S(1)} async-done(((bf16[16,48,512]{2,1,0:T(8,128)(2,1)}), bf16[16,48,512]{2,1,0:T(8,128)(2,1)S(1)}, u32[]{:S(2)}, u32[]{:S(2)}) %all-to-all-start.1) | async-done | bytes 786464 | tf_op jit(solution)/shard_map/all_to_all | solution.py:21
  72.7 18.2 %first_hop.1.rows_ref = bf16[16,96,128]{2,1,0:T(8,128)(2,1)} custom-call(s32[2048]{0:T(1024)S(1)} %bitcast.46, f8e4m3fn[8,2048,1024]{2,1,0:T(32,128)(4,1)} %count_matrix.2.counts_ref, bf16[16,48,512]{2,1,0:T(8,128)(2,1)S(1)} %all-to-all-done.1.front_ref, f32[16,128]{1,0:T(8,128)S(1)} %bitcast.45), custom_call_target="tpu_custom_call" | custom-call | flops 4294967296 | bytes 16777216 | tf_op jit(solution)/shard_map/first_hop/pallas_call | solution.py:193
  90.9 1.0 slice_convert_fusion
  91.9 0.3 copy.53
  92.2 6.9 %all-to-all-start.2 = ((bf16[16,96,128]{2,1,0:T(8,128)(2,1)}), bf16[16,96,128]{2,1,0:T(8,128)(2,1)S(1)}, u32[]{:S(2)}, u32[]{:S(2)}) async-start(bf16[16,96,128]{2,1,0:T(8,128)(2,1)} %first_hop.1.rows_ref), calls=%async_computation.2 | async-start | bytes 786432 | tf_op jit(solution)/shard_map/all_to_all | solution.py:21
  99.1 0.1 fusion.27
  99.2 0.1 mul.42
  99.4 0.2 mul.44
  99.6 8.7 %all-to-all-done.2 = bf16[16,96,128]{2,1,0:T(8,128)(2,1)S(1)} async-done(((bf16[16,96,128]{2,1,0:T(8,128)(2,1)}), bf16[16,96,128]{2,1,0:T(8,128)(2,1)S(1)}, u32[]{:S(2)}, u32[]{:S(2)}) %all-to-all-start.2) | async-done | bytes 393248 | tf_op jit(solution)/shard_map/all_to_all | solution.py:21
  108.3 1.5 fusion.1
  109.8 1.2 broadcast_in_dim.38
  111.0 3.7 %all-to-all-start.3 = ((bf16[16,256,128]{2,1,0:T(8,128)(2,1)}), bf16[16,256,128]{2,1,0:T(8,128)(2,1)S(1)}, u32[]{:S(2)}, u32[]{:S(2)}) async-start(bf16[16,256,128]{2,1,0:T(8,128)(2,1)} %broadcast_in_dim.38), calls=%async_computation.3 | async-start | bytes 2097152 | tf_op jit(solution)/shard_map/all_to_all | solution.py:21
  114.7 0.9 add_bitcast_fusion
  115.6 0.2 copy.48
  115.8 0.1 copy.51.keys_ref
  115.9 0.1 reshape.187
  116.1 0.2 reshape_reshape.3
  116.3 0.2 copy.50
  116.5 0.1 copy.52.lows_ref
  116.7 0.1 div.85.inv_ref
  116.8 0.1 reshape.183.self_ref
  117.0 0.1 reshape.184
  117.1 0.1 reshape.185
  117.1 6.9 %count_matrix.3 = bf16[1,1536,2048]{2,1,0:T(8,128)(2,1)} custom-call(f32[96,256]{1,0:T(8,128)S(1)} %copy.51.keys_ref, f32[96,256]{1,0:T(8,128)S(1)} %copy.52.lows_ref), custom_call_target="tpu_custom_call" | custom-call | flops 1610612736 | bytes 6291456 | tf_op jit(solution)/shard_map/count_matrix/pallas_call | solution.py:128
  124.0 0.7 pad_maximum_fusion.2.ends_ref
  124.7 10.0 %all-to-all-done.3.hidden_ref = bf16[16,256,128]{2,1,0:T(8,128)(2,1)S(1)} async-done(((bf16[16,256,128]{2,1,0:T(8,128)(2,1)}), bf16[16,256,128]{2,1,0:T(8,128)(2,1)S(1)}, u32[]{:S(2)}, u32[]{:S(2)}) %all-to-all-start.3) | async-done | bytes 1048608 | tf_op jit(solution)/shard_map/all_to_all | solution.py:21
  134.7 15.9 %second_layer.1 = (bf16[96,256]{1,0:T(8,128)(2,1)S(1)}, bf16[512,256]{1,0:T(8,128)(2,1)S(1)}, f32[8,256]{1,0:T(8,128)S(1)}) custom-call(bf16[16,256,128]{2,1,0:T(8,128)(2,1)S(1)} %all-to-all-done.3.hidden_ref, bf16[16,96,128]{2,1,0:T(8,128)(2,1)} %first_hop.1.rows_ref, f32[1,1536]{1,0:T(1,128)S(1)} %reshape.183.self_ref, ...), custom_call_target="tpu_custom_call" | custom-call | tf_op jit(solution)/shard_map/second_layer/pallas_call | solution.py:279
  150.7 0.5 slice.76
  152.5 0.7 broadcast_select_fusion
  153.2 0.2 pad_maximum_fusion
  153.3 15.9 %all_to_all.34 = bf16[16,39,256]{2,1,0:T(8,128)(2,1)S(1)} all-to-all(bf16[16,39,256]{2,1,0:T(8,128)(2,1)S(1)} %pad_maximum_fusion), channel_id=1, replica_groups=mesh['graph'=16,'feat'=16] {'graph'}, dimensions={0} | all-to-all | bytes 638976 | tf_op jit(solution)/shard_map/all_to_all | solution.py:21
  169.3 0.8 broadcast_in_dim.42
  170.0 3.4 %all-to-all-start.5 = ((bf16[16,38,256]{2,1,0:T(8,128)(2,1)}), bf16[16,38,256]{2,1,0:T(8,128)(2,1)S(1)}, u32[]{:S(2)}, u32[]{:S(2)}) async-start(bf16[16,38,256]{2,1,0:T(8,128)(2,1)} %broadcast_in_dim.42), calls=%async_computation.5 | async-start | bytes 655360 | tf_op jit(solution)/shard_map/all_to_all | solution.py:21
  173.5 0.6 slice_reduce_fusion
  174.7 11.4 %all-to-all-done.5 = bf16[16,38,256]{2,1,0:T(8,128)(2,1)S(1)} async-done(((bf16[16,38,256]{2,1,0:T(8,128)(2,1)}), bf16[16,38,256]{2,1,0:T(8,128)(2,1)S(1)}, u32[]{:S(2)}, u32[]{:S(2)}) %all-to-all-start.5) | async-done | bytes 311328 | tf_op jit(solution)/shard_map/all_to_all | solution.py:21
  186.2 0.6 slice.79
  186.8 0.6 slice.81
  187.4 0.9 fusion.28
  (27 shorter events, 0.5 us)
Async XLA Ops:
  7.2 65.5 %all-gather.3.cloned.1.call-start = ((), (), s32[]{:S(2)}) async-start(), calls=%async_computation.6 | async-start | bytes 1114112 | tf_op jit(solution)/shard_map/all_gather | solution.py:333
  13.2 17.4 %all-to-all-start = ((s32[16,1,512]{2,1,0:T(1,128)}), s32[16,1,512]{2,1,0:T(1,128)S(1)}, u32[]{:S(2)}, u32[]{:S(2)}) async-start(s32[16,1,512]{2,1,0:T(1,128)} %all_to_all.21), calls=%async_computation | async-start | bytes 65536 | tf_op jit(solution)/shard_map/all_to_all | solution.py:21
  30.5 1.1 copy-start
  46.3 26.4 %all-to-all-start.1 = ((bf16[16,48,512]{2,1,0:T(8,128)(2,1)}), bf16[16,48,512]{2,1,0:T(8,128)(2,1)S(1)}, u32[]{:S(2)}, u32[]{:S(2)}) async-start(bf16[16,48,512]{2,1,0:T(8,128)(2,1)} %serve.1), calls=%async_computation.1 | async-start | bytes 1572864 | tf_op jit(solution)/shard_map/all_to_all | solution.py:21
  53.5 19.2 %copy-start.3 = (s32[1,2048]{1,0:T(1,128)S(1)}, s32[1,2048]{1,0:T(1,128)}, u32[]{:S(2)}) copy-start(s32[1,2048]{1,0:T(1,128)} %param.16) | copy-start | bytes 24580
  72.7 62.0 %copy-start.1 = (bf16[256,256]{1,0:T(8,128)(2,1)S(1)}, bf16[256,256]{1,0:T(8,128)(2,1)}, u32[]{:S(2)}) copy-start(bf16[256,256]{1,0:T(8,128)(2,1)} %ws_ref.1) | copy-start | bytes 393220
  72.7 62.0 %copy-start.2 = (bf16[256,256]{1,0:T(8,128)(2,1)S(1)}, bf16[256,256]{1,0:T(8,128)(2,1)}, u32[]{:S(2)}) copy-start(bf16[256,256]{1,0:T(8,128)(2,1)} %wn_ref.1) | copy-start | bytes 393220
  92.2 16.1 %all-to-all-start.2 = ((bf16[16,96,128]{2,1,0:T(8,128)(2,1)}), bf16[16,96,128]{2,1,0:T(8,128)(2,1)S(1)}, u32[]{:S(2)}, u32[]{:S(2)}) async-start(bf16[16,96,128]{2,1,0:T(8,128)(2,1)} %first_hop.1.rows_ref), calls=%async_computation.2 | async-start | bytes 786432 | tf_op jit(solution)/shard_map/all_to_all | solution.py:21
  111.0 23.7 %all-to-all-start.3 = ((bf16[16,256,128]{2,1,0:T(8,128)(2,1)}), bf16[16,256,128]{2,1,0:T(8,128)(2,1)S(1)}, u32[]{:S(2)}, u32[]{:S(2)}) async-start(bf16[16,256,128]{2,1,0:T(8,128)(2,1)} %broadcast_in_dim.38), calls=%async_computation.3 | async-start | bytes 2097152 | tf_op jit(solution)/shard_map/all_to_all | solution.py:21
  170.0 16.1 %all-to-all-start.5 = ((bf16[16,38,256]{2,1,0:T(8,128)(2,1)}), bf16[16,38,256]{2,1,0:T(8,128)(2,1)S(1)}, u32[]{:S(2)}, u32[]{:S(2)}) async-start(bf16[16,38,256]{2,1,0:T(8,128)(2,1)} %broadcast_in_dim.42), calls=%async_computation.5 | async-start | bytes 655360 | tf_op jit(solution)/shard_map/all_to_all | solution.py:21
Sparse Core Ops, SparseCore 0:
  11.9 50.3 all-gather.2

commit v4 on v3

--- a/solution.py
+++ b/solution.py
@@ -42,20 +42,26 @@
 
     lax.fori_loop(0, rows // step, fill, 0)
 
-    def per_group(group, _):
-        base = group * cap
-
-        def pick(at, _):
-            for lane in range(32):
-                row = at * 32 + lane
-                picked[pl.ds(row, 1), :] = table[pl.ds(ids_ref[base + row], 1), :]
-            return 0
-
-        lax.fori_loop(0, cap // 32, pick, 0)
-        out_ref[group] = picked[:, 0:width].T.astype(out_ref.dtype)
+    def take(group, side):
+        for row in range(cap):
+            picked[side, row : row + 1, :] = table[pl.ds(ids_ref[group * cap + row], 1), :]
+
+    def put(group, side):
+        out_ref[group] = picked[side, :, 0:width].T.astype(out_ref.dtype)
+
+    def two(at, _):
+        group = at * 2 + 1
+        take(group, 1)
+        put(group - 1, 0)
+        take(group + 1, 0)
+        put(group, 1)
         return 0
 
-    lax.fori_loop(0, groups, per_group, 0)
+    take(0, 0)
+    lax.fori_loop(0, groups // 2 - 1, two, 0)
+    take(groups - 1, 1)
+    put(groups - 2, 0)
+    put(groups - 1, 1)
 
 
 def serve(features_t, ids, groups, cap):
@@ -68,7 +74,7 @@
             pl.BlockSpec(memory_space=pltpu.VMEM),
         ],
         out_specs=pl.BlockSpec(memory_space=pltpu.VMEM),
-        scratch_shapes=[pltpu.VMEM((rows, 128), F32), pltpu.VMEM((cap, 128), F32)],
+        scratch_shapes=[pltpu.VMEM((rows, 128), F32), pltpu.VMEM((2, cap, 128), F32)],
         compiler_params=pltpu.CompilerParams(vmem_limit_bytes=VMEM_LIMIT),
         name="serve",
     )(ids, features_t)
@@ -145,66 +151,87 @@
     )(keys, order(lows))
 
 
-def hop_kernel(self_ref, counts_ref, front_ref, inv_ref, out_ref, table, total, own):
+def hop_kernel(
+    steps, self_ref, counts_ref, front_ref, inv_ref, out_ref, table, total, own, up, down
+):
     owners, width, cap = front_ref.shape
     blocks, _, block = out_ref.shape
     step = pl.program_id(0)
-    parts = []
-    for owner in range(owners):
-        rows = front_ref[owner].astype(F32).T
-        at = pl.multiple_of((step * owners + owner) * cap, cap)
-        table[pl.ds(at, cap), 0:width] = rows
-        parts.append(rows.astype(BF))
-    part = dot(counts_ref[0].astype(BF), jnp.concatenate(parts, axis=0), NN)
+    per = owners // steps
+    half = steps // 2
 
     @pl.when(step == 0)
     def _():
-        total[...] = part
-
-    @pl.when(step > 0)
+        most = jnp.abs(front_ref[0])
+        for owner in range(1, owners):
+            most = jnp.maximum(most, jnp.abs(front_ref[owner]))
+        most = jnp.max(most.astype(F32), axis=1, keepdims=True)
+        power = jnp.ones_like(most)
+        back = jnp.ones_like(most)
+        for exponent in (32, 32, 16, 16, 8, 4, 2, 1):
+            fits = most * power * 2.0**exponent <= 224.0
+            power = jnp.where(fits, power * 2.0**exponent, power)
+            back = jnp.where(fits, back * 2.0**-exponent, back)
+        up[...] = jnp.broadcast_to(power, up.shape)
+        down[...] = jnp.broadcast_to(back, down.shape)
+        total[...] = jnp.zeros_like(total)
+
+    def product():
+        front = jnp.concatenate([front_ref[step * per + at] for at in range(per)], axis=1)
+        front = front.astype(F32) * up[:, 0:1]
+        high = front.astype(F8)
+        low = ((front - high.astype(F32)) * 16.0).astype(F8)
+        part = dot(jnp.concatenate([high, low], axis=0), counts_ref[0], NT)
+        total[...] += part[:width] + part[width:] * (1.0 / 16.0)
+
+    @pl.when(step < half)
     def _():
-        total[...] += part
-
-    @pl.when(step == pl.num_programs(0) - 1)
+        for at in range(owners // half):
+            owner = step * (owners // half) + at
+            place = pl.multiple_of(owner * cap, cap)
+            table[pl.ds(place, cap), 0:width] = front_ref[owner].astype(F32).T
+        product()
+
+    @pl.when(step >= half)
     def _():
-        def per_block(dest, _):
-            base = pl.multiple_of(dest * block, block)
-
-            def pick(at, _):
-                for lane in range(32):
-                    row = at * 32 + lane
-                    own[pl.ds(row, 1), :] = table[pl.ds(self_ref[base + row], 1), :]
-                return 0
-
-            lax.fori_loop(0, block // 32, pick, 0)
-            out_ref[dest, 0:width, :] = own[:, 0:width].T.astype(BF)
-            mean = total[pl.ds(base, block), :].T * inv_ref[pl.ds(dest, 1), :]
-            out_ref[dest, width : 2 * width, :] = mean.astype(BF)
-            return 0
-
-        lax.fori_loop(0, blocks, per_block, 0)
+        for at in range(blocks // half):
+            dest = (step - half) * (blocks // half) + at
+            for row in range(block):
+                place = at * block + row
+                own[place : place + 1, :] = table[pl.ds(self_ref[dest * block + row], 1), :]
+            rows = own[at * block : (at + 1) * block, 0:width]
+            out_ref[dest, 0:width, :] = rows.T.astype(BF)
+        product()
+
+    @pl.when(step == steps - 1)
+    def _():
+        back = down[:, 0:1]
+        for dest in range(blocks):
+            mean = total[:, dest * block : (dest + 1) * block] * back
+            out_ref[dest, width : 2 * width, :] = (mean * inv_ref[dest : dest + 1, :]).astype(BF)
 
 
 def hop(frontier, counts, self_ids, inv, blocks):
     owners, width, cap = frontier.shape
     chunks, nodes, chunk = counts.shape
     block = nodes // blocks
-    per = chunk // cap
     return pl.pallas_call(
-        hop_kernel,
+        functools.partial(hop_kernel, chunks),
         grid=(chunks,),
         out_shape=jax.ShapeDtypeStruct((blocks, 2 * width, block), BF),
         in_specs=[
             pl.BlockSpec(memory_space=pltpu.SMEM),
             pl.BlockSpec((1, nodes, chunk), lambda at: (at, 0, 0)),
-            pl.BlockSpec((per, width, cap), lambda at: (at, 0, 0)),
+            pl.BlockSpec((owners, width, cap), lambda at: (0, 0, 0)),
             pl.BlockSpec(inv.shape, lambda at: (0, 0)),
         ],
         out_specs=pl.BlockSpec((blocks, 2 * width, block), lambda at: (0, 0, 0)),
         scratch_shapes=[
             pltpu.VMEM((owners * cap, 128), F32),
-            pltpu.VMEM((nodes, width), F32),
-            pltpu.VMEM((block, 128), F32),
+            pltpu.VMEM((width, nodes), F32),
+            pltpu.VMEM((nodes * 2 // chunks, 128), F32),
+            pltpu.VMEM((width, 128), F32),
+            pltpu.VMEM((width, 128), F32),
         ],
         compiler_params=pltpu.CompilerParams(vmem_limit_bytes=VMEM_LIMIT),
         cost_estimate=pl.CostEstimate(
@@ -216,6 +243,25 @@
     )(self_ids, counts, frontier, inv)
 
 
+def first_kernel(mine_ref, early_ref, out_ref):
+    feats, depth, block = mine_ref.shape
+    weights = early_ref[:, 0:depth, :].reshape(feats * depth, early_ref.shape[2])
+    pre = dot(weights, mine_ref[...].reshape(feats * depth, block), TN)
+    hidden = jnp.maximum(pre, 0.0).astype(BF)
+    for at in range(out_ref.shape[0]):
+        out_ref[at] = hidden
+
+
+def first(mine, early):
+    feats, _, block = mine.shape
+    return pl.pallas_call(
+        first_kernel,
+        out_shape=jax.ShapeDtypeStruct((feats, early.shape[2], block), BF),
+        compiler_params=pltpu.CompilerParams(vmem_limit_bytes=VMEM_LIMIT),
+        name="first_layer",
+    )(mine, early)
+
+
 def mark_rows(ids_ref, out_ref, marks):
     total, count = out_ref.shape
     one = jnp.ones((256, count), BF); zero = jnp.zeros((256, count), BF)
@@ -225,7 +271,7 @@
         out_ref[first:first + 256, :] = jnp.where(row == marks, one, zero)
 
 def second_kernel(scale, negative_total, hidden_ref, rows_ref, self_ref, ends_ref, inv_ref, ws_ref, wn_ref, neigh_hbm,
-                  first_ref, second_ref, loss_ref, neigh, own, ends, hidden_t, sem):
+                  out_ref, neigh, own, ends, hidden_t, sem):
     copy = pltpu.make_async_copy(neigh_hbm, neigh, sem)
     copy.start()
     blocks, width, block = hidden_ref.shape
@@ -253,33 +299,47 @@
     pos_grad = -(jnp.where(pos >= 0, small, 1.0) / (1.0 + small))
     pos_loss = jnp.maximum(-pos, 0.0) + jnp.log1p(small)
     loss = jnp.sum(neg_loss, axis=0, keepdims=True) * (1.0 / negative_total) + pos_loss
-    loss_ref[...] = jnp.broadcast_to(jnp.sum(loss, axis=1, keepdims=True), loss_ref.shape)
+    loss = jnp.sum(loss, axis=1, keepdims=True)
     neg_grad = (neg_sig * (1.0 / negative_total)).astype(BF)
     source_grad = (pos_grad * dest.astype(F32) + dot(negative, neg_grad, NT)) * scale
     dest_grad = pos_grad * source.astype(F32) * scale
     negative_grad = dot(source, neg_grad, NN) * scale
     grads = jnp.concatenate([source_grad.astype(BF), dest_grad.astype(BF), negative_grad.astype(BF)], axis=1)
     eg = dot(grads, ends[...], NT).astype(BF)
-    width2 = ws_ref.shape[0]
-    second_ref[0:width2, :] = dot(hs, eg, NT).astype(BF)
-    second_ref[width2:2 * width2, :] = dot(hn, eg, NT).astype(BF)
+    groups = out_ref.shape[0]
+    many = 2 * ws_ref.shape[0] // groups
+    sums = jnp.concatenate([dot(hs, eg, NT), dot(hn, eg, NT)], axis=0).astype(BF)
+    for group in range(groups):
+        out_ref[group, 0:many, :] = sums[group * many : (group + 1) * many]
     self_back = dot(ws_ref[...], eg, NN).astype(BF)
     neigh_back = (dot(wn_ref[...], eg, NN) * inv).astype(BF)
     hidden_grad = dot(self_back, own[...], NT) + dot(neigh_back, neigh[...], NN)
     pre = jnp.where(hidden > 0, hidden_grad, 0.0).astype(BF)
     rows_one = jnp.concatenate([rows_ref[at] for at in range(blocks)], axis=1)
-    first_ref[...] = dot(rows_one, pre, NT).astype(BF)
-
-def second(hidden, rows_one, pick_neigh, self_two, ends, inv, ws, wn, scale, negative_total):
+    part = dot(rows_one, pre, NT)
+    few = part.shape[0] // groups
+    high = loss.astype(BF).astype(F32)
+    mid = (loss - high).astype(BF).astype(F32)
+    low = loss - high - mid
+    lanes = lax.broadcasted_iota(jnp.int32, (8 - few, part.shape[1]), 1)
+    tail = jnp.where(lanes == 0, high, jnp.where(lanes == 1, mid, low))
+    for group in range(groups):
+        rows = jnp.concatenate([part[group * few : (group + 1) * few], tail], axis=0)
+        out_ref[group, many : many + 8, :] = rows.astype(BF)
+
+
+def second(
+    hidden, rows_one, pick_neigh, self_two, ends, inv, ws, wn, scale, negative_total, groups
+):
     blocks, width, block = hidden.shape
     nodes = blocks * block
     targets = self_two.shape[1]
     many = ends.shape[1]
     vm = pl.BlockSpec(memory_space=pltpu.VMEM)
     return pl.pallas_call(functools.partial(second_kernel, scale, negative_total),
-        out_shape=[jax.ShapeDtypeStruct((rows_one.shape[1], width), BF), jax.ShapeDtypeStruct((2 * width, width), BF), jax.ShapeDtypeStruct((8, width), F32)],
+        out_shape=jax.ShapeDtypeStruct((groups, 2 * width // groups + 8, width), BF),
         in_specs=[vm] * 7 + [pl.BlockSpec(memory_space=pl.ANY)],
-        out_specs=[vm] * 3,
+        out_specs=vm,
         scratch_shapes=[pltpu.VMEM((targets, nodes), BF), pltpu.VMEM((nodes, targets), BF), pltpu.VMEM((targets, many), BF), pltpu.VMEM((width, nodes), BF), pltpu.SemaphoreType.DMA],
         compiler_params=pltpu.CompilerParams(vmem_limit_bytes=VMEM_LIMIT),
         name="second_layer")(hidden, rows_one, self_two, ends, inv, ws, wn, pick_neigh)
@@ -325,12 +385,12 @@
     fields = [*halves(self_two_ids), count_two.astype(F32), neigh_high, neigh_low]
     fields = [field.reshape(-1) for field in fields + list(halves(pos_pairs[0]))]
     field_sizes = [field.shape[0] for field in fields]
-    spare = (128 - 2 * width) * hidden_width - sum(field_sizes)
+    spare = -sum(field_sizes) % (16 * hidden_width)
     fields = jnp.concatenate(fields + [jnp.zeros((spare,), F32)]).astype(BF)
     early = jnp.concatenate(
         [first_self, first_neigh, fields.reshape(-1, hidden_width)], axis=0
     )
-    early = lax.all_gather(early, "feat")
+    early = gather_all(early, "feat")
 
     served = serve(features.T, asked.reshape(-1), graphs, cap)
     one_ids, served = lax.optimization_barrier((neigh_one_ids[0], served))
@@ -341,10 +401,10 @@
     frontier = swap(served, "graph")
     frontier, early = lax.optimization_barrier((frontier, early))
     rows_one = hop(frontier, one_counts, self_one_ids[0], inv_one, feats)
-    rows_one, early = lax.optimization_barrier((rows_one, early))
-    mine = swap(rows_one, "feat")
-
-    weights = early[:, : 2 * width].reshape(feats * 2 * width, hidden_width)
+    hidden = first(swap(rows_one, "feat"), early)
+    hidden, early = lax.optimization_barrier((hidden, early))
+    hidden = swap(hidden, "feat")
+
     sent = early[:, 2 * width :].reshape(feats, -1).astype(F32)
     got = []
     start = 0
@@ -361,9 +421,7 @@
     ends = jnp.concatenate([pairs.reshape(1, -1), neg_ids.astype(F32)], axis=1)
     pick_neigh = count_matrix(neigh_high, neigh_low, nodes, nodes, BF)[0]
 
-    hidden_pre = dot(weights, mine.reshape(feats * 2 * width, -1), TN)
-    hidden = gather_all(jnp.maximum(hidden_pre, 0.0).astype(BF), "feat")
-    first_part, second_part, loss_part = second(
+    parts = second(
         hidden,
         rows_one,
         pick_neigh,
@@ -374,28 +432,16 @@
         second_neigh,
         scale,
         negative_total,
-    )
-    loss_part = loss_part[0, 0]
-
-    loss_high = loss_part.astype(BF)
-    loss_mid = (loss_part - loss_high.astype(F32)).astype(BF)
-    loss_low = (loss_part - loss_high.astype(F32) - loss_mid.astype(F32)).astype(BF)
-    lanes = lax.broadcasted_iota(jnp.int32, (graphs, 1, hidden_width), 2)
-    loss_row = jnp.where(lanes == 1, loss_mid, jnp.where(lanes == 2, loss_low, loss_high))
-    parts = jnp.concatenate(
-        [
-            first_part.reshape(graphs, -1, hidden_width),
-            second_part.reshape(graphs, -1, hidden_width),
-            loss_row,
-        ],
-        axis=1,
-    )
+        graphs,
+    )
+
     sums = jnp.sum(swap(parts, "graph").astype(F32), axis=0)
     loss = jnp.sum(sums[-1, 0:3])
+    whole = gather_all(sums.astype(BF), "graph").astype(F32)
+    second_rows = 2 * hidden_width // graphs
     first_rows = 2 * width // graphs
-    whole = gather_all(sums[:-1].astype(BF), "graph").astype(F32)
-    first_sums = whole[:, :first_rows].reshape(2 * width, hidden_width)
-    second_sums = whole[:, first_rows:].reshape(2 * hidden_width, hidden_width)
+    second_sums = whole[:, :second_rows].reshape(2 * hidden_width, hidden_width)
+    first_sums = whole[:, second_rows : second_rows + first_rows].reshape(-1, hidden_width)
     return (
         first_sums[:width],
         first_sums[width:],

time: 198 us -> 174 us (0.88)
  between operations: 17.4 us -> 2.68 us
  Pallas kernels: 69.2 us -> 61.4 us
  other arithmetic: 11.9 us -> 5 us
  starting transfers between devices: 27.8 us -> 33.1 us
  waiting for transfers between devices: 40.1 us -> 43.7 us
    all_to_all x5 -> x6, starting transfers between devices: 27.8 us -> 33.1 us  [swap(): return lax.all_to_all(value, axis, split_axis=0, concat_axis=0, tiled=True)]
    pallas_call x1 -> x2, Pallas kernels: 18.2 us -> 13.9 us  [the longest x1 12.4 us: hop(): pl.pallas_call(functools.partial(hop_kernel, chunks), grid=(chunks,), out...]
    all_to_all x5 -> x6, waiting for transfers between devices: 40.1 us -> 43.7 us  [swap(): return lax.all_to_all(value, axis, split_axis=0, concat_axis=0, tiled=True)]
    pallas_call x1, Pallas kernels: 14.6 us -> 11.1 us  [serve(): pl.pallas_call(serve_kernel, out_shape=jax.ShapeDtypeStruct((groups, widt...]
  transfers between devices with their start and end apart: 6 -> 6, of which waited for: 5 -> 6; matrix products, arithmetic and copies ran while one was open for 5% -> 5% of each run, Pallas kernels for 18% -> 18%
where the time goes in v4:
time: 174 us; the launch traced here: 173 us
  Pallas kernels  61.4 us (35%)
  waiting for transfers between devices  43.7 us (25%)
  starting transfers between devices  33.1 us (19%)
  blocking collectives  15.9 us (9%)
  local copies, waits for them, and re-layouts  11.6 us (7%)
  other arithmetic  5 us (3%)
  between operations  2.68 us (2%)
    all_to_all x6, waiting for transfers between devices, swap(): return lax.all_to_all(value, axis, split_axis=0, concat_axis=0, tiled=True)  43.7 us
    all_to_all x6, starting transfers between devices, swap(): return lax.all_to_all(value, axis, split_axis=0, concat_axis=0, tiled=True)  33.1 us
    pallas_call x2, Pallas kernels, count_matrix(): pl.pallas_call(count_kernel, grid=(nodes // 256,), out_shape=jax.ShapeDty...  20.6 us
    pallas_call x1, Pallas kernels, second(): pl.pallas_call(functools.partial(second_kernel, scale, negative_total), o...  15.9 us
    all_to_all x1, blocking collectives, swap(): return lax.all_to_all(value, axis, split_axis=0, concat_axis=0, tiled=True)  15.9 us
    pallas_call x1, Pallas kernels, hop(): pl.pallas_call(functools.partial(hop_kernel, chunks), grid=(chunks,), out...  12.4 us
    pallas_call x1, Pallas kernels, serve(): pl.pallas_call(serve_kernel, out_shape=jax.ShapeDtypeStruct((groups, widt...  11.1 us
  transfers between devices with their start and end apart: 6, of which 6 were waited for; matrix products, arithmetic and copies ran while one was open for 5% of the time, Pallas kernels for 18%

profile of v4, /device:TPU:1, one launch (start us, length us, event | category | flops | bytes accessed | tf_op | source)
XLA Modules:
  0.0 173.3 jit_solution(350333861378278299)
XLA Ops:
  0.6 1.4 all_to_all.24
  2.0 10.0 %all-to-all-start = ((s32[16,1,512]{2,1,0:T(1,128)}), s32[16,1,512]{2,1,0:T(1,128)S(1)}, u32[]{:S(2)}, u32[]{:S(2)}) async-start(s32[16,1,512]{2,1,0:T(1,128)} %all_to_all.24), calls=%async_computation | async-start | bytes 65536 | tf_op jit(solution)/shard_map/all_to_all | solution.py:21
  12.0 0.8 squeeze.19
  12.8 0.7 fusion.21
  13.5 0.7 iota_compare_fusion.1
  14.1 0.1 lt.79
  14.2 0.8 squeeze.20
  15.0 0.1 concatenate.10
  15.1 0.8 pad_maximum_fusion
  15.9 3.5 %all-to-all-done = s32[16,1,512]{2,1,0:T(1,128)S(1)} async-done(((s32[16,1,512]{2,1,0:T(1,128)}), s32[16,1,512]{2,1,0:T(1,128)S(1)}, u32[]{:S(2)}, u32[]{:S(2)}) %all-to-all-start) | async-done | bytes 32800 | tf_op jit(solution)/shard_map/all_to_all | solution.py:21
  19.4 1.0 broadcast_in_dim.26
  20.4 6.8 %all-to-all-start.2 = ((bf16[16,112,256]{2,1,0:T(8,128)(2,1)}), bf16[16,112,256]{2,1,0:T(8,128)(2,1)S(1)}, u32[]{:S(2)}, u32[]{:S(2)}) async-start(bf16[16,112,256]{2,1,0:T(8,128)(2,1)} %broadcast_in_dim.26), calls=%async_computation.2 | async-start | bytes 1835008 | tf_op jit(solution)/shard_map/all_to_all | solution.py:21
  27.2 0.7 convert_divide_fusion
  27.9 0.0 copy-start
  27.9 1.1 copy-done
  29.0 11.1 %serve.1 = bf16[16,48,512]{2,1,0:T(8,128)(2,1)} custom-call(s32[8192]{0:T(1024)S(1)} %bitcast.33, bf16[48,8192]{1,0:T(8,128)(2,1)S(1)} %bitcast.32), custom_call_target="tpu_custom_call" | custom-call | tf_op jit(solution)/shard_map/serve/pallas_call | solution.py:69
  40.1 2.0 %all-to-all-done.2.early_ref = bf16[16,112,256]{2,1,0:T(8,128)(2,1)S(1)} async-done(((bf16[16,112,256]{2,1,0:T(8,128)(2,1)}), bf16[16,112,256]{2,1,0:T(8,128)(2,1)S(1)}, u32[]{:S(2)}, u32[]{:S(2)}) %all-to-all-start.2) | async-done | bytes 917536 | tf_op jit(solution)/shard_map/all_to_all | solution.py:21
  42.1 5.4 %all-to-all-start.1 = ((bf16[16,48,512]{2,1,0:T(8,128)(2,1)}), bf16[16,48,512]{2,1,0:T(8,128)(2,1)S(1)}, u32[]{:S(2)}, u32[]{:S(2)}) async-start(bf16[16,48,512]{2,1,0:T(8,128)(2,1)} %serve.1), calls=%async_computation.1 | async-start | bytes 1572864 | tf_op jit(solution)/shard_map/all_to_all | solution.py:21
  47.5 1.1 fusion.4
  48.5 0.4 reshape.133
  48.9 0.3 copy.42
  49.2 0.1 copy.44.keys_ref
  49.3 0.4 reshape.135
  49.7 0.0 copy-start.3
  49.7 0.3 copy.43
  50.0 0.1 copy.45.lows_ref
  50.1 13.6 %count_matrix.2.counts_ref = f8e4m3fn[8,2048,1024]{2,1,0:T(32,128)(4,1)} custom-call(f32[128,256]{1,0:T(8,128)S(1)} %copy.44.keys_ref, f32[128,256]{1,0:T(8,128)S(1)} %copy.45.lows_ref), custom_call_target="tpu_custom_call" | custom-call | flops 8589934592 | bytes 33554432 | tf_op jit(solution)/shard_map/count_matrix/pallas_call | solution.py:134
  63.7 6.4 %all-to-all-done.1.front_ref = bf16[16,48,512]{2,1,0:T(8,128)(2,1)S(1)} async-done(((bf16[16,48,512]{2,1,0:T(8,128)(2,1)}), bf16[16,48,512]{2,1,0:T(8,128)(2,1)S(1)}, u32[]{:S(2)}, u32[]{:S(2)}) %all-to-all-start.1) | async-done | bytes 786464 | tf_op jit(solution)/shard_map/all_to_all | solution.py:21
  70.2 0.0 copy-done.3
  70.2 12.4 %first_hop.1.rows_ref = bf16[16,96,128]{2,1,0:T(8,128)(2,1)} custom-call(s32[2048]{0:T(1024)S(1)} %bitcast.35, f8e4m3fn[8,2048,1024]{2,1,0:T(32,128)(4,1)} %count_matrix.2.counts_ref, bf16[16,48,512]{2,1,0:T(8,128)(2,1)S(1)} %all-to-all-done.1.front_ref, f32[16,128]{1,0:T(8,128)S(1)} %bitcast.34), custom_call_target="tpu_custom_call" | custom-call | flops 4294967296 | bytes 16777216 | tf_op jit(solution)/shard_map/first_hop/pallas_call | solution.py:218
  82.6 3.7 %all-to-all-start.3 = ((bf16[16,96,128]{2,1,0:T(8,128)(2,1)}), bf16[16,96,128]{2,1,0:T(8,128)(2,1)S(1)}, u32[]{:S(2)}, u32[]{:S(2)}) async-start(bf16[16,96,128]{2,1,0:T(8,128)(2,1)} %first_hop.1.rows_ref), calls=%async_computation.3 | async-start | bytes 786432 | tf_op jit(solution)/shard_map/all_to_all | solution.py:21
  86.3 9.1 %all-to-all-done.3.mine_ref = bf16[16,96,128]{2,1,0:T(8,128)(2,1)S(1)} async-done(((bf16[16,96,128]{2,1,0:T(8,128)(2,1)}), bf16[16,96,128]{2,1,0:T(8,128)(2,1)S(1)}, u32[]{:S(2)}, u32[]{:S(2)}) %all-to-all-start.3) | async-done | bytes 393248 | tf_op jit(solution)/shard_map/all_to_all | solution.py:21
  95.5 1.4 first_layer.1
  96.9 0.2 copy.53
  97.1 0.1 fusion.26
  97.2 0.1 mul.42
  97.4 0.2 mul.44
  97.6 3.8 %all-to-all-start.4 = ((bf16[16,256,128]{2,1,0:T(8,128)(2,1)}), bf16[16,256,128]{2,1,0:T(8,128)(2,1)S(1)}, u32[]{:S(2)}, u32[]{:S(2)}) async-start(bf16[16,256,128]{2,1,0:T(8,128)(2,1)} %first_layer.1), calls=%async_computation.4 | async-start | bytes 2097152 | tf_op jit(solution)/shard_map/all_to_all | solution.py:21
  101.5 0.1 add_bitcast_fusion
  101.5 0.2 copy.48
  101.8 0.1 copy.51.keys_ref
  101.9 0.1 reshape.145
  102.0 0.2 reshape_reshape.3
  102.3 0.2 copy.50
  102.5 0.1 copy.52.lows_ref
  102.6 0.1 slice_divide_fusion
  102.7 0.1 div.85.inv_ref
  102.8 0.1 reshape.141.self_ref
  102.9 0.1 slice_add_fusion
  102.9 0.1 reshape.142
  103.0 0.1 reshape.143
  103.1 6.9 %count_matrix.3 = bf16[1,1536,2048]{2,1,0:T(8,128)(2,1)} custom-call(f32[96,256]{1,0:T(8,128)S(1)} %copy.51.keys_ref, f32[96,256]{1,0:T(8,128)S(1)} %copy.52.lows_ref), custom_call_target="tpu_custom_call" | custom-call | flops 1610612736 | bytes 6291456 | tf_op jit(solution)/shard_map/count_matrix/pallas_call | solution.py:134
  110.1 11.3 %all-to-all-done.4.hidden_ref = bf16[16,256,128]{2,1,0:T(8,128)(2,1)S(1)} async-done(((bf16[16,256,128]{2,1,0:T(8,128)(2,1)}), bf16[16,256,128]{2,1,0:T(8,128)(2,1)S(1)}, u32[]{:S(2)}, u32[]{:S(2)}) %all-to-all-start.4) | async-done | bytes 1048608 | tf_op jit(solution)/shard_map/all_to_all | solution.py:21
  121.3 0.0 copy-done.2
  121.3 15.9 %second_layer.1 = bf16[16,40,256]{2,1,0:T(8,128)(2,1)S(1)} custom-call(bf16[16,256,128]{2,1,0:T(8,128)(2,1)S(1)} %all-to-all-done.4.hidden_ref, bf16[16,96,128]{2,1,0:T(8,128)(2,1)} %first_hop.1.rows_ref, f32[1,1536]{1,0:T(1,128)S(1)} %reshape.141.self_ref, f32[1,1536]{1,0:T(1,128)S(1)} %pad_maximum_fusion.1.ends_ref, f32[1,1536]{1,0:T(1,128)S(1)} %div.85.inv_ref, ...), custom_call_target="tpu_custom_call" | custom-call | tf_op jit(solution)/shard_map/second_layer/pallas_call | solution.py:339
  137.2 15.9 %all_to_all.39 = bf16[16,40,256]{2,1,0:T(8,128)(2,1)S(1)} all-to-all(bf16[16,40,256]{2,1,0:T(8,128)(2,1)S(1)} %second_layer.1), channel_id=1, replica_groups=mesh['graph'=16,'feat'=16] {'graph'}, dimensions={0} | all-to-all | bytes 655360 | tf_op jit(solution)/shard_map/all_to_all | solution.py:21
  153.1 0.1 convert_reduce_fusion
  153.2 0.8 broadcast_in_dim.27
  153.9 3.4 %all-to-all-start.6 = ((bf16[16,40,256]{2,1,0:T(8,128)(2,1)}), bf16[16,40,256]{2,1,0:T(8,128)(2,1)S(1)}, u32[]{:S(2)}, u32[]{:S(2)}) async-start(bf16[16,40,256]{2,1,0:T(8,128)(2,1)} %broadcast_in_dim.27), calls=%async_computation.6 | async-start | bytes 655360 | tf_op jit(solution)/shard_map/all_to_all | solution.py:21
  157.4 0.6 slice_reduce_fusion
  158.6 11.4 %all-to-all-done.6 = bf16[16,40,256]{2,1,0:T(8,128)(2,1)S(1)} async-done(((bf16[16,40,256]{2,1,0:T(8,128)(2,1)}), bf16[16,40,256]{2,1,0:T(8,128)(2,1)S(1)}, u32[]{:S(2)}, u32[]{:S(2)}) %all-to-all-start.6) | async-done | bytes 327712 | tf_op jit(solution)/shard_map/all_to_all | solution.py:21
  170.1 0.6 slice.66
  170.7 0.6 slice.68
  171.3 0.8 fusion.24
  (22 shorter events, 0.3 us)
Async XLA Ops:
  2.0 17.4 %all-to-all-start = ((s32[16,1,512]{2,1,0:T(1,128)}), s32[16,1,512]{2,1,0:T(1,128)S(1)}, u32[]{:S(2)}, u32[]{:S(2)}) async-start(s32[16,1,512]{2,1,0:T(1,128)} %all_to_all.24), calls=%async_computation | async-start | bytes 65536 | tf_op jit(solution)/shard_map/all_to_all | solution.py:21
  20.4 21.7 %all-to-all-start.2 = ((bf16[16,112,256]{2,1,0:T(8,128)(2,1)}), bf16[16,112,256]{2,1,0:T(8,128)(2,1)S(1)}, u32[]{:S(2)}, u32[]{:S(2)}) async-start(bf16[16,112,256]{2,1,0:T(8,128)(2,1)} %broadcast_in_dim.26), calls=%async_computation.2 | async-start | bytes 1835008 | tf_op jit(solution)/shard_map/all_to_all | solution.py:21
  27.9 1.1 copy-start
  42.1 28.1 %all-to-all-start.1 = ((bf16[16,48,512]{2,1,0:T(8,128)(2,1)}), bf16[16,48,512]{2,1,0:T(8,128)(2,1)S(1)}, u32[]{:S(2)}, u32[]{:S(2)}) async-start(bf16[16,48,512]{2,1,0:T(8,128)(2,1)} %serve.1), calls=%async_computation.1 | async-start | bytes 1572864 | tf_op jit(solution)/shard_map/all_to_all | solution.py:21
  49.7 20.5 %copy-start.3 = (s32[1,2048]{1,0:T(1,128)S(1)}, s32[1,2048]{1,0:T(1,128)}, u32[]{:S(2)}) copy-start(s32[1,2048]{1,0:T(1,128)} %param.16) | copy-start | bytes 24580
  63.7 22.6 %copy-start.4 = (s32[1,512]{1,0:T(1,128)S(1)}, s32[1,512]{1,0:T(1,128)}, u32[]{:S(2)}) copy-start(s32[1,512]{1,0:T(1,128)} %param.23) | copy-start | bytes 6148
  70.2 51.2 %copy-start.1 = (bf16[256,256]{1,0:T(8,128)(2,1)S(1)}, bf16[256,256]{1,0:T(8,128)(2,1)}, u32[]{:S(2)}) copy-start(bf16[256,256]{1,0:T(8,128)(2,1)} %ws_ref.1) | copy-start | bytes 393220
  70.2 51.2 %copy-start.2 = (bf16[256,256]{1,0:T(8,128)(2,1)S(1)}, bf16[256,256]{1,0:T(8,128)(2,1)}, u32[]{:S(2)}) copy-start(bf16[256,256]{1,0:T(8,128)(2,1)} %wn_ref.1) | copy-start | bytes 393220
  82.6 12.9 %all-to-all-start.3 = ((bf16[16,96,128]{2,1,0:T(8,128)(2,1)}), bf16[16,96,128]{2,1,0:T(8,128)(2,1)S(1)}, u32[]{:S(2)}, u32[]{:S(2)}) async-start(bf16[16,96,128]{2,1,0:T(8,128)(2,1)} %first_hop.1.rows_ref), calls=%async_computation.3 | async-start | bytes 786432 | tf_op jit(solution)/shard_map/all_to_all | solution.py:21
  97.6 23.7 %all-to-all-start.4 = ((bf16[16,256,128]{2,1,0:T(8,128)(2,1)}), bf16[16,256,128]{2,1,0:T(8,128)(2,1)S(1)}, u32[]{:S(2)}, u32[]{:S(2)}) async-start(bf16[16,256,128]{2,1,0:T(8,128)(2,1)} %first_layer.1), calls=%async_computation.4 | async-start | bytes 2097152 | tf_op jit(solution)/shard_map/all_to_all | solution.py:21
  153.9 16.1 %all-to-all-start.6 = ((bf16[16,40,256]{2,1,0:T(8,128)(2,1)}), bf16[16,40,256]{2,1,0:T(8,128)(2,1)S(1)}, u32[]{:S(2)}, u32[]{:S(2)}) async-start(bf16[16,40,256]{2,1,0:T(8,128)(2,1)} %broadcast_in_dim.27), calls=%async_computation.6 | async-start | bytes 655360 | tf_op jit(solution)/shard_map/all_to_all | solution.py:21

commit v5 on v4

--- a/solution.py
+++ b/solution.py
@@ -43,8 +43,11 @@
     lax.fori_loop(0, rows // step, fill, 0)
 
     def take(group, side):
-        for row in range(cap):
-            picked[side, row : row + 1, :] = table[pl.ds(ids_ref[group * cap + row], 1), :]
+        for row in range(0, cap, 8):
+            rows = [
+                table[pl.ds(ids_ref[group * cap + row + at], 1), :] for at in range(8)
+            ]
+            picked[side, row : row + 8, :] = jnp.concatenate(rows, axis=0)
 
     def put(group, side):
         out_ref[group] = picked[side, :, 0:width].T.astype(out_ref.dtype)
@@ -80,14 +83,51 @@
     )(ids, features_t)
 
 
-def count_kernel(keys_ref, lows_ref, out_ref, marks):
+def pack_kernel(
+    across, self_ref, neigh_ref, count_ref, pairs_ref, ws_ref, wn_ref, feat_ref, out_ref, copy_ref, rows
+):
+    copy_ref[...] = feat_ref[...]
+    width = ws_ref.shape[0]
+    fan, share = neigh_ref.shape
+    pairs = pairs_ref.shape[1]
+
+    def place(ids):
+        return (ids & 127) * across + (ids >> 7)
+
+    rows[...] = jnp.zeros_like(rows)
+    neigh = place(neigh_ref[...])
+    live = lax.broadcasted_iota(jnp.int32, (fan, share), 0) < count_ref[...]
+    rows[0:fan, 0:share] = jnp.where(live, neigh & 255, -1).astype(F32)
+    rows[0:fan, 128 : 128 + share] = (neigh >> 8).astype(F32)
+    own = place(self_ref[...])
+    rows[fan : fan + 1, 0:share] = (own & 255).astype(F32)
+    rows[fan : fan + 1, 128 : 128 + share] = (own >> 8).astype(F32)
+    rows[fan + 1 : fan + 2, 0:share] = count_ref[...].astype(F32)
+    rows[fan + 2 : fan + 4, 0:pairs] = (pairs_ref[...] & 255).astype(F32)
+    rows[fan + 2 : fan + 4, 128 : 128 + pairs] = (pairs_ref[...] >> 8).astype(F32)
+    out_ref[0:width, :] = ws_ref[...]
+    out_ref[width : 2 * width, :] = wn_ref[...]
+    out_ref[2 * width :, :] = rows[...].astype(BF)
+
+
+def pack(self_two, neigh_two, count_two, pairs, ws, wn, features_t, across):
+    width, wide = ws.shape
+    return pl.pallas_call(
+        functools.partial(pack_kernel, across),
+        out_shape=[
+            jax.ShapeDtypeStruct((2 * width + 32, wide), BF),
+            jax.ShapeDtypeStruct(features_t.shape, BF),
+        ],
+        scratch_shapes=[pltpu.VMEM((32, wide), F32)],
+        compiler_params=pltpu.CompilerParams(vmem_limit_bytes=16 * 2**20),
+        name="pack",
+    )(self_two, neigh_two, count_two, pairs, ws, wn, features_t)
+
+
+def count_blocks(keys_ref, lows_ref, base, out_ref, marks):
     chunks, _, chunk = out_ref.shape
     spans = chunks * chunk // 256
     across = chunk // 256
-
-    @pl.when(pl.program_id(0) == 0)
-    def _():
-        marks[...] = lax.broadcasted_iota(jnp.int32, (256, 256), 0).astype(F32).astype(BF)
 
     def stretch(row, rows):
         small = jnp.broadcast_to(row, (16, 256)).astype(BF)
@@ -99,13 +139,13 @@
         place = pl.multiple_of(pair * 32, 32)
         rights = []
         for at in (pair * 2, pair * 2 + 1):
-            low = stretch(lows_ref[pl.ds(at, 1), :], 256)
+            low = stretch(lows_ref[pl.ds(base + at, 1), :], 256)
             rights.append(jnp.where(low == marks[...], one, zero))
         for first in range(0, spans, 16):
             size = min(16, spans - first)
             parts = []
             for side in range(2):
-                row = keys_ref[pl.ds(pair * 2 + side, 1), :]
+                row = keys_ref[pl.ds(base + pair * 2 + side, 1), :]
                 key = stretch(row - float(first * 16), size * 16)
                 left = jnp.where(
                     key == marks[0 : size * 16, :], one[: size * 16], zero[: size * 16]
@@ -123,42 +163,91 @@
     lax.fori_loop(0, 8, block, 0, unroll=4)
 
 
-def count_matrix(highs, lows, total, chunk, kind):
-    fan, nodes = highs.shape
-
-    def order(value):
-        return value.reshape(fan, nodes // 16, 16).transpose(1, 0, 2).reshape(nodes // 16, -1)
-
-    node = (lax.broadcasted_iota(jnp.int32, (fan, nodes), 1) % 16).astype(F32)
-    keys = order(highs * 16.0 + node)
+def all_marks():
+    return lax.broadcasted_iota(jnp.int32, (256, 256), 0).astype(F32).astype(BF)
+
+
+def count_one_kernel(ids_ref, live_ref, out_ref, marks, keys, lows):
+    fan = ids_ref.shape[0]
+
+    @pl.when(pl.program_id(0) == 0)
+    def _():
+        marks[...] = all_marks()
+        slots = lax.broadcasted_iota(jnp.int32, (fan, 128), 0)
+        high = []
+        low = []
+        for node in range(16):
+            ids = ids_ref[:, node * 128 : (node + 1) * 128]
+            live = slots < live_ref[:, node * 128 : (node + 1) * 128]
+            high.append(((ids >> 8) * 16 + node).astype(F32))
+            low.append(jnp.where(live, ids & 255, -1).astype(F32))
+        keys[...] = jnp.concatenate(high, axis=0).T
+        lows[...] = jnp.concatenate(low, axis=0).T
+
+    count_blocks(keys, lows, pl.program_id(0) * 16, out_ref, marks)
+
+
+def count_one_matrix(ids, live, total, chunk):
+    fan, nodes = ids.shape
     return pl.pallas_call(
-        count_kernel,
+        count_one_kernel,
         grid=(nodes // 256,),
-        out_shape=jax.ShapeDtypeStruct((total // chunk, nodes, chunk), kind),
+        out_shape=jax.ShapeDtypeStruct((total // chunk, nodes, chunk), F8),
+        in_specs=[
+            pl.BlockSpec((fan, nodes), lambda at: (0, 0)),
+            pl.BlockSpec((1, nodes), lambda at: (0, 0)),
+        ],
+        out_specs=pl.BlockSpec((total // chunk, 256, chunk), lambda at: (0, at, 0)),
+        scratch_shapes=[
+            pltpu.VMEM((256, 256), BF),
+            pltpu.VMEM((128, 256), F32),
+            pltpu.VMEM((128, 256), F32),
+        ],
+        compiler_params=pltpu.CompilerParams(vmem_limit_bytes=VMEM_LIMIT),
+        cost_estimate=pl.CostEstimate(
+            flops=2 * nodes * total * 256, bytes_accessed=nodes * total, transcendentals=0
+        ),
+        name="count_one",
+    )(ids, live)
+
+
+def count_two_kernel(keys_ref, lows_ref, out_ref, marks):
+    @pl.when(pl.program_id(0) == 0)
+    def _():
+        marks[...] = all_marks()
+
+    count_blocks(keys_ref, lows_ref, 0, out_ref, marks)
+
+
+def count_two_matrix(keys, lows, total):
+    nodes = keys.shape[0] * 16
+    return pl.pallas_call(
+        count_two_kernel,
+        grid=(nodes // 256,),
+        out_shape=jax.ShapeDtypeStruct((1, nodes, total), BF),
         in_specs=[
             pl.BlockSpec((16, 256), lambda at: (at, 0)),
             pl.BlockSpec((16, 256), lambda at: (at, 0)),
         ],
-        out_specs=pl.BlockSpec((total // chunk, 256, chunk), lambda at: (0, at, 0)),
+        out_specs=pl.BlockSpec((1, 256, total), lambda at: (0, at, 0)),
         scratch_shapes=[pltpu.VMEM((256, 256), BF)],
         compiler_params=pltpu.CompilerParams(vmem_limit_bytes=VMEM_LIMIT),
         cost_estimate=pl.CostEstimate(
-            flops=2 * nodes * total * 256,
-            bytes_accessed=2 * nodes * total,
-            transcendentals=0,
+            flops=2 * nodes * total * 256, bytes_accessed=2 * nodes * total, transcendentals=0
         ),
-        name="count_matrix",
-    )(keys, order(lows))
+        name="count_two",
+    )(keys, lows)
 
 
 def hop_kernel(
-    steps, self_ref, counts_ref, front_ref, inv_ref, out_ref, table, total, own, up, down
+    steps, self_ref, counts_ref, front_ref, out_ref, table, total, own, up, down, live
 ):
     owners, width, cap = front_ref.shape
     blocks, _, block = out_ref.shape
     step = pl.program_id(0)
     per = owners // steps
     half = steps // 2
+    across = blocks * block // 128
 
     @pl.when(step == 0)
     def _():
@@ -175,14 +264,17 @@
         up[...] = jnp.broadcast_to(power, up.shape)
         down[...] = jnp.broadcast_to(back, down.shape)
         total[...] = jnp.zeros_like(total)
+        live[...] = jnp.zeros_like(live)
 
     def product():
         front = jnp.concatenate([front_ref[step * per + at] for at in range(per)], axis=1)
         front = front.astype(F32) * up[:, 0:1]
         high = front.astype(F8)
         low = ((front - high.astype(F32)) * 16.0).astype(F8)
-        part = dot(jnp.concatenate([high, low], axis=0), counts_ref[0], NT)
-        total[...] += part[:width] + part[width:] * (1.0 / 16.0)
+        ones = jnp.ones((32, front.shape[1]), F8)
+        part = dot(jnp.concatenate([high, low, ones], axis=0), counts_ref[0], NT)
+        total[...] += part[:width] + part[width : 2 * width] * (1.0 / 16.0)
+        live[...] += part[2 * width : 2 * width + 8]
 
     @pl.when(step < half)
     def _():
@@ -198,7 +290,8 @@
             dest = (step - half) * (blocks // half) + at
             for row in range(block):
                 place = at * block + row
-                own[place : place + 1, :] = table[pl.ds(self_ref[dest * block + row], 1), :]
+                node = row % across * 128 + dest * (block // across) + row // across
+                own[place : place + 1, :] = table[pl.ds(self_ref[node], 1), :]
             rows = own[at * block : (at + 1) * block, 0:width]
             out_ref[dest, 0:width, :] = rows.T.astype(BF)
         product()
@@ -206,12 +299,14 @@
     @pl.when(step == steps - 1)
     def _():
         back = down[:, 0:1]
+        inv = 1.0 / live[0:1, :]
         for dest in range(blocks):
             mean = total[:, dest * block : (dest + 1) * block] * back
-            out_ref[dest, width : 2 * width, :] = (mean * inv_ref[dest : dest + 1, :]).astype(BF)
-
-
-def hop(frontier, counts, self_ids, inv, blocks):
+            mean = mean * inv[:, dest * block : (dest + 1) * block]
+            out_ref[dest, width : 2 * width, :] = mean.astype(BF)
+
+
+def hop(frontier, counts, self_ids, blocks):
     owners, width, cap = frontier.shape
     chunks, nodes, chunk = counts.shape
     block = nodes // blocks
@@ -223,7 +318,6 @@
             pl.BlockSpec(memory_space=pltpu.SMEM),
             pl.BlockSpec((1, nodes, chunk), lambda at: (at, 0, 0)),
             pl.BlockSpec((owners, width, cap), lambda at: (0, 0, 0)),
-            pl.BlockSpec(inv.shape, lambda at: (0, 0)),
         ],
         out_specs=pl.BlockSpec((blocks, 2 * width, block), lambda at: (0, 0, 0)),
         scratch_shapes=[
@@ -232,6 +326,7 @@
             pltpu.VMEM((nodes * 2 // chunks, 128), F32),
             pltpu.VMEM((width, 128), F32),
             pltpu.VMEM((width, 128), F32),
+            pltpu.VMEM((8, nodes), F32),
         ],
         compiler_params=pltpu.CompilerParams(vmem_limit_bytes=VMEM_LIMIT),
         cost_estimate=pl.CostEstimate(
@@ -240,26 +335,42 @@
             transcendentals=0,
         ),
         name="first_hop",
-    )(self_ids, counts, frontier, inv)
-
-
-def first_kernel(mine_ref, early_ref, out_ref):
-    feats, depth, block = mine_ref.shape
-    weights = early_ref[:, 0:depth, :].reshape(feats * depth, early_ref.shape[2])
-    pre = dot(weights, mine_ref[...].reshape(feats * depth, block), TN)
+    )(self_ids, counts, frontier)
+
+
+def first_kernel(side, me_ref, mine_ref, *refs):
+    early_refs, (out_ref, fields_ref) = refs[:side], refs[side:]
+    _, depth, block = mine_ref.shape
+    row, column = me_ref[0], me_ref[1]
+    weights = []
+    mine = []
+    for far in range(side):
+        for near in range(side):
+            owner = lax.rem(row + side - far, side) * side + lax.rem(column + side - near, side)
+            weights.append(early_refs[far][near, 0:depth, :])
+            mine.append(mine_ref[owner])
+            fields_ref[owner] = early_refs[far][near, depth:, :].astype(F32)
+    pre = dot(jnp.concatenate(weights, axis=0), jnp.concatenate(mine, axis=0), TN)
     hidden = jnp.maximum(pre, 0.0).astype(BF)
     for at in range(out_ref.shape[0]):
         out_ref[at] = hidden
 
 
-def first(mine, early):
-    feats, _, block = mine.shape
+def first(mine, early, me):
+    feats, depth, block = mine.shape
+    side, rows, wide = early[0].shape
+    vm = pl.BlockSpec(memory_space=pltpu.VMEM)
     return pl.pallas_call(
-        first_kernel,
-        out_shape=jax.ShapeDtypeStruct((feats, early.shape[2], block), BF),
+        functools.partial(first_kernel, side),
+        out_shape=[
+            jax.ShapeDtypeStruct((feats, wide, block), BF),
+            jax.ShapeDtypeStruct((feats, rows - depth, wide), F32),
+        ],
+        in_specs=[pl.BlockSpec(memory_space=pltpu.SMEM)] + [vm] * (1 + side),
+        out_specs=[vm, vm],
         compiler_params=pltpu.CompilerParams(vmem_limit_bytes=VMEM_LIMIT),
         name="first_layer",
-    )(mine, early)
+    )(me, mine, *early)
 
 
 def mark_rows(ids_ref, out_ref, marks):
@@ -344,10 +455,6 @@
         compiler_params=pltpu.CompilerParams(vmem_limit_bytes=VMEM_LIMIT),
         name="second_layer")(hidden, rows_one, self_two, ends, inv, ws, wn, pick_neigh)
 
-def halves(ids):
-    return (ids // 256).astype(F32), (ids % 256).astype(F32)
-
-
 def local(
     features,
     frontier_ids,
@@ -379,48 +486,53 @@
 
     asked = swap(frontier_ids[0], "graph")
 
-    slots = lax.broadcasted_iota(jnp.int32, (fan, 1), 0)
-    neigh_high, neigh_low = halves(neigh_two_ids[0])
-    neigh_low = jnp.where(slots < count_two, neigh_low, -1.0)
-    fields = [*halves(self_two_ids), count_two.astype(F32), neigh_high, neigh_low]
-    fields = [field.reshape(-1) for field in fields + list(halves(pos_pairs[0]))]
-    field_sizes = [field.shape[0] for field in fields]
-    spare = -sum(field_sizes) % (16 * hidden_width)
-    fields = jnp.concatenate(fields + [jnp.zeros((spare,), F32)]).astype(BF)
-    early = jnp.concatenate(
-        [first_self, first_neigh, fields.reshape(-1, hidden_width)], axis=0
+    early, features_t = pack(
+        self_two_ids,
+        neigh_two_ids[0],
+        count_two,
+        pos_pairs[0],
+        first_self,
+        first_neigh,
+        features.T,
+        nodes // 128,
     )
-    early = gather_all(early, "feat")
-
-    served = serve(features.T, asked.reshape(-1), graphs, cap)
-    one_ids, served = lax.optimization_barrier((neigh_one_ids[0], served))
-    one_high, one_low = halves(one_ids)
-    one_low = jnp.where(slots < count_one, one_low, -1.0)
-    one_counts = count_matrix(one_high, one_low, front, 2 * cap, F8)
-    inv_one = (1.0 / count_one.astype(F32)).reshape(feats, -1)
+    side = math.isqrt(feats)
+    me = lax.axis_index("feat")
+    me = jnp.stack([me // side, me % side]).astype(jnp.int32)
+    along = [
+        [(at, at // side * side + (at + far) % side) for at in range(feats)]
+        for far in range(1, side)
+    ]
+    across = [
+        [(at, (at + far * side) % feats) for at in range(feats)] for far in range(1, side)
+    ]
+    asked, early = lax.optimization_barrier((asked, early))
+    early = jnp.stack([early] + [lax.ppermute(early, "feat", pairs) for pairs in along])
+    served = serve(features_t, asked.reshape(-1), graphs, cap)
+    one_ids, served, early = lax.optimization_barrier((neigh_one_ids[0], served, early))
+    early = [early] + [lax.ppermute(early, "feat", pairs) for pairs in across]
+    one_counts = count_one_matrix(one_ids, count_one, front, 2 * cap)
     frontier = swap(served, "graph")
     frontier, early = lax.optimization_barrier((frontier, early))
-    rows_one = hop(frontier, one_counts, self_one_ids[0], inv_one, feats)
-    hidden = first(swap(rows_one, "feat"), early)
-    hidden, early = lax.optimization_barrier((hidden, early))
+    rows_one = hop(frontier, one_counts, self_one_ids[0], feats)
+    hidden, sent = first(swap(rows_one, "feat"), early, me)
     hidden = swap(hidden, "feat")
 
-    sent = early[:, 2 * width :].reshape(feats, -1).astype(F32)
-    got = []
-    start = 0
-    for size in field_sizes:
-        got.append(sent[:, start : start + size])
-        start += size
-    self_two = (got[0] * 256.0 + got[1]).reshape(1, -1)
-    inv_two = 1.0 / got[2].reshape(1, -1)
-    neigh_high, neigh_low = (
-        value.reshape(feats, fan, share).transpose(1, 0, 2).reshape(fan, -1) for value in got[3:5]
-    )
-    pairs = (got[5] * 256.0 + got[6]).reshape(feats, 2, pair_share).transpose(1, 0, 2)
+    def blocks(value):
+        value = value.reshape(feats, fan, share // 16, 16).transpose(0, 2, 1, 3)
+        return value.reshape(-1, fan * 16)
+
+    node = (lax.broadcasted_iota(jnp.int32, (feats, fan, share), 2) % 16).astype(F32)
+    keys = blocks(sent[:, :fan, 128 : 128 + share] * 16.0 + node)
+    pick_neigh = count_two_matrix(keys, blocks(sent[:, :fan, :share]), nodes)[0]
+    self_two = sent[:, fan, :share] + sent[:, fan, 128 : 128 + share] * 256.0
+    self_two = self_two.reshape(1, -1)
+    inv_two = 1.0 / sent[:, fan + 1, :share].reshape(1, -1)
+    pairs = sent[:, fan + 2 : fan + 4]
+    pairs = pairs[:, :, :pair_share] + pairs[:, :, 128 : 128 + pair_share] * 256.0
+    pairs = pairs.transpose(1, 0, 2)
     pair_total = feats * pair_share
     ends = jnp.concatenate([pairs.reshape(1, -1), neg_ids.astype(F32)], axis=1)
-    pick_neigh = count_matrix(neigh_high, neigh_low, nodes, nodes, BF)[0]
-
     parts = second(
         hidden,
         rows_one,

time: 174 us -> 169 us (0.971)
  waiting for transfers between devices: 43.7 us -> 32.3 us
  local copies, waits for them, and re-layouts: 11.6 us -> 16.8 us
  starting transfers between devices: 33.1 us -> 37.9 us
  other arithmetic: 5 us -> 0.88 us
    all_to_all x6 -> x5, waiting for transfers between devices: 43.7 us -> 32.3 us  [swap(): return lax.all_to_all(value, axis, split_axis=0, concat_axis=0, tiled=True)]
    ppermute x0 -> x6, starting transfers between devices: none -> 9.19 us  [the longest x3 4.98 us: local(): early = [early] + [lax.ppermute(early, 'feat', pairs) for pairs in across]]
    unnamed x11 -> x28, local copies, waits for them, and re-layouts: 1.3 us -> 6.91 us
    all_to_all x6 -> x5, starting transfers between devices: 33.1 us -> 28.7 us  [swap(): return lax.all_to_all(value, axis, split_axis=0, concat_axis=0, tiled=True)]
    reshape x10 -> x4, local copies, waits for them, and re-layouts: 1.38 us -> 3.34 us  [the longest x2 2.87 us: blocks(): return value.reshape(-1, fan * 16)]
    pallas_call x3 -> x4, Pallas kernels: 22 us -> 22.7 us  [the longest x1 13.7 us: count_one_matrix(): pl.pallas_call(count_one_kernel, grid=(nodes // 256,), out_shape=jax.Shap...]
  transfers between devices with their start and end apart: 6 -> 11, of which waited for: 6 -> 5; matrix products, arithmetic and copies ran while one was open for 5% -> 4% of each run, Pallas kernels for 18% -> 18%
where the time goes in v5:
time: 169 us; the launch traced here: 167 us
  Pallas kernels  61 us (36%)
  starting transfers between devices  37.9 us (22%)
  waiting for transfers between devices  32.3 us (19%)
  local copies, waits for them, and re-layouts  16.8 us (10%)
  blocking collectives  15.9 us (9%)
  between operations  2.61 us (2%)
    all_to_all x5, waiting for transfers between devices, swap(): return lax.all_to_all(value, axis, split_axis=0, concat_axis=0, tiled=True)  32.3 us
    all_to_all x5, starting transfers between devices, swap(): return lax.all_to_all(value, axis, split_axis=0, concat_axis=0, tiled=True)  28.7 us
    pallas_call x1, Pallas kernels, second(): pl.pallas_call(functools.partial(second_kernel, scale, negative_total), o...  15.9 us
    all_to_all x1, blocking collectives, swap(): return lax.all_to_all(value, axis, split_axis=0, concat_axis=0, tiled=True)  15.9 us
    pallas_call x1, Pallas kernels, count_one_matrix(): pl.pallas_call(count_one_kernel, grid=(nodes // 256,), out_shape=jax.Shap...  13.7 us
    pallas_call x1, Pallas kernels, hop(): pl.pallas_call(functools.partial(hop_kernel, chunks), grid=(chunks,), out...  12.5 us
    pallas_call x1, Pallas kernels, serve(): pl.pallas_call(serve_kernel, out_shape=jax.ShapeDtypeStruct((groups, widt...  9.95 us
    pallas_call x1, Pallas kernels, count_two_matrix(): pl.pallas_call(count_two_kernel, grid=(nodes // 256,), out_shape=jax.Shap...  6.93 us
  transfers between devices with their start and end apart: 11, of which 5 were waited for; matrix products, arithmetic and copies ran while one was open for 4% of the time, Pallas kernels for 18%

profile of v5, /device:TPU:1, one launch (start us, length us, event | category | flops | bytes accessed | tf_op | source)
XLA Modules:
  0.0 167.4 jit_solution(738187794282742460)
XLA Ops:
  0.6 1.4 all_to_all.23
  2.0 10.0 %all-to-all-start = ((s32[16,1,512]{2,1,0:T(1,128)}), s32[16,1,512]{2,1,0:T(1,128)S(1)}, u32[]{:S(2)}, u32[]{:S(2)}) async-start(s32[16,1,512]{2,1,0:T(1,128)} %all_to_all.23), calls=%async_computation | async-start | bytes 65536 | tf_op jit(solution)/shard_map/all_to_all | solution.py:21
  12.0 0.0 copy-start
  12.0 1.1 copy-done
  13.1 0.0 copy-start.3
  13.1 0.7 copy-done.3
  13.9 0.7 copy-done.4
  14.6 0.7 copy-done.5
  15.3 0.7 copy-done.7
  16.0 0.7 copy-done.8
  16.7 0.7 copy-done.9
  17.3 0.1 pack.1
  17.4 2.0 %all-to-all-done = s32[16,1,512]{2,1,0:T(1,128)S(1)} async-done(((s32[16,1,512]{2,1,0:T(1,128)}), s32[16,1,512]{2,1,0:T(1,128)S(1)}, u32[]{:S(2)}, u32[]{:S(2)}) %all-to-all-start) | async-done | bytes 32800 | tf_op jit(solution)/shard_map/all_to_all | solution.py:21
  19.4 2.5 %collective-permute-start.2 = (bf16[128,256]{1,0:T(8,128)(2,1)S(1)}, bf16[128,256]{1,0:T(8,128)(2,1)S(1)}, u32[]{:S(2)}, u32[]{:S(2)}) collective-permute-start(bf16[128,256]{1,0:T(8,128)(2,1)S(1)} %get-tuple-element.22), channel_id=1, source_target_pairs={{0,3},{1,0},{2,1},{3,2},{4,7},{5,4},{6,5},{7,6},{8,11},{9,8},{10,9... | collective-permute-start | bytes 196616 | tf_op jit(solution)/shard_map/ppermute | solution.py:510
  21.9 0.0 collective-permute-start
  21.9 1.7 %collective-permute-start.1 = (bf16[128,256]{1,0:T(8,128)(2,1)S(1)}, bf16[128,256]{1,0:T(8,128)(2,1)S(1)}, u32[]{:S(2)}, u32[]{:S(2)}) collective-permute-start(bf16[128,256]{1,0:T(8,128)(2,1)S(1)} %get-tuple-element.22), channel_id=1, source_target_pairs={{0,2},{1,3},{2,0},{3,1},{4,6},{5,7},{6,4},{7,5},{8,10},{9,11},{10,... | collective-permute-start | bytes 196616 | tf_op jit(solution)/shard_map/ppermute | solution.py:510
  23.6 10.0 %serve.1 = bf16[16,48,512]{2,1,0:T(8,128)(2,1)} custom-call(s32[8192]{0:T(1024)S(1)} %bitcast.28, bf16[48,8192]{1,0:T(8,128)(2,1)S(1)} %get-tuple-element.21.feat_ref), custom_call_target="tpu_custom_call" | custom-call | tf_op jit(solution)/shard_map/serve/pallas_call | solution.py:72
  33.6 0.0 collective-permute-done.2
  33.6 0.0 collective-permute-done
  33.6 0.0 collective-permute-done.1
  33.6 0.0 copy-start.6
  33.6 6.1 %all-to-all-start.1 = ((bf16[16,48,512]{2,1,0:T(8,128)(2,1)}), bf16[16,48,512]{2,1,0:T(8,128)(2,1)S(1)}, u32[]{:S(2)}, u32[]{:S(2)}) async-start(bf16[16,48,512]{2,1,0:T(8,128)(2,1)} %serve.1), calls=%async_computation.1 | async-start | bytes 1572864 | tf_op jit(solution)/shard_map/all_to_all | solution.py:21
  39.8 1.3 collective-permute-start.3
  41.1 2.6 %collective-permute-start.4 = (bf16[4,128,256]{2,1,0:T(8,128)(2,1)S(1)}, bf16[4,128,256]{2,1,0:T(8,128)(2,1)S(1)}, u32[]{:S(2)}, u32[]{:S(2)}) collective-permute-start(bf16[4,128,256]{2,1,0:T(8,128)(2,1)S(1)} %pad_maximum_fusion.refs_0_), channel_id=1, source_target_pairs={{0,8},{1,9},{2,10},{3,11},{4,12},{5,13},{6,14},{7,15},{8,0},{9,1},... | collective-permute-start | bytes 786440 | tf_op jit(solution)/shard_map/ppermute | solution.py:513
  43.7 1.1 collective-permute-start.5
  44.8 0.9 copy-done.10
  45.7 0.7 copy-done.11
  46.4 13.7 %count_one.1.counts_ref = f8e4m3fn[8,2048,1024]{2,1,0:T(32,128)(4,1)} custom-call(s32[16,2048]{1,0:T(8,128)S(1)} %bitcast.33, s32[1,2048]{1,0:T(1,128)S(1)} %copy-done.11), custom_call_target="tpu_custom_call" | custom-call | flops 8589934592 | bytes 16777216 | tf_op jit(solution)/shard_map/count_one/pallas_call | solution.py:192
  60.1 0.0 collective-permute-done.3.refs_1_
  60.1 0.0 collective-permute-done.4.refs_2_
  60.1 0.0 collective-permute-done.5.refs_3_
  60.1 2.3 %all-to-all-done.1.front_ref = bf16[16,48,512]{2,1,0:T(8,128)(2,1)S(1)} async-done(((bf16[16,48,512]{2,1,0:T(8,128)(2,1)}), bf16[16,48,512]{2,1,0:T(8,128)(2,1)S(1)}, u32[]{:S(2)}, u32[]{:S(2)}) %all-to-all-start.1) | async-done | bytes 786464 | tf_op jit(solution)/shard_map/all_to_all | solution.py:21
  62.5 0.0 copy-done.6
  62.5 12.5 %first_hop.1.rows_ref = bf16[16,96,128]{2,1,0:T(8,128)(2,1)} custom-call(s32[2048]{0:T(1024)S(1)} %bitcast.31, f8e4m3fn[8,2048,1024]{2,1,0:T(32,128)(4,1)} %count_one.1.counts_ref, bf16[16,48,512]{2,1,0:T(8,128)(2,1)S(1)} %all-to-all-done.1.front_ref), custom_call_target="tpu_custom_call" | custom-call | flops 4294967296 | bytes 16777216 | tf_op jit(solution)/shard_map/first_hop/pallas_call | solution.py:313
  74.9 5.5 %all-to-all-start.2 = ((bf16[16,96,128]{2,1,0:T(8,128)(2,1)}), bf16[16,96,128]{2,1,0:T(8,128)(2,1)S(1)}, u32[]{:S(2)}, u32[]{:S(2)}) async-start(bf16[16,96,128]{2,1,0:T(8,128)(2,1)} %first_hop.1.rows_ref), calls=%async_computation.2 | async-start | bytes 786432 | tf_op jit(solution)/shard_map/all_to_all | solution.py:21
  80.5 0.1 pad_add_fusion.me_ref
  80.6 9.1 %all-to-all-done.2.mine_ref = bf16[16,96,128]{2,1,0:T(8,128)(2,1)S(1)} async-done(((bf16[16,96,128]{2,1,0:T(8,128)(2,1)}), bf16[16,96,128]{2,1,0:T(8,128)(2,1)S(1)}, u32[]{:S(2)}, u32[]{:S(2)}) %all-to-all-start.2) | async-done | bytes 393248 | tf_op jit(solution)/shard_map/all_to_all | solution.py:21
  89.7 2.0 %first_layer.1 = (bf16[16,256,128]{2,1,0:T(8,128)(2,1)}, f32[16,32,256]{2,1,0:T(8,128)S(1)}) custom-call(s32[2]{0:T(128)S(1)} %pad_add_fusion.me_ref, bf16[16,96,128]{2,1,0:T(8,128)(2,1)S(1)} %all-to-all-done.2.mine_ref, bf16[4,128,256]{2,1,0:T(8,128)(2,1)S(1)} %pad_maximum_fusion.refs_0_, bf16[4,128,256]{2,1,0:T(8,128)(2,1)S(1)} %collective-permute-done.3.refs_1_, ...), custom_call_target="tpu_custom_call" | custom-call | tf_op jit(solution)/shard_map/first_layer/pallas_call | solution.py:363
  91.7 3.7 %all-to-all-start.3 = ((bf16[16,256,128]{2,1,0:T(8,128)(2,1)}), bf16[16,256,128]{2,1,0:T(8,128)(2,1)S(1)}, u32[]{:S(2)}, u32[]{:S(2)}) async-start(bf16[16,256,128]{2,1,0:T(8,128)(2,1)} %get-tuple-element.31), calls=%async_computation.3 | async-start | bytes 2097152 | tf_op jit(solution)/shard_map/all_to_all | solution.py:21
  95.3 0.0 copy-done.12
  95.4 0.2 reshape.80
  95.6 1.0 copy.26
  96.7 1.4 reshape.81.keys_ref
  98.1 0.2 reshape.82
  98.3 1.0 copy.27
  99.4 1.4 reshape.83.lows_ref
  100.8 0.1 reshape.79
  100.9 0.1 divide_reduce_fusion
  101.0 0.1 add.33.self_ref
  101.0 0.1 div.24.inv_ref
  101.1 6.9 %count_two.1 = bf16[1,1536,2048]{2,1,0:T(8,128)(2,1)} custom-call(f32[96,256]{1,0:T(8,128)S(1)} %reshape.81.keys_ref, f32[96,256]{1,0:T(8,128)S(1)} %reshape.83.lows_ref), custom_call_target="tpu_custom_call" | custom-call | flops 1610612736 | bytes 6291456 | tf_op jit(solution)/shard_map/count_two/pallas_call | solution.py:224
  108.1 7.3 %all-to-all-done.3.hidden_ref = bf16[16,256,128]{2,1,0:T(8,128)(2,1)S(1)} async-done(((bf16[16,256,128]{2,1,0:T(8,128)(2,1)}), bf16[16,256,128]{2,1,0:T(8,128)(2,1)S(1)}, u32[]{:S(2)}, u32[]{:S(2)}) %all-to-all-start.3) | async-done | bytes 1048608 | tf_op jit(solution)/shard_map/all_to_all | solution.py:21
  115.4 0.0 copy-done.1
  115.4 0.0 copy-done.2
  115.4 15.9 %second_layer.1 = bf16[16,40,256]{2,1,0:T(8,128)(2,1)S(1)} custom-call(bf16[16,256,128]{2,1,0:T(8,128)(2,1)S(1)} %all-to-all-done.3.hidden_ref, bf16[16,96,128]{2,1,0:T(8,128)(2,1)} %first_hop.1.rows_ref, f32[1,1536]{1,0:T(1,128)S(1)} %add.33.self_ref, f32[1,1536]{1,0:T(1,128)S(1)} %pad_maximum_fusion.1.ends_ref, f32[1,1536]{1,0:T(1,128)S(1)} %div.24.inv_ref, ...), custom_call_target="tpu_custom_call" | custom-call | tf_op jit(solution)/shard_map/second_layer/pallas_call | solution.py:450
  131.3 15.9 %all_to_all.37 = bf16[16,40,256]{2,1,0:T(8,128)(2,1)S(1)} all-to-all(bf16[16,40,256]{2,1,0:T(8,128)(2,1)S(1)} %second_layer.1), channel_id=1, replica_groups=mesh['graph'=16,'feat'=16] {'graph'}, dimensions={0} | all-to-all | bytes 655360 | tf_op jit(solution)/shard_map/all_to_all | solution.py:21
  147.2 0.1 convert_reduce_fusion
  147.2 0.8 broadcast_in_dim.2
  148.0 3.4 %all-to-all-start.5 = ((bf16[16,40,256]{2,1,0:T(8,128)(2,1)}), bf16[16,40,256]{2,1,0:T(8,128)(2,1)S(1)}, u32[]{:S(2)}, u32[]{:S(2)}) async-start(bf16[16,40,256]{2,1,0:T(8,128)(2,1)} %broadcast_in_dim.2), calls=%async_computation.5 | async-start | bytes 655360 | tf_op jit(solution)/shard_map/all_to_all | solution.py:21
  151.4 0.6 slice_reduce_fusion
  152.7 11.4 %all-to-all-done.5 = bf16[16,40,256]{2,1,0:T(8,128)(2,1)S(1)} async-done(((bf16[16,40,256]{2,1,0:T(8,128)(2,1)}), bf16[16,40,256]{2,1,0:T(8,128)(2,1)S(1)}, u32[]{:S(2)}, u32[]{:S(2)}) %all-to-all-start.5) | async-done | bytes 327712 | tf_op jit(solution)/shard_map/all_to_all | solution.py:21
  164.1 0.6 slice.65
  164.8 0.6 slice.67
  165.4 0.8 fusion.1
  (22 shorter events, 0.1 us)
Async XLA Ops:
  2.0 17.4 %all-to-all-start = ((s32[16,1,512]{2,1,0:T(1,128)}), s32[16,1,512]{2,1,0:T(1,128)S(1)}, u32[]{:S(2)}, u32[]{:S(2)}) async-start(s32[16,1,512]{2,1,0:T(1,128)} %all_to_all.23), calls=%async_computation | async-start | bytes 65536 | tf_op jit(solution)/shard_map/all_to_all | solution.py:21
  12.0 1.1 copy-start
  13.1 0.7 copy-start.3
  13.9 0.7 copy-start.4
  14.6 0.7 copy-start.5
  15.3 0.7 copy-start.7
  16.0 0.7 copy-start.8
  16.7 0.7 copy-start.9
  19.4 14.2 %collective-permute-start.2 = (bf16[128,256]{1,0:T(8,128)(2,1)S(1)}, bf16[128,256]{1,0:T(8,128)(2,1)S(1)}, u32[]{:S(2)}, u32[]{:S(2)}) collective-permute-start(bf16[128,256]{1,0:T(8,128)(2,1)S(1)} %get-tuple-element.22), channel_id=1, source_target_pairs={{0,3},{1,0},{2,1},{3,2},{4,7},{5,4},{6,5},{7,6},{8,11},{9,8},{10,9... | collective-permute-start | bytes 196616 | tf_op jit(solution)/shard_map/ppermute | solution.py:510
  21.9 11.7 %collective-permute-start = (bf16[128,256]{1,0:T(8,128)(2,1)S(1)}, bf16[128,256]{1,0:T(8,128)(2,1)S(1)}, u32[]{:S(2)}, u32[]{:S(2)}) collective-permute-start(bf16[128,256]{1,0:T(8,128)(2,1)S(1)} %get-tuple-element.22), channel_id=1, source_target_pairs={{0,1},{1,2},{2,3},{3,0},{4,5},{5,6},{6,7},{7,4},{8,9},{9,10},{10,1... | collective-permute-start | bytes 196616 | tf_op jit(solution)/shard_map/ppermute | solution.py:510
  21.9 11.7 %collective-permute-start.1 = (bf16[128,256]{1,0:T(8,128)(2,1)S(1)}, bf16[128,256]{1,0:T(8,128)(2,1)S(1)}, u32[]{:S(2)}, u32[]{:S(2)}) collective-permute-start(bf16[128,256]{1,0:T(8,128)(2,1)S(1)} %get-tuple-element.22), channel_id=1, source_target_pairs={{0,2},{1,3},{2,0},{3,1},{4,6},{5,7},{6,4},{7,5},{8,10},{9,11},{10,... | collective-permute-start | bytes 196616 | tf_op jit(solution)/shard_map/ppermute | solution.py:510
  33.6 28.8 %copy-start.6 = (s32[1,2048]{1,0:T(1,128)S(1)}, s32[1,2048]{1,0:T(1,128)}, u32[]{:S(2)}) copy-start(s32[1,2048]{1,0:T(1,128)} %param.16) | copy-start | bytes 24580
  33.6 28.8 %all-to-all-start.1 = ((bf16[16,48,512]{2,1,0:T(8,128)(2,1)}), bf16[16,48,512]{2,1,0:T(8,128)(2,1)S(1)}, u32[]{:S(2)}, u32[]{:S(2)}) async-start(bf16[16,48,512]{2,1,0:T(8,128)(2,1)} %serve.1), calls=%async_computation.1 | async-start | bytes 1572864 | tf_op jit(solution)/shard_map/all_to_all | solution.py:21
  39.8 20.3 %collective-permute-start.3 = (bf16[4,128,256]{2,1,0:T(8,128)(2,1)S(1)}, bf16[4,128,256]{2,1,0:T(8,128)(2,1)S(1)}, u32[]{:S(2)}, u32[]{:S(2)}) collective-permute-start(bf16[4,128,256]{2,1,0:T(8,128)(2,1)S(1)} %pad_maximum_fusion.refs_0_), channel_id=1, source_target_pairs={{0,4},{1,5},{2,6},{3,7},{4,8},{5,9},{6,10},{7,11},{8,12},{9,13},{1... | collective-permute-start | bytes 786440 | tf_op jit(solution)/shard_map/ppermute | solution.py:513
  41.1 19.0 %collective-permute-start.4 = (bf16[4,128,256]{2,1,0:T(8,128)(2,1)S(1)}, bf16[4,128,256]{2,1,0:T(8,128)(2,1)S(1)}, u32[]{:S(2)}, u32[]{:S(2)}) collective-permute-start(bf16[4,128,256]{2,1,0:T(8,128)(2,1)S(1)} %pad_maximum_fusion.refs_0_), channel_id=1, source_target_pairs={{0,8},{1,9},{2,10},{3,11},{4,12},{5,13},{6,14},{7,15},{8,0},{9,1},... | collective-permute-start | bytes 786440 | tf_op jit(solution)/shard_map/ppermute | solution.py:513
  43.7 16.4 %collective-permute-start.5 = (bf16[4,128,256]{2,1,0:T(8,128)(2,1)S(1)}, bf16[4,128,256]{2,1,0:T(8,128)(2,1)S(1)}, u32[]{:S(2)}, u32[]{:S(2)}) collective-permute-start(bf16[4,128,256]{2,1,0:T(8,128)(2,1)S(1)} %pad_maximum_fusion.refs_0_), channel_id=1, source_target_pairs={{0,12},{1,13},{2,14},{3,15},{4,0},{5,1},{6,2},{7,3},{8,4},{9,5},{1... | collective-permute-start | bytes 786440 | tf_op jit(solution)/shard_map/ppermute | solution.py:513
  44.8 0.9 copy-start.10
  45.7 0.7 copy-start.11
  60.1 35.2 %copy-start.12 = (s32[1,512]{1,0:T(1,128)S(1)}, s32[1,512]{1,0:T(1,128)}, u32[]{:S(2)}) copy-start(s32[1,512]{1,0:T(1,128)} %param.23) | copy-start | bytes 6148
  62.5 52.9 %copy-start.1 = (bf16[256,256]{1,0:T(8,128)(2,1)S(1)}, bf16[256,256]{1,0:T(8,128)(2,1)}, u32[]{:S(2)}) copy-start(bf16[256,256]{1,0:T(8,128)(2,1)} %ws_ref.3) | copy-start | bytes 393220
  62.5 52.9 %copy-start.2 = (bf16[256,256]{1,0:T(8,128)(2,1)S(1)}, bf16[256,256]{1,0:T(8,128)(2,1)}, u32[]{:S(2)}) copy-start(bf16[256,256]{1,0:T(8,128)(2,1)} %wn_ref.3) | copy-start | bytes 393220
  74.9 14.8 %all-to-all-start.2 = ((bf16[16,96,128]{2,1,0:T(8,128)(2,1)}), bf16[16,96,128]{2,1,0:T(8,128)(2,1)S(1)}, u32[]{:S(2)}, u32[]{:S(2)}) async-start(bf16[16,96,128]{2,1,0:T(8,128)(2,1)} %first_hop.1.rows_ref), calls=%async_computation.2 | async-start | bytes 786432 | tf_op jit(solution)/shard_map/all_to_all | solution.py:21
  91.7 23.7 %all-to-all-start.3 = ((bf16[16,256,128]{2,1,0:T(8,128)(2,1)}), bf16[16,256,128]{2,1,0:T(8,128)(2,1)S(1)}, u32[]{:S(2)}, u32[]{:S(2)}) async-start(bf16[16,256,128]{2,1,0:T(8,128)(2,1)} %get-tuple-element.31), calls=%async_computation.3 | async-start | bytes 2097152 | tf_op jit(solution)/shard_map/all_to_all | solution.py:21
  148.0 16.1 %all-to-all-start.5 = ((bf16[16,40,256]{2,1,0:T(8,128)(2,1)}), bf16[16,40,256]{2,1,0:T(8,128)(2,1)S(1)}, u32[]{:S(2)}, u32[]{:S(2)}) async-start(bf16[16,40,256]{2,1,0:T(8,128)(2,1)} %broadcast_in_dim.2), calls=%async_computation.5 | async-start | bytes 655360 | tf_op jit(solution)/shard_map/all_to_all | solution.py:21

commit v6 on v5

--- a/solution.py
+++ b/solution.py
@@ -24,6 +24,10 @@
 def gather_all(value, axis):
     size = lax.axis_size(axis)
     return swap(jnp.broadcast_to(value[None], (size,) + value.shape), axis)
+
+
+def in_hbm(value):
+    return pltpu.with_memory_space_constraint(value, pltpu.HBM)
 
 
 def dot(former, latter, dims):
@@ -83,10 +87,17 @@
     )(ids, features_t)
 
 
-def pack_kernel(
-    across, self_ref, neigh_ref, count_ref, pairs_ref, ws_ref, wn_ref, feat_ref, out_ref, copy_ref, rows
-):
-    copy_ref[...] = feat_ref[...]
+def pack_kernel(across, *refs):
+    sources, (out_ref, copy_ref), held, rows, sems = refs[:7], refs[7:9], refs[9:15], refs[15], refs[16]
+    copies = [
+        pltpu.make_async_copy(source, place, sems.at[at])
+        for at, (source, place) in enumerate(zip(sources, [*held, copy_ref]))
+    ]
+    for copy in copies:
+        copy.start()
+    for copy in copies:
+        copy.wait()
+    self_ref, neigh_ref, count_ref, pairs_ref, ws_ref, wn_ref = held
     width = ws_ref.shape[0]
     fan, share = neigh_ref.shape
     pairs = pairs_ref.shape[1]
@@ -112,16 +123,24 @@
 
 def pack(self_two, neigh_two, count_two, pairs, ws, wn, features_t, across):
     width, wide = ws.shape
+    operands = (self_two, neigh_two, count_two, pairs, ws, wn, features_t)
+    held = [pltpu.VMEM(value.shape, value.dtype) for value in operands[:6]]
     return pl.pallas_call(
         functools.partial(pack_kernel, across),
         out_shape=[
             jax.ShapeDtypeStruct((2 * width + 32, wide), BF),
             jax.ShapeDtypeStruct(features_t.shape, BF),
         ],
-        scratch_shapes=[pltpu.VMEM((32, wide), F32)],
+        in_specs=[pl.BlockSpec(memory_space=pl.ANY)] * len(operands),
+        out_specs=[pl.BlockSpec(memory_space=pltpu.VMEM)] * 2,
+        scratch_shapes=[
+            *held,
+            pltpu.VMEM((32, wide), F32),
+            pltpu.SemaphoreType.DMA((len(operands),)),
+        ],
         compiler_params=pltpu.CompilerParams(vmem_limit_bytes=16 * 2**20),
         name="pack",
-    )(self_two, neigh_two, count_two, pairs, ws, wn, features_t)
+    )(*(in_hbm(value) for value in operands))
 
 
 def count_blocks(keys_ref, lows_ref, base, out_ref, marks):
@@ -167,12 +186,18 @@
     return lax.broadcasted_iota(jnp.int32, (256, 256), 0).astype(F32).astype(BF)
 
 
-def count_one_kernel(ids_ref, live_ref, out_ref, marks, keys, lows):
+def count_one_kernel(ids_from, live_from, out_ref, marks, keys, lows, ids_ref, live_ref, sems):
     fan = ids_ref.shape[0]
 
     @pl.when(pl.program_id(0) == 0)
     def _():
+        first = pltpu.make_async_copy(ids_from, ids_ref, sems.at[0])
+        other = pltpu.make_async_copy(live_from, live_ref, sems.at[1])
+        first.start()
+        other.start()
         marks[...] = all_marks()
+        first.wait()
+        other.wait()
         slots = lax.broadcasted_iota(jnp.int32, (fan, 128), 0)
         high = []
         low = []
@@ -193,50 +218,58 @@
         count_one_kernel,
         grid=(nodes // 256,),
         out_shape=jax.ShapeDtypeStruct((total // chunk, nodes, chunk), F8),
-        in_specs=[
-            pl.BlockSpec((fan, nodes), lambda at: (0, 0)),
-            pl.BlockSpec((1, nodes), lambda at: (0, 0)),
-        ],
+        in_specs=[pl.BlockSpec(memory_space=pl.ANY)] * 2,
         out_specs=pl.BlockSpec((total // chunk, 256, chunk), lambda at: (0, at, 0)),
         scratch_shapes=[
             pltpu.VMEM((256, 256), BF),
             pltpu.VMEM((128, 256), F32),
             pltpu.VMEM((128, 256), F32),
+            pltpu.VMEM((fan, nodes), jnp.int32),
+            pltpu.VMEM((1, nodes), jnp.int32),
+            pltpu.SemaphoreType.DMA((2,)),
         ],
         compiler_params=pltpu.CompilerParams(vmem_limit_bytes=VMEM_LIMIT),
         cost_estimate=pl.CostEstimate(
             flops=2 * nodes * total * 256, bytes_accessed=nodes * total, transcendentals=0
         ),
         name="count_one",
-    )(ids, live)
-
-
-def count_two_kernel(keys_ref, lows_ref, out_ref, marks):
+    )(in_hbm(ids), in_hbm(live))
+
+
+def count_two_kernel(fan, sent_ref, out_ref, marks, keys, lows):
     @pl.when(pl.program_id(0) == 0)
     def _():
         marks[...] = all_marks()
-
-    count_blocks(keys_ref, lows_ref, 0, out_ref, marks)
-
-
-def count_two_matrix(keys, lows, total):
-    nodes = keys.shape[0] * 16
+        high = []
+        low = []
+        for device in range(sent_ref.shape[0]):
+            low.append(sent_ref[device, 0:fan, 0:128])
+            high.append(sent_ref[device, 0:fan, 128:256] * 16.0 + float(device))
+        keys[...] = jnp.concatenate(high, axis=0).T
+        lows[...] = jnp.concatenate(low, axis=0).T
+
+    count_blocks(keys, lows, pl.program_id(0) * 16, out_ref, marks)
+
+
+def count_two_matrix(sent, fan, share, total):
+    nodes = sent.shape[0] * share
     return pl.pallas_call(
-        count_two_kernel,
+        functools.partial(count_two_kernel, fan),
         grid=(nodes // 256,),
         out_shape=jax.ShapeDtypeStruct((1, nodes, total), BF),
-        in_specs=[
-            pl.BlockSpec((16, 256), lambda at: (at, 0)),
-            pl.BlockSpec((16, 256), lambda at: (at, 0)),
-        ],
+        in_specs=[pl.BlockSpec(sent.shape, lambda at: (0, 0, 0))],
         out_specs=pl.BlockSpec((1, 256, total), lambda at: (0, at, 0)),
-        scratch_shapes=[pltpu.VMEM((256, 256), BF)],
+        scratch_shapes=[
+            pltpu.VMEM((256, 256), BF),
+            pltpu.VMEM((128, 256), F32),
+            pltpu.VMEM((128, 256), F32),
+        ],
         compiler_params=pltpu.CompilerParams(vmem_limit_bytes=VMEM_LIMIT),
         cost_estimate=pl.CostEstimate(
             flops=2 * nodes * total * 256, bytes_accessed=2 * nodes * total, transcendentals=0
         ),
         name="count_two",
-    )(keys, lows)
+    )(sent)
 
 
 def hop_kernel(
@@ -518,21 +551,16 @@
     hidden, sent = first(swap(rows_one, "feat"), early, me)
     hidden = swap(hidden, "feat")
 
-    def blocks(value):
-        value = value.reshape(feats, fan, share // 16, 16).transpose(0, 2, 1, 3)
-        return value.reshape(-1, fan * 16)
-
-    node = (lax.broadcasted_iota(jnp.int32, (feats, fan, share), 2) % 16).astype(F32)
-    keys = blocks(sent[:, :fan, 128 : 128 + share] * 16.0 + node)
-    pick_neigh = count_two_matrix(keys, blocks(sent[:, :fan, :share]), nodes)[0]
+    pick_neigh = count_two_matrix(sent, fan, share, nodes)[0]
     self_two = sent[:, fan, :share] + sent[:, fan, 128 : 128 + share] * 256.0
-    self_two = self_two.reshape(1, -1)
-    inv_two = 1.0 / sent[:, fan + 1, :share].reshape(1, -1)
+    self_two = self_two.T.reshape(1, -1)
+    inv_two = 1.0 / sent[:, fan + 1, :share].T.reshape(1, -1)
     pairs = sent[:, fan + 2 : fan + 4]
     pairs = pairs[:, :, :pair_share] + pairs[:, :, 128 : 128 + pair_share] * 256.0
     pairs = pairs.transpose(1, 0, 2)
     pair_total = feats * pair_share
-    ends = jnp.concatenate([pairs.reshape(1, -1), neg_ids.astype(F32)], axis=1)
+    ends = jnp.concatenate([pairs.reshape(1, -1).astype(jnp.int32), neg_ids], axis=1)
+    ends = (ends % share * feats + ends // share).astype(F32)
     parts = second(
         hidden,
         rows_one,

time: 169 us -> 167 us (0.988)
  local copies, waits for them, and re-layouts: 16.8 us -> 4.75 us
  waiting for transfers between devices: 32.3 us -> 42.2 us
  Pallas kernels: 61 us -> 63.2 us
    all_to_all x5, waiting for transfers between devices: 32.3 us -> 42.2 us  [swap(): return lax.all_to_all(value, axis, split_axis=0, concat_axis=0, tiled=True)]
    unnamed x28 -> x11, local copies, waits for them, and re-layouts: 6.91 us -> 0.04 us
    reshape x5 -> x1, local copies, waits for them, and re-layouts: 3.42 us -> 0.09 us  [local(): self_two = self_two.T.reshape(1, -1)]
    transpose x3 -> x1, local copies, waits for them, and re-layouts: 2.05 us -> 0.09 us  [local(): self_two = self_two.T.reshape(1, -1)]
  transfers between devices with their start and end apart: 11 -> 11, of which waited for: 5 -> 5; matrix products, arithmetic and copies ran while one was open for 4% -> 1% of each run, Pallas kernels for 18% -> 20%
where the time goes in v6:
time: 167 us; the launch traced here: 166 us
  Pallas kernels  63.2 us (38%)
  waiting for transfers between devices  42.2 us (25%)
  starting transfers between devices  36.6 us (22%)
  blocking collectives  15.9 us (10%)
  local copies, waits for them, and re-layouts  4.75 us (3%)
  between operations  2.61 us (2%)
    all_to_all x5, waiting for transfers between devices, swap(): return lax.all_to_all(value, axis, split_axis=0, concat_axis=0, tiled=True)  42.2 us
    all_to_all x5, starting transfers between devices, swap(): return lax.all_to_all(value, axis, split_axis=0, concat_axis=0, tiled=True)  27.4 us
    pallas_call x1, Pallas kernels, second(): pl.pallas_call(functools.partial(second_kernel, scale, negative_total), o...  15.9 us
    all_to_all x1, blocking collectives, swap(): return lax.all_to_all(value, axis, split_axis=0, concat_axis=0, tiled=True)  15.9 us
    pallas_call x1, Pallas kernels, count_one_matrix(): pl.pallas_call(count_one_kernel, grid=(nodes // 256,), out_shape=jax.Shap...  14.6 us
    pallas_call x1, Pallas kernels, hop(): pl.pallas_call(functools.partial(hop_kernel, chunks), grid=(chunks,), out...  12.4 us
    pallas_call x1, Pallas kernels, serve(): pl.pallas_call(serve_kernel, out_shape=jax.ShapeDtypeStruct((groups, widt...  9.94 us
    pallas_call x1, Pallas kernels, count_two_matrix(): pl.pallas_call(functools.partial(count_two_kernel, fan), grid=(nodes // 2...  7.07 us
  transfers between devices with their start and end apart: 11, of which 5 were waited for; matrix products, arithmetic and copies ran while one was open for 1% of the time, Pallas kernels for 20%

profile of v6, /device:TPU:1, one launch (start us, length us, event | category | flops | bytes accessed | tf_op | source)
XLA Modules:
  0.0 166.2 jit_solution(12851286311694180383)
XLA Ops:
  0.6 1.4 all_to_all.23
  2.0 10.0 %all-to-all-start = ((s32[16,1,512]{2,1,0:T(1,128)}), s32[16,1,512]{2,1,0:T(1,128)S(1)}, u32[]{:S(2)}, u32[]{:S(2)}) async-start(s32[16,1,512]{2,1,0:T(1,128)} %all_to_all.23), calls=%async_computation | async-start | bytes 65536 | tf_op jit(solution)/shard_map/all_to_all | solution.py:21
  12.0 1.3 pack.1
  13.3 6.1 %all-to-all-done = s32[16,1,512]{2,1,0:T(1,128)S(1)} async-done(((s32[16,1,512]{2,1,0:T(1,128)}), s32[16,1,512]{2,1,0:T(1,128)S(1)}, u32[]{:S(2)}, u32[]{:S(2)}) %all-to-all-start) | async-done | bytes 32800 | tf_op jit(solution)/shard_map/all_to_all | solution.py:21
  19.4 2.5 %collective-permute-start.2 = (bf16[128,256]{1,0:T(8,128)(2,1)S(1)}, bf16[128,256]{1,0:T(8,128)(2,1)S(1)}, u32[]{:S(2)}, u32[]{:S(2)}) collective-permute-start(bf16[128,256]{1,0:T(8,128)(2,1)S(1)} %get-tuple-element.22), channel_id=1, source_target_pairs={{0,3},{1,0},{2,1},{3,2},{4,7},{5,4},{6,5},{7,6},{8,11},{9,8},{10,9... | collective-permute-start | bytes 196616 | tf_op jit(solution)/shard_map/ppermute | solution.py:543
  21.9 0.0 collective-permute-start
  21.9 1.7 %collective-permute-start.1 = (bf16[128,256]{1,0:T(8,128)(2,1)S(1)}, bf16[128,256]{1,0:T(8,128)(2,1)S(1)}, u32[]{:S(2)}, u32[]{:S(2)}) collective-permute-start(bf16[128,256]{1,0:T(8,128)(2,1)S(1)} %get-tuple-element.22), channel_id=1, source_target_pairs={{0,2},{1,3},{2,0},{3,1},{4,6},{5,7},{6,4},{7,5},{8,10},{9,11},{10,... | collective-permute-start | bytes 196616 | tf_op jit(solution)/shard_map/ppermute | solution.py:543
  23.6 9.9 %serve.1 = bf16[16,48,512]{2,1,0:T(8,128)(2,1)} custom-call(s32[8192]{0:T(1024)S(1)} %bitcast.27, bf16[48,8192]{1,0:T(8,128)(2,1)S(1)} %get-tuple-element.21.feat_ref), custom_call_target="tpu_custom_call" | custom-call | tf_op jit(solution)/shard_map/serve/pallas_call | solution.py:76
  33.6 0.0 collective-permute-done.2
  33.6 0.0 collective-permute-done
  33.6 0.0 collective-permute-done.1
  33.6 0.0 copy-start.2
  33.6 4.6 %all-to-all-start.1 = ((bf16[16,48,512]{2,1,0:T(8,128)(2,1)}), bf16[16,48,512]{2,1,0:T(8,128)(2,1)S(1)}, u32[]{:S(2)}, u32[]{:S(2)}) async-start(bf16[16,48,512]{2,1,0:T(8,128)(2,1)} %serve.1), calls=%async_computation.1 | async-start | bytes 1572864 | tf_op jit(solution)/shard_map/all_to_all | solution.py:21
  38.3 1.3 collective-permute-start.3
  39.6 2.6 %collective-permute-start.4 = (bf16[4,128,256]{2,1,0:T(8,128)(2,1)S(1)}, bf16[4,128,256]{2,1,0:T(8,128)(2,1)S(1)}, u32[]{:S(2)}, u32[]{:S(2)}) collective-permute-start(bf16[4,128,256]{2,1,0:T(8,128)(2,1)S(1)} %pad_maximum_fusion.refs_0_), channel_id=1, source_target_pairs={{0,8},{1,9},{2,10},{3,11},{4,12},{5,13},{6,14},{7,15},{8,0},{9,1},... | collective-permute-start | bytes 786440 | tf_op jit(solution)/shard_map/ppermute | solution.py:546
  42.2 1.1 collective-permute-start.5
  43.3 14.6 %count_one.1.counts_ref = f8e4m3fn[8,2048,1024]{2,1,0:T(32,128)(4,1)} custom-call(s32[16,2048]{1,0:T(8,128)} %bitcast.42, s32[1,2048]{1,0:T(1,128)} %live_from.1), custom_call_target="tpu_custom_call" | custom-call | flops 8589934592 | bytes 16777216 | tf_op jit(solution)/shard_map/count_one/pallas_call | solution.py:217
  57.9 0.0 copy-start.3
  57.9 0.0 copy-start
  57.9 0.0 copy-start.1
  57.9 0.0 collective-permute-done.3.refs_1_
  58.0 0.0 collective-permute-done.4.refs_2_
  58.0 0.0 collective-permute-done.5.refs_3_
  58.0 3.0 %all-to-all-done.1.front_ref = bf16[16,48,512]{2,1,0:T(8,128)(2,1)S(1)} async-done(((bf16[16,48,512]{2,1,0:T(8,128)(2,1)}), bf16[16,48,512]{2,1,0:T(8,128)(2,1)S(1)}, u32[]{:S(2)}, u32[]{:S(2)}) %all-to-all-start.1) | async-done | bytes 786464 | tf_op jit(solution)/shard_map/all_to_all | solution.py:21
  61.0 0.0 copy-done.2
  61.0 12.4 %first_hop.1.rows_ref = bf16[16,96,128]{2,1,0:T(8,128)(2,1)} custom-call(s32[2048]{0:T(1024)S(1)} %bitcast.29, f8e4m3fn[8,2048,1024]{2,1,0:T(32,128)(4,1)} %count_one.1.counts_ref, bf16[16,48,512]{2,1,0:T(8,128)(2,1)S(1)} %all-to-all-done.1.front_ref), custom_call_target="tpu_custom_call" | custom-call | flops 4294967296 | bytes 16777216 | tf_op jit(solution)/shard_map/first_hop/pallas_call | solution.py:346
  73.4 5.5 %all-to-all-start.2 = ((bf16[16,96,128]{2,1,0:T(8,128)(2,1)}), bf16[16,96,128]{2,1,0:T(8,128)(2,1)S(1)}, u32[]{:S(2)}, u32[]{:S(2)}) async-start(bf16[16,96,128]{2,1,0:T(8,128)(2,1)} %first_hop.1.rows_ref), calls=%async_computation.2 | async-start | bytes 786432 | tf_op jit(solution)/shard_map/all_to_all | solution.py:21
  79.0 0.1 pad_add_fusion.me_ref
  79.1 9.1 %all-to-all-done.2.mine_ref = bf16[16,96,128]{2,1,0:T(8,128)(2,1)S(1)} async-done(((bf16[16,96,128]{2,1,0:T(8,128)(2,1)}), bf16[16,96,128]{2,1,0:T(8,128)(2,1)S(1)}, u32[]{:S(2)}, u32[]{:S(2)}) %all-to-all-start.2) | async-done | bytes 393248 | tf_op jit(solution)/shard_map/all_to_all | solution.py:21
  88.2 2.0 %first_layer.1 = (bf16[16,256,128]{2,1,0:T(8,128)(2,1)}, f32[16,32,256]{2,1,0:T(8,128)S(1)}) custom-call(s32[2]{0:T(128)S(1)} %pad_add_fusion.me_ref, bf16[16,96,128]{2,1,0:T(8,128)(2,1)S(1)} %all-to-all-done.2.mine_ref, bf16[4,128,256]{2,1,0:T(8,128)(2,1)S(1)} %pad_maximum_fusion.refs_0_, bf16[4,128,256]{2,1,0:T(8,128)(2,1)S(1)} %collective-permute-done.3.refs_1_, ...), custom_call_target="tpu_custom_call" | custom-call | tf_op jit(solution)/shard_map/first_layer/pallas_call | solution.py:396
  90.1 0.1 copy.27
  90.2 0.1 div.45.inv_ref
  90.3 0.1 copy.25
  90.4 0.1 reshape.198.self_ref
  90.5 3.8 %all-to-all-start.3 = ((bf16[16,256,128]{2,1,0:T(8,128)(2,1)}), bf16[16,256,128]{2,1,0:T(8,128)(2,1)S(1)}, u32[]{:S(2)}, u32[]{:S(2)}) async-start(bf16[16,256,128]{2,1,0:T(8,128)(2,1)} %get-tuple-element.31), calls=%async_computation.3 | async-start | bytes 2097152 | tf_op jit(solution)/shard_map/all_to_all | solution.py:21
  94.4 0.1 concatenate.31
  94.5 0.0 copy-done.3
  94.5 7.1 %count_two.1 = bf16[1,1536,2048]{2,1,0:T(8,128)(2,1)} custom-call(f32[16,32,256]{2,1,0:T(8,128)S(1)} %get-tuple-element.32.sent_ref), custom_call_target="tpu_custom_call" | custom-call | flops 1610612736 | bytes 6291456 | tf_op jit(solution)/shard_map/count_two/pallas_call | solution.py:256
  101.6 0.1 fusion.2.ends_ref
  101.6 12.6 %all-to-all-done.3.hidden_ref = bf16[16,256,128]{2,1,0:T(8,128)(2,1)S(1)} async-done(((bf16[16,256,128]{2,1,0:T(8,128)(2,1)}), bf16[16,256,128]{2,1,0:T(8,128)(2,1)S(1)}, u32[]{:S(2)}, u32[]{:S(2)}) %all-to-all-start.3) | async-done | bytes 1048608 | tf_op jit(solution)/shard_map/all_to_all | solution.py:21
  114.2 0.0 copy-done
  114.2 0.0 copy-done.1
  114.2 15.9 %second_layer.1 = bf16[16,40,256]{2,1,0:T(8,128)(2,1)S(1)} custom-call(bf16[16,256,128]{2,1,0:T(8,128)(2,1)S(1)} %all-to-all-done.3.hidden_ref, bf16[16,96,128]{2,1,0:T(8,128)(2,1)} %first_hop.1.rows_ref, f32[1,1536]{1,0:T(1,128)S(1)} %reshape.198.self_ref, f32[1,1536]{1,0:T(1,128)S(1)} %fusion.2.ends_ref, f32[1,1536]{1,0:T(1,128)S(1)} %div.45.inv_ref, ...), custom_call_target="tpu_custom_call" | custom-call | tf_op jit(solution)/shard_map/second_layer/pallas_call | solution.py:483
  130.2 15.9 %all_to_all.37 = bf16[16,40,256]{2,1,0:T(8,128)(2,1)S(1)} all-to-all(bf16[16,40,256]{2,1,0:T(8,128)(2,1)S(1)} %second_layer.1), channel_id=1, replica_groups=mesh['graph'=16,'feat'=16] {'graph'}, dimensions={0} | all-to-all | bytes 655360 | tf_op jit(solution)/shard_map/all_to_all | solution.py:21
  146.0 0.1 convert_reduce_fusion
  146.1 0.7 broadcast_in_dim.2
  146.8 3.4 %all-to-all-start.5 = ((bf16[16,40,256]{2,1,0:T(8,128)(2,1)}), bf16[16,40,256]{2,1,0:T(8,128)(2,1)S(1)}, u32[]{:S(2)}, u32[]{:S(2)}) async-start(bf16[16,40,256]{2,1,0:T(8,128)(2,1)} %broadcast_in_dim.2), calls=%async_computation.5 | async-start | bytes 655360 | tf_op jit(solution)/shard_map/all_to_all | solution.py:21
  150.3 0.6 slice_reduce_fusion
  151.5 11.4 %all-to-all-done.5 = bf16[16,40,256]{2,1,0:T(8,128)(2,1)S(1)} async-done(((bf16[16,40,256]{2,1,0:T(8,128)(2,1)}), bf16[16,40,256]{2,1,0:T(8,128)(2,1)S(1)}, u32[]{:S(2)}, u32[]{:S(2)}) %all-to-all-start.5) | async-done | bytes 327712 | tf_op jit(solution)/shard_map/all_to_all | solution.py:21
  163.0 0.6 slice.57
  163.6 0.6 slice.59
  164.2 0.8 fusion.3
  (10 shorter events, 0.1 us)
Async XLA Ops:
  2.0 17.4 %all-to-all-start = ((s32[16,1,512]{2,1,0:T(1,128)}), s32[16,1,512]{2,1,0:T(1,128)S(1)}, u32[]{:S(2)}, u32[]{:S(2)}) async-start(s32[16,1,512]{2,1,0:T(1,128)} %all_to_all.23), calls=%async_computation | async-start | bytes 65536 | tf_op jit(solution)/shard_map/all_to_all | solution.py:21
  19.4 14.2 %collective-permute-start.2 = (bf16[128,256]{1,0:T(8,128)(2,1)S(1)}, bf16[128,256]{1,0:T(8,128)(2,1)S(1)}, u32[]{:S(2)}, u32[]{:S(2)}) collective-permute-start(bf16[128,256]{1,0:T(8,128)(2,1)S(1)} %get-tuple-element.22), channel_id=1, source_target_pairs={{0,3},{1,0},{2,1},{3,2},{4,7},{5,4},{6,5},{7,6},{8,11},{9,8},{10,9... | collective-permute-start | bytes 196616 | tf_op jit(solution)/shard_map/ppermute | solution.py:543
  21.9 11.7 %collective-permute-start = (bf16[128,256]{1,0:T(8,128)(2,1)S(1)}, bf16[128,256]{1,0:T(8,128)(2,1)S(1)}, u32[]{:S(2)}, u32[]{:S(2)}) collective-permute-start(bf16[128,256]{1,0:T(8,128)(2,1)S(1)} %get-tuple-element.22), channel_id=1, source_target_pairs={{0,1},{1,2},{2,3},{3,0},{4,5},{5,6},{6,7},{7,4},{8,9},{9,10},{10,1... | collective-permute-start | bytes 196616 | tf_op jit(solution)/shard_map/ppermute | solution.py:543
  21.9 11.7 %collective-permute-start.1 = (bf16[128,256]{1,0:T(8,128)(2,1)S(1)}, bf16[128,256]{1,0:T(8,128)(2,1)S(1)}, u32[]{:S(2)}, u32[]{:S(2)}) collective-permute-start(bf16[128,256]{1,0:T(8,128)(2,1)S(1)} %get-tuple-element.22), channel_id=1, source_target_pairs={{0,2},{1,3},{2,0},{3,1},{4,6},{5,7},{6,4},{7,5},{8,10},{9,11},{10,... | collective-permute-start | bytes 196616 | tf_op jit(solution)/shard_map/ppermute | solution.py:543
  33.6 27.4 %copy-start.2 = (s32[1,2048]{1,0:T(1,128)S(1)}, s32[1,2048]{1,0:T(1,128)}, u32[]{:S(2)}) copy-start(s32[1,2048]{1,0:T(1,128)} %param.16) | copy-start | bytes 24580
  33.6 27.4 %all-to-all-start.1 = ((bf16[16,48,512]{2,1,0:T(8,128)(2,1)}), bf16[16,48,512]{2,1,0:T(8,128)(2,1)S(1)}, u32[]{:S(2)}, u32[]{:S(2)}) async-start(bf16[16,48,512]{2,1,0:T(8,128)(2,1)} %serve.1), calls=%async_computation.1 | async-start | bytes 1572864 | tf_op jit(solution)/shard_map/all_to_all | solution.py:21
  38.3 19.7 %collective-permute-start.3 = (bf16[4,128,256]{2,1,0:T(8,128)(2,1)S(1)}, bf16[4,128,256]{2,1,0:T(8,128)(2,1)S(1)}, u32[]{:S(2)}, u32[]{:S(2)}) collective-permute-start(bf16[4,128,256]{2,1,0:T(8,128)(2,1)S(1)} %pad_maximum_fusion.refs_0_), channel_id=1, source_target_pairs={{0,4},{1,5},{2,6},{3,7},{4,8},{5,9},{6,10},{7,11},{8,12},{9,13},{1... | collective-permute-start | bytes 786440 | tf_op jit(solution)/shard_map/ppermute | solution.py:546
  39.6 18.4 %collective-permute-start.4 = (bf16[4,128,256]{2,1,0:T(8,128)(2,1)S(1)}, bf16[4,128,256]{2,1,0:T(8,128)(2,1)S(1)}, u32[]{:S(2)}, u32[]{:S(2)}) collective-permute-start(bf16[4,128,256]{2,1,0:T(8,128)(2,1)S(1)} %pad_maximum_fusion.refs_0_), channel_id=1, source_target_pairs={{0,8},{1,9},{2,10},{3,11},{4,12},{5,13},{6,14},{7,15},{8,0},{9,1},... | collective-permute-start | bytes 786440 | tf_op jit(solution)/shard_map/ppermute | solution.py:546
  42.2 15.8 %collective-permute-start.5 = (bf16[4,128,256]{2,1,0:T(8,128)(2,1)S(1)}, bf16[4,128,256]{2,1,0:T(8,128)(2,1)S(1)}, u32[]{:S(2)}, u32[]{:S(2)}) collective-permute-start(bf16[4,128,256]{2,1,0:T(8,128)(2,1)S(1)} %pad_maximum_fusion.refs_0_), channel_id=1, source_target_pairs={{0,12},{1,13},{2,14},{3,15},{4,0},{5,1},{6,2},{7,3},{8,4},{9,5},{1... | collective-permute-start | bytes 786440 | tf_op jit(solution)/shard_map/ppermute | solution.py:546
  57.9 36.6 %copy-start.3 = (s32[1,512]{1,0:T(1,128)S(1)}, s32[1,512]{1,0:T(1,128)}, u32[]{:S(2)}) copy-start(s32[1,512]{1,0:T(1,128)} %param.23) | copy-start | bytes 6148
  57.9 56.3 %copy-start = (bf16[256,256]{1,0:T(8,128)(2,1)S(1)}, bf16[256,256]{1,0:T(8,128)(2,1)}, u32[]{:S(2)}) copy-start(bf16[256,256]{1,0:T(8,128)(2,1)} %ws_ref.1) | copy-start | bytes 393220
  57.9 56.3 %copy-start.1 = (bf16[256,256]{1,0:T(8,128)(2,1)S(1)}, bf16[256,256]{1,0:T(8,128)(2,1)}, u32[]{:S(2)}) copy-start(bf16[256,256]{1,0:T(8,128)(2,1)} %wn_ref.1) | copy-start | bytes 393220
  73.4 14.7 %all-to-all-start.2 = ((bf16[16,96,128]{2,1,0:T(8,128)(2,1)}), bf16[16,96,128]{2,1,0:T(8,128)(2,1)S(1)}, u32[]{:S(2)}, u32[]{:S(2)}) async-start(bf16[16,96,128]{2,1,0:T(8,128)(2,1)} %first_hop.1.rows_ref), calls=%async_computation.2 | async-start | bytes 786432 | tf_op jit(solution)/shard_map/all_to_all | solution.py:21
  90.5 23.7 %all-to-all-start.3 = ((bf16[16,256,128]{2,1,0:T(8,128)(2,1)}), bf16[16,256,128]{2,1,0:T(8,128)(2,1)S(1)}, u32[]{:S(2)}, u32[]{:S(2)}) async-start(bf16[16,256,128]{2,1,0:T(8,128)(2,1)} %get-tuple-element.31), calls=%async_computation.3 | async-start | bytes 2097152 | tf_op jit(solution)/shard_map/all_to_all | solution.py:21
  146.8 16.1 %all-to-all-start.5 = ((bf16[16,40,256]{2,1,0:T(8,128)(2,1)}), bf16[16,40,256]{2,1,0:T(8,128)(2,1)S(1)}, u32[]{:S(2)}, u32[]{:S(2)}) async-start(bf16[16,40,256]{2,1,0:T(8,128)(2,1)} %broadcast_in_dim.2), calls=%async_computation.5 | async-start | bytes 655360 | tf_op jit(solution)/shard_map/all_to_all | solution.py:21

commit v7 on v6

--- a/solution.py
+++ b/solution.py
@@ -179,7 +179,7 @@
                 ).astype(out_ref.dtype)
         return 0
 
-    lax.fori_loop(0, 8, block, 0, unroll=4)
+    lax.fori_loop(0, 8, block, 0, unroll=8)
 
 
 def all_marks():
@@ -256,7 +256,7 @@
     return pl.pallas_call(
         functools.partial(count_two_kernel, fan),
         grid=(nodes // 256,),
-        out_shape=jax.ShapeDtypeStruct((1, nodes, total), BF),
+        out_shape=jax.ShapeDtypeStruct((1, nodes, total), F8),
         in_specs=[pl.BlockSpec(sent.shape, lambda at: (0, 0, 0))],
         out_specs=pl.BlockSpec((1, 256, total), lambda at: (0, at, 0)),
         scratch_shapes=[
@@ -415,8 +415,8 @@
         out_ref[first:first + 256, :] = jnp.where(row == marks, one, zero)
 
 def second_kernel(scale, negative_total, hidden_ref, rows_ref, self_ref, ends_ref, inv_ref, ws_ref, wn_ref, neigh_hbm,
-                  out_ref, neigh, own, ends, hidden_t, sem):
-    copy = pltpu.make_async_copy(neigh_hbm, neigh, sem)
+                  out_ref, neigh, own, ends, hidden_t, sem, held):
+    copy = pltpu.make_async_copy(neigh_hbm, held, sem)
     copy.start()
     blocks, width, block = hidden_ref.shape
     for at in range(blocks):
@@ -429,6 +429,7 @@
     hidden = hidden_t[...]
     hs = dot(hidden, own[...], NN).astype(BF)
     copy.wait()
+    neigh[...] = held[...].astype(BF)
     hn = (dot(hidden, neigh[...], NT) * inv).astype(BF)
     embed = (dot(ws_ref[...], hs, TN) + dot(wn_ref[...], hn, TN)).astype(BF)
     rows = dot(embed, ends[...], NN).astype(BF)
@@ -484,7 +485,7 @@
         out_shape=jax.ShapeDtypeStruct((groups, 2 * width // groups + 8, width), BF),
         in_specs=[vm] * 7 + [pl.BlockSpec(memory_space=pl.ANY)],
         out_specs=vm,
-        scratch_shapes=[pltpu.VMEM((targets, nodes), BF), pltpu.VMEM((nodes, targets), BF), pltpu.VMEM((targets, many), BF), pltpu.VMEM((width, nodes), BF), pltpu.SemaphoreType.DMA],
+        scratch_shapes=[pltpu.VMEM((targets, nodes), BF), pltpu.VMEM((nodes, targets), BF), pltpu.VMEM((targets, many), BF), pltpu.VMEM((width, nodes), BF), pltpu.SemaphoreType.DMA, pltpu.VMEM((targets, nodes), F8)],
         compiler_params=pltpu.CompilerParams(vmem_limit_bytes=VMEM_LIMIT),
         name="second_layer")(hidden, rows_one, self_two, ends, inv, ws, wn, pick_neigh)
 

time: 167 us -> 166 us (level)
  Pallas kernels: 63.2 us -> 58.8 us
  waiting for transfers between devices: 42.2 us -> 44.2 us
    all_to_all x5, waiting for transfers between devices: 42.2 us -> 44.2 us  [swap(): return lax.all_to_all(value, axis, split_axis=0, concat_axis=0, tiled=True)]
    pallas_call x1, Pallas kernels: 7.07 us -> 5.21 us  [count_two_matrix(): pl.pallas_call(functools.partial(count_two_kernel, fan), grid=(nodes // 2...]
    pallas_call x1, Pallas kernels: 14.6 us -> 12.9 us  [count_one_matrix(): pl.pallas_call(count_one_kernel, grid=(nodes // 256,), out_shape=jax.Shap...]
  transfers between devices with their start and end apart: 11 -> 11, of which waited for: 5 -> 5; matrix products, arithmetic and copies ran while one was open for 1% -> 1% of each run, Pallas kernels for 20% -> 18%
where the time goes in v7:
time: 166 us; the launch traced here: 165 us
  Pallas kernels  58.8 us (35%)
  waiting for transfers between devices  44.2 us (27%)
  starting transfers between devices  36.6 us (22%)
  blocking collectives  15.9 us (10%)
  local copies, waits for them, and re-layouts  6.4 us (4%)
  between operations  2.63 us (2%)
    all_to_all x5, waiting for transfers between devices, swap(): return lax.all_to_all(value, axis, split_axis=0, concat_axis=0, tiled=True)  44.2 us
    all_to_all x5, starting transfers between devices, swap(): return lax.all_to_all(value, axis, split_axis=0, concat_axis=0, tiled=True)  27.4 us
    all_to_all x1, blocking collectives, swap(): return lax.all_to_all(value, axis, split_axis=0, concat_axis=0, tiled=True)  15.9 us
    pallas_call x1, Pallas kernels, second(): pl.pallas_call(functools.partial(second_kernel, scale, negative_total), o...  15 us
    pallas_call x1, Pallas kernels, count_one_matrix(): pl.pallas_call(count_one_kernel, grid=(nodes // 256,), out_shape=jax.Shap...  12.9 us
    pallas_call x1, Pallas kernels, hop(): pl.pallas_call(functools.partial(hop_kernel, chunks), grid=(chunks,), out...  12.4 us
    pallas_call x1, Pallas kernels, serve(): pl.pallas_call(serve_kernel, out_shape=jax.ShapeDtypeStruct((groups, widt...  9.94 us
    pallas_call x1, Pallas kernels, count_two_matrix(): pl.pallas_call(functools.partial(count_two_kernel, fan), grid=(nodes // 2...  5.21 us
  transfers between devices with their start and end apart: 11, of which 5 were waited for; matrix products, arithmetic and copies ran while one was open for 1% of the time, Pallas kernels for 18%

profile of v7, /device:TPU:1, one launch (start us, length us, event | category | flops | bytes accessed | tf_op | source)
XLA Modules:
  0.0 165.4 jit_solution(1948508095731372233)
XLA Ops:
  0.6 1.4 all_to_all.23
  2.0 10.0 %all-to-all-start = ((s32[16,1,512]{2,1,0:T(1,128)}), s32[16,1,512]{2,1,0:T(1,128)S(1)}, u32[]{:S(2)}, u32[]{:S(2)}) async-start(s32[16,1,512]{2,1,0:T(1,128)} %all_to_all.23), calls=%async_computation | async-start | bytes 65536 | tf_op jit(solution)/shard_map/all_to_all | solution.py:21
  12.0 1.3 pack.1
  13.3 6.1 %all-to-all-done = s32[16,1,512]{2,1,0:T(1,128)S(1)} async-done(((s32[16,1,512]{2,1,0:T(1,128)}), s32[16,1,512]{2,1,0:T(1,128)S(1)}, u32[]{:S(2)}, u32[]{:S(2)}) %all-to-all-start) | async-done | bytes 32800 | tf_op jit(solution)/shard_map/all_to_all | solution.py:21
  19.4 2.5 %collective-permute-start.2 = (bf16[128,256]{1,0:T(8,128)(2,1)S(1)}, bf16[128,256]{1,0:T(8,128)(2,1)S(1)}, u32[]{:S(2)}, u32[]{:S(2)}) collective-permute-start(bf16[128,256]{1,0:T(8,128)(2,1)S(1)} %get-tuple-element.22), channel_id=1, source_target_pairs={{0,3},{1,0},{2,1},{3,2},{4,7},{5,4},{6,5},{7,6},{8,11},{9,8},{10,9... | collective-permute-start | bytes 196616 | tf_op jit(solution)/shard_map/ppermute | solution.py:544
  21.9 0.0 collective-permute-start
  21.9 1.7 %collective-permute-start.1 = (bf16[128,256]{1,0:T(8,128)(2,1)S(1)}, bf16[128,256]{1,0:T(8,128)(2,1)S(1)}, u32[]{:S(2)}, u32[]{:S(2)}) collective-permute-start(bf16[128,256]{1,0:T(8,128)(2,1)S(1)} %get-tuple-element.22), channel_id=1, source_target_pairs={{0,2},{1,3},{2,0},{3,1},{4,6},{5,7},{6,4},{7,5},{8,10},{9,11},{10,... | collective-permute-start | bytes 196616 | tf_op jit(solution)/shard_map/ppermute | solution.py:544
  23.6 9.9 %serve.1 = bf16[16,48,512]{2,1,0:T(8,128)(2,1)} custom-call(s32[8192]{0:T(1024)S(1)} %bitcast.28, bf16[48,8192]{1,0:T(8,128)(2,1)S(1)} %get-tuple-element.21.feat_ref), custom_call_target="tpu_custom_call" | custom-call | tf_op jit(solution)/shard_map/serve/pallas_call | solution.py:76
  33.6 0.0 collective-permute-done.2
  33.6 0.0 collective-permute-done
  33.6 0.0 collective-permute-done.1
  33.6 0.0 copy-start.3
  33.6 4.7 %all-to-all-start.1 = ((bf16[16,48,512]{2,1,0:T(8,128)(2,1)}), bf16[16,48,512]{2,1,0:T(8,128)(2,1)S(1)}, u32[]{:S(2)}, u32[]{:S(2)}) async-start(bf16[16,48,512]{2,1,0:T(8,128)(2,1)} %serve.1), calls=%async_computation.1 | async-start | bytes 1572864 | tf_op jit(solution)/shard_map/all_to_all | solution.py:21
  38.3 1.3 collective-permute-start.3
  39.6 2.6 %collective-permute-start.4 = (bf16[4,128,256]{2,1,0:T(8,128)(2,1)S(1)}, bf16[4,128,256]{2,1,0:T(8,128)(2,1)S(1)}, u32[]{:S(2)}, u32[]{:S(2)}) collective-permute-start(bf16[4,128,256]{2,1,0:T(8,128)(2,1)S(1)} %pad_maximum_fusion.refs_0_), channel_id=1, source_target_pairs={{0,8},{1,9},{2,10},{3,11},{4,12},{5,13},{6,14},{7,15},{8,0},{9,1},... | collective-permute-start | bytes 786440 | tf_op jit(solution)/shard_map/ppermute | solution.py:547
  42.2 1.1 collective-permute-start.5
  43.3 12.9 %count_one.1.counts_ref = f8e4m3fn[8,2048,1024]{2,1,0:T(32,128)(4,1)} custom-call(s32[16,2048]{1,0:T(8,128)} %bitcast.42, s32[1,2048]{1,0:T(1,128)} %live_from.1), custom_call_target="tpu_custom_call" | custom-call | flops 8589934592 | bytes 16777216 | tf_op jit(solution)/shard_map/count_one/pallas_call | solution.py:217
  56.2 0.0 copy-start.4
  56.2 0.0 copy-start.1
  56.2 0.0 copy-start.2
  56.2 0.0 collective-permute-done.3.refs_1_
  56.2 0.0 collective-permute-done.4.refs_2_
  56.2 0.0 collective-permute-done.5.refs_3_
  56.3 4.7 %all-to-all-done.1.front_ref = bf16[16,48,512]{2,1,0:T(8,128)(2,1)S(1)} async-done(((bf16[16,48,512]{2,1,0:T(8,128)(2,1)}), bf16[16,48,512]{2,1,0:T(8,128)(2,1)S(1)}, u32[]{:S(2)}, u32[]{:S(2)}) %all-to-all-start.1) | async-done | bytes 786464 | tf_op jit(solution)/shard_map/all_to_all | solution.py:21
  61.0 0.0 copy-done.3
  61.0 12.4 %first_hop.1.rows_ref = bf16[16,96,128]{2,1,0:T(8,128)(2,1)} custom-call(s32[2048]{0:T(1024)S(1)} %bitcast.30, f8e4m3fn[8,2048,1024]{2,1,0:T(32,128)(4,1)} %count_one.1.counts_ref, bf16[16,48,512]{2,1,0:T(8,128)(2,1)S(1)} %all-to-all-done.1.front_ref), custom_call_target="tpu_custom_call" | custom-call | flops 4294967296 | bytes 16777216 | tf_op jit(solution)/shard_map/first_hop/pallas_call | solution.py:346
  73.4 5.5 %all-to-all-start.2 = ((bf16[16,96,128]{2,1,0:T(8,128)(2,1)}), bf16[16,96,128]{2,1,0:T(8,128)(2,1)S(1)}, u32[]{:S(2)}, u32[]{:S(2)}) async-start(bf16[16,96,128]{2,1,0:T(8,128)(2,1)} %first_hop.1.rows_ref), calls=%async_computation.2 | async-start | bytes 786432 | tf_op jit(solution)/shard_map/all_to_all | solution.py:21
  79.0 0.1 pad_add_fusion.me_ref
  79.1 9.1 %all-to-all-done.2.mine_ref = bf16[16,96,128]{2,1,0:T(8,128)(2,1)S(1)} async-done(((bf16[16,96,128]{2,1,0:T(8,128)(2,1)}), bf16[16,96,128]{2,1,0:T(8,128)(2,1)S(1)}, u32[]{:S(2)}, u32[]{:S(2)}) %all-to-all-start.2) | async-done | bytes 393248 | tf_op jit(solution)/shard_map/all_to_all | solution.py:21
  88.2 2.0 %first_layer.1 = (bf16[16,256,128]{2,1,0:T(8,128)(2,1)}, f32[16,32,256]{2,1,0:T(8,128)S(1)}) custom-call(s32[2]{0:T(128)S(1)} %pad_add_fusion.me_ref, bf16[16,96,128]{2,1,0:T(8,128)(2,1)S(1)} %all-to-all-done.2.mine_ref, bf16[4,128,256]{2,1,0:T(8,128)(2,1)S(1)} %pad_maximum_fusion.refs_0_, bf16[4,128,256]{2,1,0:T(8,128)(2,1)S(1)} %collective-permute-done.3.refs_1_, ...), custom_call_target="tpu_custom_call" | custom-call | tf_op jit(solution)/shard_map/first_layer/pallas_call | solution.py:396
  90.2 0.1 copy.27
  90.3 0.1 div.45.inv_ref
  90.4 0.1 copy.25
  90.5 0.1 reshape.198.self_ref
  90.6 3.8 %all-to-all-start.3 = ((bf16[16,256,128]{2,1,0:T(8,128)(2,1)}), bf16[16,256,128]{2,1,0:T(8,128)(2,1)S(1)}, u32[]{:S(2)}, u32[]{:S(2)}) async-start(bf16[16,256,128]{2,1,0:T(8,128)(2,1)} %get-tuple-element.31), calls=%async_computation.3 | async-start | bytes 2097152 | tf_op jit(solution)/shard_map/all_to_all | solution.py:21
  94.4 0.1 concatenate.31
  94.5 0.0 copy-done.4
  94.5 5.2 %count_two.1 = f8e4m3fn[1,1536,2048]{2,1,0:T(32,128)(4,1)S(1)} custom-call(f32[16,32,256]{2,1,0:T(8,128)S(1)} %get-tuple-element.32.sent_ref), custom_call_target="tpu_custom_call" | custom-call | flops 1610612736 | bytes 6291456 | tf_op jit(solution)/shard_map/count_two/pallas_call | solution.py:256
  99.8 0.0 copy-start
  99.8 1.6 copy-done
  101.4 0.1 fusion.2.ends_ref
  101.5 12.8 %all-to-all-done.3.hidden_ref = bf16[16,256,128]{2,1,0:T(8,128)(2,1)S(1)} async-done(((bf16[16,256,128]{2,1,0:T(8,128)(2,1)}), bf16[16,256,128]{2,1,0:T(8,128)(2,1)S(1)}, u32[]{:S(2)}, u32[]{:S(2)}) %all-to-all-start.3) | async-done | bytes 1048608 | tf_op jit(solution)/shard_map/all_to_all | solution.py:21
  114.3 0.0 copy-done.1
  114.3 0.0 copy-done.2
  114.3 15.0 %second_layer.1 = bf16[16,40,256]{2,1,0:T(8,128)(2,1)S(1)} custom-call(bf16[16,256,128]{2,1,0:T(8,128)(2,1)S(1)} %all-to-all-done.3.hidden_ref, bf16[16,96,128]{2,1,0:T(8,128)(2,1)} %first_hop.1.rows_ref, f32[1,1536]{1,0:T(1,128)S(1)} %reshape.198.self_ref, f32[1,1536]{1,0:T(1,128)S(1)} %fusion.2.ends_ref, f32[1,1536]{1,0:T(1,128)S(1)} %div.45.inv_ref, ...), custom_call_target="tpu_custom_call" | custom-call | tf_op jit(solution)/shard_map/second_layer/pallas_call | solution.py:484
  129.3 15.9 %all_to_all.37 = bf16[16,40,256]{2,1,0:T(8,128)(2,1)S(1)} all-to-all(bf16[16,40,256]{2,1,0:T(8,128)(2,1)S(1)} %second_layer.1), channel_id=1, replica_groups=mesh['graph'=16,'feat'=16] {'graph'}, dimensions={0} | all-to-all | bytes 655360 | tf_op jit(solution)/shard_map/all_to_all | solution.py:21
  145.2 0.1 convert_reduce_fusion
  145.2 0.8 broadcast_in_dim.2
  146.0 3.4 %all-to-all-start.5 = ((bf16[16,40,256]{2,1,0:T(8,128)(2,1)}), bf16[16,40,256]{2,1,0:T(8,128)(2,1)S(1)}, u32[]{:S(2)}, u32[]{:S(2)}) async-start(bf16[16,40,256]{2,1,0:T(8,128)(2,1)} %broadcast_in_dim.2), calls=%async_computation.5 | async-start | bytes 655360 | tf_op jit(solution)/shard_map/all_to_all | solution.py:21
  149.4 0.6 slice_reduce_fusion
  150.7 11.4 %all-to-all-done.5 = bf16[16,40,256]{2,1,0:T(8,128)(2,1)S(1)} async-done(((bf16[16,40,256]{2,1,0:T(8,128)(2,1)}), bf16[16,40,256]{2,1,0:T(8,128)(2,1)S(1)}, u32[]{:S(2)}, u32[]{:S(2)}) %all-to-all-start.5) | async-done | bytes 327712 | tf_op jit(solution)/shard_map/all_to_all | solution.py:21
  162.1 0.6 slice.57
  162.8 0.6 slice.59
  163.4 0.8 fusion.3
  (10 shorter events, 0.1 us)
Async XLA Ops:
  2.0 17.4 %all-to-all-start = ((s32[16,1,512]{2,1,0:T(1,128)}), s32[16,1,512]{2,1,0:T(1,128)S(1)}, u32[]{:S(2)}, u32[]{:S(2)}) async-start(s32[16,1,512]{2,1,0:T(1,128)} %all_to_all.23), calls=%async_computation | async-start | bytes 65536 | tf_op jit(solution)/shard_map/all_to_all | solution.py:21
  19.4 14.2 %collective-permute-start.2 = (bf16[128,256]{1,0:T(8,128)(2,1)S(1)}, bf16[128,256]{1,0:T(8,128)(2,1)S(1)}, u32[]{:S(2)}, u32[]{:S(2)}) collective-permute-start(bf16[128,256]{1,0:T(8,128)(2,1)S(1)} %get-tuple-element.22), channel_id=1, source_target_pairs={{0,3},{1,0},{2,1},{3,2},{4,7},{5,4},{6,5},{7,6},{8,11},{9,8},{10,9... | collective-permute-start | bytes 196616 | tf_op jit(solution)/shard_map/ppermute | solution.py:544
  21.9 11.7 %collective-permute-start = (bf16[128,256]{1,0:T(8,128)(2,1)S(1)}, bf16[128,256]{1,0:T(8,128)(2,1)S(1)}, u32[]{:S(2)}, u32[]{:S(2)}) collective-permute-start(bf16[128,256]{1,0:T(8,128)(2,1)S(1)} %get-tuple-element.22), channel_id=1, source_target_pairs={{0,1},{1,2},{2,3},{3,0},{4,5},{5,6},{6,7},{7,4},{8,9},{9,10},{10,1... | collective-permute-start | bytes 196616 | tf_op jit(solution)/shard_map/ppermute | solution.py:544
  21.9 11.7 %collective-permute-start.1 = (bf16[128,256]{1,0:T(8,128)(2,1)S(1)}, bf16[128,256]{1,0:T(8,128)(2,1)S(1)}, u32[]{:S(2)}, u32[]{:S(2)}) collective-permute-start(bf16[128,256]{1,0:T(8,128)(2,1)S(1)} %get-tuple-element.22), channel_id=1, source_target_pairs={{0,2},{1,3},{2,0},{3,1},{4,6},{5,7},{6,4},{7,5},{8,10},{9,11},{10,... | collective-permute-start | bytes 196616 | tf_op jit(solution)/shard_map/ppermute | solution.py:544
  33.6 27.4 %copy-start.3 = (s32[1,2048]{1,0:T(1,128)S(1)}, s32[1,2048]{1,0:T(1,128)}, u32[]{:S(2)}) copy-start(s32[1,2048]{1,0:T(1,128)} %param.16) | copy-start | bytes 24580
  33.6 27.4 %all-to-all-start.1 = ((bf16[16,48,512]{2,1,0:T(8,128)(2,1)}), bf16[16,48,512]{2,1,0:T(8,128)(2,1)S(1)}, u32[]{:S(2)}, u32[]{:S(2)}) async-start(bf16[16,48,512]{2,1,0:T(8,128)(2,1)} %serve.1), calls=%async_computation.1 | async-start | bytes 1572864 | tf_op jit(solution)/shard_map/all_to_all | solution.py:21
  38.3 17.9 %collective-permute-start.3 = (bf16[4,128,256]{2,1,0:T(8,128)(2,1)S(1)}, bf16[4,128,256]{2,1,0:T(8,128)(2,1)S(1)}, u32[]{:S(2)}, u32[]{:S(2)}) collective-permute-start(bf16[4,128,256]{2,1,0:T(8,128)(2,1)S(1)} %pad_maximum_fusion.refs_0_), channel_id=1, source_target_pairs={{0,4},{1,5},{2,6},{3,7},{4,8},{5,9},{6,10},{7,11},{8,12},{9,13},{1... | collective-permute-start | bytes 786440 | tf_op jit(solution)/shard_map/ppermute | solution.py:547
  39.6 16.7 %collective-permute-start.4 = (bf16[4,128,256]{2,1,0:T(8,128)(2,1)S(1)}, bf16[4,128,256]{2,1,0:T(8,128)(2,1)S(1)}, u32[]{:S(2)}, u32[]{:S(2)}) collective-permute-start(bf16[4,128,256]{2,1,0:T(8,128)(2,1)S(1)} %pad_maximum_fusion.refs_0_), channel_id=1, source_target_pairs={{0,8},{1,9},{2,10},{3,11},{4,12},{5,13},{6,14},{7,15},{8,0},{9,1},... | collective-permute-start | bytes 786440 | tf_op jit(solution)/shard_map/ppermute | solution.py:547
  42.2 14.0 %collective-permute-start.5 = (bf16[4,128,256]{2,1,0:T(8,128)(2,1)S(1)}, bf16[4,128,256]{2,1,0:T(8,128)(2,1)S(1)}, u32[]{:S(2)}, u32[]{:S(2)}) collective-permute-start(bf16[4,128,256]{2,1,0:T(8,128)(2,1)S(1)} %pad_maximum_fusion.refs_0_), channel_id=1, source_target_pairs={{0,12},{1,13},{2,14},{3,15},{4,0},{5,1},{6,2},{7,3},{8,4},{9,5},{1... | collective-permute-start | bytes 786440 | tf_op jit(solution)/shard_map/ppermute | solution.py:547
  56.2 38.3 %copy-start.4 = (s32[1,512]{1,0:T(1,128)S(1)}, s32[1,512]{1,0:T(1,128)}, u32[]{:S(2)}) copy-start(s32[1,512]{1,0:T(1,128)} %param.23) | copy-start | bytes 6148
  56.2 58.1 %copy-start.1 = (bf16[256,256]{1,0:T(8,128)(2,1)S(1)}, bf16[256,256]{1,0:T(8,128)(2,1)}, u32[]{:S(2)}) copy-start(bf16[256,256]{1,0:T(8,128)(2,1)} %ws_ref.1) | copy-start | bytes 393220
  56.2 58.1 %copy-start.2 = (bf16[256,256]{1,0:T(8,128)(2,1)S(1)}, bf16[256,256]{1,0:T(8,128)(2,1)}, u32[]{:S(2)}) copy-start(bf16[256,256]{1,0:T(8,128)(2,1)} %wn_ref.1) | copy-start | bytes 393220
  73.4 14.7 %all-to-all-start.2 = ((bf16[16,96,128]{2,1,0:T(8,128)(2,1)}), bf16[16,96,128]{2,1,0:T(8,128)(2,1)S(1)}, u32[]{:S(2)}, u32[]{:S(2)}) async-start(bf16[16,96,128]{2,1,0:T(8,128)(2,1)} %first_hop.1.rows_ref), calls=%async_computation.2 | async-start | bytes 786432 | tf_op jit(solution)/shard_map/all_to_all | solution.py:21
  90.6 23.7 %all-to-all-start.3 = ((bf16[16,256,128]{2,1,0:T(8,128)(2,1)}), bf16[16,256,128]{2,1,0:T(8,128)(2,1)S(1)}, u32[]{:S(2)}, u32[]{:S(2)}) async-start(bf16[16,256,128]{2,1,0:T(8,128)(2,1)} %get-tuple-element.31), calls=%async_computation.3 | async-start | bytes 2097152 | tf_op jit(solution)/shard_map/all_to_all | solution.py:21
  99.8 1.7 %copy-start = (f8e4m3fn[1,1536,2048]{2,1,0:T(32,128)(4,1)}, f8e4m3fn[1,1536,2048]{2,1,0:T(32,128)(4,1)S(1)}, u32[]{:S(2)}) copy-start(f8e4m3fn[1,1536,2048]{2,1,0:T(32,128)(4,1)S(1)} %count_two.1) | copy-start | bytes 9437188
  146.0 16.1 %all-to-all-start.5 = ((bf16[16,40,256]{2,1,0:T(8,128)(2,1)}), bf16[16,40,256]{2,1,0:T(8,128)(2,1)S(1)}, u32[]{:S(2)}, u32[]{:S(2)}) async-start(bf16[16,40,256]{2,1,0:T(8,128)(2,1)} %broadcast_in_dim.2), calls=%async_computation.5 | async-start | bytes 655360 | tf_op jit(solution)/shard_map/all_to_all | solution.py:21

commit v8 on v7

--- a/solution.py
+++ b/solution.py
@@ -186,7 +186,7 @@
     return lax.broadcasted_iota(jnp.int32, (256, 256), 0).astype(F32).astype(BF)
 
 
-def count_one_kernel(ids_from, live_from, out_ref, marks, keys, lows, ids_ref, live_ref, sems):
+def count_one_kernel(ids_from, live_from, out_ref, done_ref, marks, keys, lows, ids_ref, live_ref, sems):
     fan = ids_ref.shape[0]
 
     @pl.when(pl.program_id(0) == 0)
@@ -198,6 +198,7 @@
         marks[...] = all_marks()
         first.wait()
         other.wait()
+        done_ref[...] = jnp.zeros_like(done_ref)
         slots = lax.broadcasted_iota(jnp.int32, (fan, 128), 0)
         high = []
         low = []
@@ -217,9 +218,15 @@
     return pl.pallas_call(
         count_one_kernel,
         grid=(nodes // 256,),
-        out_shape=jax.ShapeDtypeStruct((total // chunk, nodes, chunk), F8),
+        out_shape=[
+            jax.ShapeDtypeStruct((total // chunk, nodes, chunk), F8),
+            jax.ShapeDtypeStruct((8, 128), F32),
+        ],
         in_specs=[pl.BlockSpec(memory_space=pl.ANY)] * 2,
-        out_specs=pl.BlockSpec((total // chunk, 256, chunk), lambda at: (0, at, 0)),
+        out_specs=[
+            pl.BlockSpec((total // chunk, 256, chunk), lambda at: (0, at, 0)),
+            pl.BlockSpec((8, 128), lambda at: (0, 0)),
+        ],
         scratch_shapes=[
             pltpu.VMEM((256, 256), BF),
             pltpu.VMEM((128, 256), F32),
@@ -540,12 +547,13 @@
     across = [
         [(at, (at + far * side) % feats) for at in range(feats)] for far in range(1, side)
     ]
-    asked, early = lax.optimization_barrier((asked, early))
-    early = jnp.stack([early] + [lax.ppermute(early, "feat", pairs) for pairs in along])
     served = serve(features_t, asked.reshape(-1), graphs, cap)
     one_ids, served, early = lax.optimization_barrier((neigh_one_ids[0], served, early))
+    early = jnp.stack([early] + [lax.ppermute(early, "feat", pairs) for pairs in along])
+    one_counts, done = count_one_matrix(one_ids, count_one, front, 2 * cap)
+    early, done = lax.optimization_barrier((early, done))
+    me = me + done[0, :2].astype(jnp.int32)
     early = [early] + [lax.ppermute(early, "feat", pairs) for pairs in across]
-    one_counts = count_one_matrix(one_ids, count_one, front, 2 * cap)
     frontier = swap(served, "graph")
     frontier, early = lax.optimization_barrier((frontier, early))
     rows_one = hop(frontier, one_counts, self_one_ids[0], feats)

time: 166 us -> 173 us (1.042)
  blocking collectives: 15.9 us -> 22.8 us
  starting transfers between devices: 36.6 us -> 32.2 us
  waiting for transfers between devices: 44.2 us -> 48.6 us
    ppermute x3, waiting for transfers between devices: 0.01 us -> 14.3 us  [local(): early = [early] + [lax.ppermute(early, 'feat', pairs) for pairs in across]]
    all_to_all x5, waiting for transfers between devices: 44.2 us -> 34.3 us  [swap(): return lax.all_to_all(value, axis, split_axis=0, concat_axis=0, tiled=True)]
    all_to_all x1, blocking collectives: 15.9 us -> 22.8 us  [swap(): return lax.all_to_all(value, axis, split_axis=0, concat_axis=0, tiled=True)]
    all_to_all x5, starting transfers between devices: 27.4 us -> 24.7 us  [swap(): return lax.all_to_all(value, axis, split_axis=0, concat_axis=0, tiled=True)]
  transfers between devices with their start and end apart: 11 -> 11, of which waited for: 5 -> 7; matrix products, arithmetic and copies ran while one was open for 1% -> 1% of each run, Pallas kernels for 18% -> 11%
where the time goes in v8:
time: 173 us; the launch traced here: 172 us
  Pallas kernels  58.8 us (34%)
  waiting for transfers between devices  48.6 us (28%)
  starting transfers between devices  32.2 us (19%)
  blocking collectives  22.8 us (13%)
  local copies, waits for them, and re-layouts  6.38 us (4%)
  between operations  2.63 us (2%)
    all_to_all x5, waiting for transfers between devices, swap(): return lax.all_to_all(value, axis, split_axis=0, concat_axis=0, tiled=True)  34.3 us
    all_to_all x5, starting transfers between devices, swap(): return lax.all_to_all(value, axis, split_axis=0, concat_axis=0, tiled=True)  24.7 us
    all_to_all x1, blocking collectives, swap(): return lax.all_to_all(value, axis, split_axis=0, concat_axis=0, tiled=True)  22.8 us
    pallas_call x1, Pallas kernels, second(): pl.pallas_call(functools.partial(second_kernel, scale, negative_total), o...  15 us
    ppermute x3, waiting for transfers between devices, local(): early = [early] + [lax.ppermute(early, 'feat', pairs) for pairs in across]  14.3 us
    pallas_call x1, Pallas kernels, count_one_matrix(): pl.pallas_call(count_one_kernel, grid=(nodes // 256,), out_shape=[jax.Sha...  12.9 us
    pallas_call x1, Pallas kernels, hop(): pl.pallas_call(functools.partial(hop_kernel, chunks), grid=(chunks,), out...  12.4 us
    pallas_call x1, Pallas kernels, serve(): pl.pallas_call(serve_kernel, out_shape=jax.ShapeDtypeStruct((groups, widt...  9.93 us
  transfers between devices with their start and end apart: 11, of which 7 were waited for; matrix products, arithmetic and copies ran while one was open for 1% of the time, Pallas kernels for 11%

profile of v8, /device:TPU:1, one launch (start us, length us, event | category | flops | bytes accessed | tf_op | source)
XLA Modules:
  0.0 172.3 jit_solution(2559079533713348441)
XLA Ops:
  0.6 1.4 all_to_all.21
  2.0 10.0 %all-to-all-start = ((s32[16,1,512]{2,1,0:T(1,128)}), s32[16,1,512]{2,1,0:T(1,128)S(1)}, u32[]{:S(2)}, u32[]{:S(2)}) async-start(s32[16,1,512]{2,1,0:T(1,128)} %all_to_all.21), calls=%async_computation | async-start | bytes 65536 | tf_op jit(solution)/shard_map/all_to_all | solution.py:21
  12.0 1.3 pack.1
  13.3 6.1 %all-to-all-done = s32[16,1,512]{2,1,0:T(1,128)S(1)} async-done(((s32[16,1,512]{2,1,0:T(1,128)}), s32[16,1,512]{2,1,0:T(1,128)S(1)}, u32[]{:S(2)}, u32[]{:S(2)}) %all-to-all-start) | async-done | bytes 32800 | tf_op jit(solution)/shard_map/all_to_all | solution.py:21
  19.4 9.9 %serve.1 = bf16[16,48,512]{2,1,0:T(8,128)(2,1)} custom-call(s32[8192]{0:T(1024)S(1)} %bitcast.26, bf16[48,8192]{1,0:T(8,128)(2,1)S(1)} %get-tuple-element.21.feat_ref), custom_call_target="tpu_custom_call" | custom-call | tf_op jit(solution)/shard_map/serve/pallas_call | solution.py:76
  29.3 0.0 copy-start.3
  29.3 3.9 %all-to-all-start.1 = ((bf16[16,48,512]{2,1,0:T(8,128)(2,1)}), bf16[16,48,512]{2,1,0:T(8,128)(2,1)S(1)}, u32[]{:S(2)}, u32[]{:S(2)}) async-start(bf16[16,48,512]{2,1,0:T(8,128)(2,1)} %serve.1), calls=%async_computation.1 | async-start | bytes 1572864 | tf_op jit(solution)/shard_map/all_to_all | solution.py:21
  33.3 2.5 %collective-permute-start.2 = (bf16[128,256]{1,0:T(8,128)(2,1)S(1)}, bf16[128,256]{1,0:T(8,128)(2,1)S(1)}, u32[]{:S(2)}, u32[]{:S(2)}) collective-permute-start(bf16[128,256]{1,0:T(8,128)(2,1)S(1)} %get-tuple-element.23), channel_id=1, source_target_pairs={{0,3},{1,0},{2,1},{3,2},{4,7},{5,4},{6,5},{7,6},{8,11},{9,8},{10,9... | collective-permute-start | bytes 196616 | tf_op jit(solution)/shard_map/ppermute | solution.py:552
  35.7 0.5 collective-permute-start.1
  36.3 0.6 collective-permute-start
  36.9 12.9 %count_one.1 = (f8e4m3fn[8,2048,1024]{2,1,0:T(32,128)(4,1)}, f32[8,128]{1,0:T(8,128)S(1)}) custom-call(s32[16,2048]{1,0:T(8,128)} %bitcast.39, s32[1,2048]{1,0:T(1,128)} %live_from.1), custom_call_target="tpu_custom_call" | custom-call | flops 8589934592 | bytes 16777216 | tf_op jit(solution)/shard_map/count_one/pallas_call | solution.py:218
  49.8 0.0 copy-start.4
  49.8 0.0 copy-start.1
  49.8 0.0 copy-start.2
  49.8 0.0 collective-permute-done.2
  49.8 0.0 collective-permute-done.1
  49.8 0.0 collective-permute-done
  49.9 2.8 %collective-permute-start.5 = (bf16[4,128,256]{2,1,0:T(8,128)(2,1)S(1)}, bf16[4,128,256]{2,1,0:T(8,128)(2,1)S(1)}, u32[]{:S(2)}, u32[]{:S(2)}) collective-permute-start(bf16[4,128,256]{2,1,0:T(8,128)(2,1)S(1)} %pad_maximum_fusion.refs_0_), channel_id=1, source_target_pairs={{0,12},{1,13},{2,14},{3,15},{4,0},{5,1},{6,2},{7,3},{8,4},{9,5},{1... | collective-permute-start | bytes 786440 | tf_op jit(solution)/shard_map/ppermute | solution.py:556
  52.7 0.3 collective-permute-start.4
  53.1 0.7 collective-permute-start.3
  53.8 4.5 %collective-permute-done.5.refs_3_ = bf16[4,128,256]{2,1,0:T(8,128)(2,1)S(1)} collective-permute-done((bf16[4,128,256]{2,1,0:T(8,128)(2,1)S(1)}, bf16[4,128,256]{2,1,0:T(8,128)(2,1)S(1)}, u32[]{:S(2)}, u32[]{:S(2)}) %collective-permute-start.5) | collective-permute-done | bytes 262176 | tf_op jit(solution)/shard_map/ppermute | solution.py:556
  58.2 2.4 %collective-permute-done.4.refs_2_ = bf16[4,128,256]{2,1,0:T(8,128)(2,1)S(1)} collective-permute-done((bf16[4,128,256]{2,1,0:T(8,128)(2,1)S(1)}, bf16[4,128,256]{2,1,0:T(8,128)(2,1)S(1)}, u32[]{:S(2)}, u32[]{:S(2)}) %collective-permute-start.4) | collective-permute-done | bytes 262176 | tf_op jit(solution)/shard_map/ppermute | solution.py:556
  60.7 7.4 %collective-permute-done.3.refs_1_ = bf16[4,128,256]{2,1,0:T(8,128)(2,1)S(1)} collective-permute-done((bf16[4,128,256]{2,1,0:T(8,128)(2,1)S(1)}, bf16[4,128,256]{2,1,0:T(8,128)(2,1)S(1)}, u32[]{:S(2)}, u32[]{:S(2)}) %collective-permute-start.3) | collective-permute-done | bytes 262176 | tf_op jit(solution)/shard_map/ppermute | solution.py:556
  68.1 0.0 all-to-all-done.1.front_ref
  68.1 0.0 copy-done.3
  68.1 12.4 %first_hop.1.rows_ref = bf16[16,96,128]{2,1,0:T(8,128)(2,1)} custom-call(s32[2048]{0:T(1024)S(1)} %bitcast.28, f8e4m3fn[8,2048,1024]{2,1,0:T(32,128)(4,1)} %get-tuple-element.27.counts_ref, bf16[16,48,512]{2,1,0:T(8,128)(2,1)S(1)} %all-to-all-done.1.front_ref), custom_call_target="tpu_custom_call" | custom-call | flops 4294967296 | bytes 16777216 | tf_op jit(solution)/shard_map/first_hop/pallas_call | solution.py:353
  80.5 3.6 %all-to-all-start.2 = ((bf16[16,96,128]{2,1,0:T(8,128)(2,1)}), bf16[16,96,128]{2,1,0:T(8,128)(2,1)S(1)}, u32[]{:S(2)}, u32[]{:S(2)}) async-start(bf16[16,96,128]{2,1,0:T(8,128)(2,1)} %first_hop.1.rows_ref), calls=%async_computation.2 | async-start | bytes 786432 | tf_op jit(solution)/shard_map/all_to_all | solution.py:21
  84.1 0.1 add_add_fusion.me_ref
  84.2 9.2 %all-to-all-done.2.mine_ref = bf16[16,96,128]{2,1,0:T(8,128)(2,1)S(1)} async-done(((bf16[16,96,128]{2,1,0:T(8,128)(2,1)}), bf16[16,96,128]{2,1,0:T(8,128)(2,1)S(1)}, u32[]{:S(2)}, u32[]{:S(2)}) %all-to-all-start.2) | async-done | bytes 393248 | tf_op jit(solution)/shard_map/all_to_all | solution.py:21
  93.4 2.0 %first_layer.1 = (bf16[16,256,128]{2,1,0:T(8,128)(2,1)}, f32[16,32,256]{2,1,0:T(8,128)S(1)}) custom-call(s32[2]{0:T(128)S(1)} %add_add_fusion.me_ref, bf16[16,96,128]{2,1,0:T(8,128)(2,1)S(1)} %all-to-all-done.2.mine_ref, bf16[4,128,256]{2,1,0:T(8,128)(2,1)S(1)} %pad_maximum_fusion.refs_0_, bf16[4,128,256]{2,1,0:T(8,128)(2,1)S(1)} %collective-permute-done.3.refs_1_, ...), custom_call_target="tpu_custom_call" | custom-call | tf_op jit(solution)/shard_map/first_layer/pallas_call | solution.py:403
  95.4 3.8 %all-to-all-start.3 = ((bf16[16,256,128]{2,1,0:T(8,128)(2,1)}), bf16[16,256,128]{2,1,0:T(8,128)(2,1)S(1)}, u32[]{:S(2)}, u32[]{:S(2)}) async-start(bf16[16,256,128]{2,1,0:T(8,128)(2,1)} %get-tuple-element.35), calls=%async_computation.3 | async-start | bytes 2097152 | tf_op jit(solution)/shard_map/all_to_all | solution.py:21
  99.3 0.1 concatenate.31
  99.4 0.1 copy.25
  99.4 0.1 reshape.200.self_ref
  99.5 0.1 copy.27
  99.6 0.1 div.45.inv_ref
  99.7 0.0 copy-done.4
  99.8 5.2 %count_two.1 = f8e4m3fn[1,1536,2048]{2,1,0:T(32,128)(4,1)S(1)} custom-call(f32[16,32,256]{2,1,0:T(8,128)S(1)} %get-tuple-element.36.sent_ref), custom_call_target="tpu_custom_call" | custom-call | flops 1610612736 | bytes 6291456 | tf_op jit(solution)/shard_map/count_two/pallas_call | solution.py:263
  105.0 0.0 copy-start
  105.0 1.6 copy-done
  106.6 0.1 fusion.2.ends_ref
  106.7 7.6 %all-to-all-done.3.hidden_ref = bf16[16,256,128]{2,1,0:T(8,128)(2,1)S(1)} async-done(((bf16[16,256,128]{2,1,0:T(8,128)(2,1)}), bf16[16,256,128]{2,1,0:T(8,128)(2,1)S(1)}, u32[]{:S(2)}, u32[]{:S(2)}) %all-to-all-start.3) | async-done | bytes 1048608 | tf_op jit(solution)/shard_map/all_to_all | solution.py:21
  114.3 0.0 copy-done.1
  114.3 0.0 copy-done.2
  114.3 15.0 %second_layer.1 = bf16[16,40,256]{2,1,0:T(8,128)(2,1)S(1)} custom-call(bf16[16,256,128]{2,1,0:T(8,128)(2,1)S(1)} %all-to-all-done.3.hidden_ref, bf16[16,96,128]{2,1,0:T(8,128)(2,1)} %first_hop.1.rows_ref, f32[1,1536]{1,0:T(1,128)S(1)} %reshape.200.self_ref, f32[1,1536]{1,0:T(1,128)S(1)} %fusion.2.ends_ref, f32[1,1536]{1,0:T(1,128)S(1)} %div.45.inv_ref, ...), custom_call_target="tpu_custom_call" | custom-call | tf_op jit(solution)/shard_map/second_layer/pallas_call | solution.py:491
  129.3 22.8 %all_to_all.34 = bf16[16,40,256]{2,1,0:T(8,128)(2,1)S(1)} all-to-all(bf16[16,40,256]{2,1,0:T(8,128)(2,1)S(1)} %second_layer.1), channel_id=1, replica_groups=mesh['graph'=16,'feat'=16] {'graph'}, dimensions={0} | all-to-all | bytes 655360 | tf_op jit(solution)/shard_map/all_to_all | solution.py:21
  152.1 0.1 convert_reduce_fusion
  152.2 0.8 broadcast_in_dim.2
  153.0 3.4 %all-to-all-start.5 = ((bf16[16,40,256]{2,1,0:T(8,128)(2,1)}), bf16[16,40,256]{2,1,0:T(8,128)(2,1)S(1)}, u32[]{:S(2)}, u32[]{:S(2)}) async-start(bf16[16,40,256]{2,1,0:T(8,128)(2,1)} %broadcast_in_dim.2), calls=%async_computation.5 | async-start | bytes 655360 | tf_op jit(solution)/shard_map/all_to_all | solution.py:21
  156.4 0.6 slice_reduce_fusion
  157.7 11.4 %all-to-all-done.5 = bf16[16,40,256]{2,1,0:T(8,128)(2,1)S(1)} async-done(((bf16[16,40,256]{2,1,0:T(8,128)(2,1)}), bf16[16,40,256]{2,1,0:T(8,128)(2,1)S(1)}, u32[]{:S(2)}, u32[]{:S(2)}) %all-to-all-start.5) | async-done | bytes 327712 | tf_op jit(solution)/shard_map/all_to_all | solution.py:21
  169.1 0.6 slice.63
  169.7 0.6 slice.61
  170.3 0.8 fusion.3
  (8 shorter events, 0.1 us)
Async XLA Ops:
  2.0 17.4 %all-to-all-start = ((s32[16,1,512]{2,1,0:T(1,128)}), s32[16,1,512]{2,1,0:T(1,128)S(1)}, u32[]{:S(2)}, u32[]{:S(2)}) async-start(s32[16,1,512]{2,1,0:T(1,128)} %all_to_all.21), calls=%async_computation | async-start | bytes 65536 | tf_op jit(solution)/shard_map/all_to_all | solution.py:21
  29.3 38.7 %copy-start.3 = (s32[1,2048]{1,0:T(1,128)S(1)}, s32[1,2048]{1,0:T(1,128)}, u32[]{:S(2)}) copy-start(s32[1,2048]{1,0:T(1,128)} %param.16) | copy-start | bytes 24580
  29.3 38.7 %all-to-all-start.1 = ((bf16[16,48,512]{2,1,0:T(8,128)(2,1)}), bf16[16,48,512]{2,1,0:T(8,128)(2,1)S(1)}, u32[]{:S(2)}, u32[]{:S(2)}) async-start(bf16[16,48,512]{2,1,0:T(8,128)(2,1)} %serve.1), calls=%async_computation.1 | async-start | bytes 1572864 | tf_op jit(solution)/shard_map/all_to_all | solution.py:21
  33.3 16.6 %collective-permute-start.2 = (bf16[128,256]{1,0:T(8,128)(2,1)S(1)}, bf16[128,256]{1,0:T(8,128)(2,1)S(1)}, u32[]{:S(2)}, u32[]{:S(2)}) collective-permute-start(bf16[128,256]{1,0:T(8,128)(2,1)S(1)} %get-tuple-element.23), channel_id=1, source_target_pairs={{0,3},{1,0},{2,1},{3,2},{4,7},{5,4},{6,5},{7,6},{8,11},{9,8},{10,9... | collective-permute-start | bytes 196616 | tf_op jit(solution)/shard_map/ppermute | solution.py:552
  35.7 14.1 %collective-permute-start.1 = (bf16[128,256]{1,0:T(8,128)(2,1)S(1)}, bf16[128,256]{1,0:T(8,128)(2,1)S(1)}, u32[]{:S(2)}, u32[]{:S(2)}) collective-permute-start(bf16[128,256]{1,0:T(8,128)(2,1)S(1)} %get-tuple-element.23), channel_id=1, source_target_pairs={{0,2},{1,3},{2,0},{3,1},{4,6},{5,7},{6,4},{7,5},{8,10},{9,11},{10,... | collective-permute-start | bytes 196616 | tf_op jit(solution)/shard_map/ppermute | solution.py:552
  36.3 13.6 %collective-permute-start = (bf16[128,256]{1,0:T(8,128)(2,1)S(1)}, bf16[128,256]{1,0:T(8,128)(2,1)S(1)}, u32[]{:S(2)}, u32[]{:S(2)}) collective-permute-start(bf16[128,256]{1,0:T(8,128)(2,1)S(1)} %get-tuple-element.23), channel_id=1, source_target_pairs={{0,1},{1,2},{2,3},{3,0},{4,5},{5,6},{6,7},{7,4},{8,9},{9,10},{10,1... | collective-permute-start | bytes 196616 | tf_op jit(solution)/shard_map/ppermute | solution.py:552
  49.8 50.0 %copy-start.4 = (s32[1,512]{1,0:T(1,128)S(1)}, s32[1,512]{1,0:T(1,128)}, u32[]{:S(2)}) copy-start(s32[1,512]{1,0:T(1,128)} %param.23) | copy-start | bytes 6148
  49.8 64.5 %copy-start.1 = (bf16[256,256]{1,0:T(8,128)(2,1)S(1)}, bf16[256,256]{1,0:T(8,128)(2,1)}, u32[]{:S(2)}) copy-start(bf16[256,256]{1,0:T(8,128)(2,1)} %ws_ref.1) | copy-start | bytes 393220
  49.8 64.5 %copy-start.2 = (bf16[256,256]{1,0:T(8,128)(2,1)S(1)}, bf16[256,256]{1,0:T(8,128)(2,1)}, u32[]{:S(2)}) copy-start(bf16[256,256]{1,0:T(8,128)(2,1)} %wn_ref.1) | copy-start | bytes 393220
  49.9 8.3 %collective-permute-start.5 = (bf16[4,128,256]{2,1,0:T(8,128)(2,1)S(1)}, bf16[4,128,256]{2,1,0:T(8,128)(2,1)S(1)}, u32[]{:S(2)}, u32[]{:S(2)}) collective-permute-start(bf16[4,128,256]{2,1,0:T(8,128)(2,1)S(1)} %pad_maximum_fusion.refs_0_), channel_id=1, source_target_pairs={{0,12},{1,13},{2,14},{3,15},{4,0},{5,1},{6,2},{7,3},{8,4},{9,5},{1... | collective-permute-start | bytes 786440 | tf_op jit(solution)/shard_map/ppermute | solution.py:556
  52.7 8.0 %collective-permute-start.4 = (bf16[4,128,256]{2,1,0:T(8,128)(2,1)S(1)}, bf16[4,128,256]{2,1,0:T(8,128)(2,1)S(1)}, u32[]{:S(2)}, u32[]{:S(2)}) collective-permute-start(bf16[4,128,256]{2,1,0:T(8,128)(2,1)S(1)} %pad_maximum_fusion.refs_0_), channel_id=1, source_target_pairs={{0,8},{1,9},{2,10},{3,11},{4,12},{5,13},{6,14},{7,15},{8,0},{9,1},... | collective-permute-start | bytes 786440 | tf_op jit(solution)/shard_map/ppermute | solution.py:556
  53.1 15.0 %collective-permute-start.3 = (bf16[4,128,256]{2,1,0:T(8,128)(2,1)S(1)}, bf16[4,128,256]{2,1,0:T(8,128)(2,1)S(1)}, u32[]{:S(2)}, u32[]{:S(2)}) collective-permute-start(bf16[4,128,256]{2,1,0:T(8,128)(2,1)S(1)} %pad_maximum_fusion.refs_0_), channel_id=1, source_target_pairs={{0,4},{1,5},{2,6},{3,7},{4,8},{5,9},{6,10},{7,11},{8,12},{9,13},{1... | collective-permute-start | bytes 786440 | tf_op jit(solution)/shard_map/ppermute | solution.py:556
  80.5 12.9 %all-to-all-start.2 = ((bf16[16,96,128]{2,1,0:T(8,128)(2,1)}), bf16[16,96,128]{2,1,0:T(8,128)(2,1)S(1)}, u32[]{:S(2)}, u32[]{:S(2)}) async-start(bf16[16,96,128]{2,1,0:T(8,128)(2,1)} %first_hop.1.rows_ref), calls=%async_computation.2 | async-start | bytes 786432 | tf_op jit(solution)/shard_map/all_to_all | solution.py:21
  95.4 18.9 %all-to-all-start.3 = ((bf16[16,256,128]{2,1,0:T(8,128)(2,1)}), bf16[16,256,128]{2,1,0:T(8,128)(2,1)S(1)}, u32[]{:S(2)}, u32[]{:S(2)}) async-start(bf16[16,256,128]{2,1,0:T(8,128)(2,1)} %get-tuple-element.35), calls=%async_computation.3 | async-start | bytes 2097152 | tf_op jit(solution)/shard_map/all_to_all | solution.py:21
  105.0 1.7 copy-start
  153.0 16.1 %all-to-all-start.5 = ((bf16[16,40,256]{2,1,0:T(8,128)(2,1)}), bf16[16,40,256]{2,1,0:T(8,128)(2,1)S(1)}, u32[]{:S(2)}, u32[]{:S(2)}) async-start(bf16[16,40,256]{2,1,0:T(8,128)(2,1)} %broadcast_in_dim.2), calls=%async_computation.5 | async-start | bytes 655360 | tf_op jit(solution)/shard_map/all_to_all | solution.py:21
